TPU v7x, 512 devices: a whole 4x4x16 slice. The times are simulated.
512 devices in a mesh: batch: 128 (over y_lo, x, z), rep: 4 (over y_hi, core).
Axes of the slice: x: 4, y: 4 (y_hi: 2, y_lo: 2; y = y_hi * 2 + y_lo), z: 16, core: 2. Of those that a mesh axis runs over, the one named last changes fastest.
Arguments:
- queries: bfloat16 [65536, 4096], P(('batch', 'rep')), may hold values from -24 to 24
- passages: bfloat16 [768, 4096], P('batch'), may hold values from -6 to 6
- positives: int32 [65536], P(('batch', 'rep')), may hold values from 0 to 767
- negatives: int32 [65536, 7], P(('batch', 'rep')), may hold values from 0 to 767
Outputs:
- query_grad: float32 [65536, 4096], P(('batch', 'rep'))
- passage_grad: float32 [768, 4096], P('batch')
All inputs are finite; a program needn't handle non-finite values.
Results may differ from a plain program's by a relative error of at most 0.0014.
Values may be sent and summed in bfloat16 or wider, within the bound.
No kernel may reach another device: no remote copies, remote signals or barrier semaphores. Data moves between devices by JAX's collectives and lax.ppermute only.
A program may use at most 64 MiB of HBM per device.

v0:
```python
import jax
import jax.numpy as jnp
from jax import lax
from jax.sharding import PartitionSpec as P


def loss_weights(scores, positives, negatives):
    columns = jnp.arange(scores.shape[1], dtype=jnp.int32)
    picked = negatives[:, :, None] == columns[None, None, :]
    hard = jnp.sum(jnp.where(picked, scores[:, None, :], jnp.float32(0.0)), axis=2)
    top = jnp.max(scores, axis=1)
    total = jnp.sum(jnp.exp(scores - top[:, None]), axis=1) + jnp.sum(
        jnp.exp(hard - top[:, None]), axis=1
    )
    lse = top + jnp.log(total)
    extra = jnp.sum(
        jnp.where(picked, jnp.exp(hard - lse[:, None])[:, :, None], jnp.float32(0.0)), axis=1
    )
    target = (positives[:, None] == columns[None, :]).astype(jnp.float32)
    return (jnp.exp(scores - lse[:, None]) + extra - target).astype(jnp.bfloat16)


def shards(queries, passages, positives, negatives):
    pooled = lax.all_gather(passages, "batch", axis=0, tiled=True)
    scores = jnp.dot(queries, pooled.T, preferred_element_type=jnp.float32) * 0.0625
    weights = loss_weights(scores, positives, negatives)
    query_grad = jnp.dot(weights, pooled, preferred_element_type=jnp.float32) * 0.0625
    group_weights = lax.all_gather(weights, "rep", axis=0, tiled=True)
    group_columns = lax.all_to_all(queries, "rep", split_axis=1, concat_axis=0, tiled=True)
    product = lax.dot_general(
        group_weights, group_columns, (((0,), (0,)), ((), ())), preferred_element_type=jnp.float32
    )
    owned = lax.psum_scatter(product * 0.0625, "batch", scatter_dimension=0, tiled=True)
    passage_grad = lax.all_gather(owned, "rep", axis=1, tiled=True)
    return (query_grad, passage_grad)


def solution(mesh):
    placed = (
        P(("batch", "rep"), None),
        P("batch", None),
        P(("batch", "rep")),
        P(("batch", "rep"), None),
    )
    return jax.shard_map(
        shards,
        mesh=mesh,
        in_specs=placed,
        out_specs=(P(("batch", "rep"), None), P("batch", None)),
        check_vma=False,
    )
```

profile of v0, /device:TPU:1, one launch (start us, length us, event | category | flops | bytes accessed | tf_op | source)
XLA Modules:
  0.0 1125.0 jit_solution(7212455133166325292)
XLA Ops:
  7.2 0.7 all-gather.3.cloned.1.call-update
  7.9 1.6 copy.14
  9.5 24.2 %all_to_all.19 = bf16[128,4,1024]{0,2,1:T(8,128)(2,1)S(1)} all-to-all(bf16[128,4,1024]{0,2,1:T(8,128)(2,1)S(1)} %bitcast.14), channel_id=1, replica_groups=mesh['batch'=128,'rep'=4] {'rep'}, dimensions={1} | all-to-all | bytes 2097152 | tf_op jit(solution)/shard_map/all_to_all | solution.py:29
  33.8 1.3 copy.15
  35.1 498.8 %all-gather.3.cloned.1.call-done = bf16[128,6,4096]{2,1,0:T(8,128)(2,1)} async-done(((bf16[1,6,4096]{2,1,0:T(8,128)(2,1)}), bf16[128,6,4096]{2,1,0:T(8,128)(2,1)}) %all-gather.3.cloned.1.call-update) | async-done | bytes 6291472 | tf_op jit(solution)/shard_map/all_gather | solution.py:24
  533.8 10.2 reshape.39
  544.0 5.1 fusion.1
  549.2 0.5 select_reduce_fusion.1
  550.5 95.0 %all_gather.10 = bf16[512,768]{1,0:T(8,128)(2,1)S(1)} all-gather(bf16[128,768]{1,0:T(8,128)(2,1)S(1)} %subtract_convert_fusion), channel_id=1, replica_groups=mesh['batch'=128,'rep'=4] {'rep'}, dimensions={0}, use_global_device_ids=true | all-gather | bytes 983040 | tf_op jit(solution)/shard_map/all_gather | solution.py:28
  645.5 1.0 convolution_multiply_fusion.1
  646.5 274.5 %fusion = f32[8,1024]{1,0:T(8,128)S(1)} fusion(f32[768,1024]{1,0:T(8,128)S(1)} %convolution_multiply_fusion.1), kind=kCustom, calls=%all-reduce-scatter | all-reduce-scatter fusion | flops 1048577 | bytes 3180544
  920.9 1.3 collective-permute-start
  922.3 1.3 collective-permute-start.31
  923.6 1.3 collective-permute-start.1
  924.9 1.3 collective-permute-start.10
  926.2 1.3 collective-permute-start.11
  927.5 7.2 collective-permute-start.12
  934.7 1.3 collective-permute-start.13
  936.0 10.0 collective-permute-start.14
  946.0 1.3 collective-permute-start.15
  947.3 1.7 collective-permute-start.16
  949.0 3.7 collective-permute-start.17
  952.8 5.3 collective-permute-start.18
  958.1 6.4 collective-permute-start.19
  964.5 3.4 collective-permute-start.2
  967.9 2.0 collective-permute-start.20
  969.9 3.7 collective-permute-start.21
  973.6 5.8 collective-permute-start.22
  979.4 2.5 collective-permute-start.23
  982.0 2.8 collective-permute-start.24
  984.8 4.4 collective-permute-start.25
  989.2 1.3 collective-permute-start.26
  990.5 1.3 collective-permute-start.27
  991.8 1.3 collective-permute-start.28
  993.1 5.5 collective-permute-start.29
  998.6 5.0 collective-permute-start.3
  1003.6 1.3 collective-permute-start.30
  1004.9 9.1 collective-permute-start.4
  1014.0 1.3 dynamic-slice.4
  1015.9 1.3 collective-permute-start.5
  1017.2 2.4 collective-permute-start.6
  1019.7 10.9 collective-permute-start.7
  1030.6 9.2 collective-permute-start.8
  1039.8 1.3 collective-permute-start.9
  1041.1 5.1 convolution_multiply_fusion
  1046.3 3.5 concatenate
  1049.7 67.8 %all_gather.11 = f32[6,4096]{1,0:T(8,128)S(1)} all-gather(f32[6,1024]{1,0:T(8,128)S(1)} %constant_dynamic-slice_fusion), channel_id=1, replica_groups=mesh['batch'=128,'rep'=4] {'rep'}, dimensions={1}, use_global_device_ids=true | all-gather | bytes 122880 | tf_op jit(solution)/shard_map/all_gather | solution.py:34
  1117.5 0.7 copy.17
  (49 shorter events, 0.9 us)
Async XLA Ops:
  7.2 526.7 %all-gather.3.cloned.1.call-start = ((), (), s32[]{:S(2)}) async-start(), calls=%async_computation.1 | async-start | bytes 8454144 | tf_op jit(solution)/shard_map/all_gather | solution.py:24
  35.1 509.0 %copy-start = (bf16[128,4096]{1,0:T(8,128)(2,1)S(1)}, bf16[128,4096]{1,0:T(8,128)(2,1)}, u32[]{:S(2)}) copy-start(bf16[128,4096]{1,0:T(8,128)(2,1)} %param.4) | copy-start | bytes 3145732
  544.0 5.1 copy-start.2
  544.0 6.3 copy-start.3
  549.1 96.3 %copy-start.1 = (bf16[4,128,1024]{2,1,0:T(8,128)(2,1)S(1)}, bf16[4,128,1024]{2,1,0:T(8,128)(2,1)}, u32[]{:S(2)}) copy-start(bf16[4,128,1024]{2,1,0:T(8,128)(2,1)} %copy.15) | copy-start | bytes 3145732
  920.9 13.7 %collective-permute-start = (f32[8,1024]{1,0:T(8,128)S(1)}, f32[8,1024]{1,0:T(8,128)S(1)}, u32[]{:S(2)}, u32[]{:S(2)}) collective-permute-start(f32[8,1024]{1,0:T(8,128)S(1)} %fusion), channel_id=1, source_target_pairs={{0,4},{4,8},{8,12},{12,16},{16,20},{20,24},{24,28},{28,32},{32,36}... | collective-permute-start | bytes 98312
  922.3 5.2 collective-permute-start.31
  923.6 12.4 %collective-permute-start.1 = (f32[8,1024]{1,0:T(8,128)S(1)}, f32[8,1024]{1,0:T(8,128)S(1)}, u32[]{:S(2)}, u32[]{:S(2)}) collective-permute-start(f32[8,1024]{1,0:T(8,128)S(1)} %fusion), channel_id=1, source_target_pairs={{0,8},{4,12},{8,16},{12,20},{16,24},{20,28},{24,32},{28,36},{32,40... | collective-permute-start | bytes 98312
  924.9 21.2 %collective-permute-start.10 = (f32[8,1024]{1,0:T(8,128)S(1)}, f32[8,1024]{1,0:T(8,128)S(1)}, u32[]{:S(2)}, u32[]{:S(2)}) collective-permute-start(f32[8,1024]{1,0:T(8,128)S(1)} %fusion), channel_id=1, source_target_pairs={{0,44},{4,48},{8,52},{12,56},{16,60},{20,64},{24,68},{28,72},{32,7... | collective-permute-start | bytes 98312
  926.2 21.2 %collective-permute-start.11 = (f32[8,1024]{1,0:T(8,128)S(1)}, f32[8,1024]{1,0:T(8,128)S(1)}, u32[]{:S(2)}, u32[]{:S(2)}) collective-permute-start(f32[8,1024]{1,0:T(8,128)S(1)} %fusion), channel_id=1, source_target_pairs={{0,48},{4,52},{8,56},{12,60},{16,64},{20,68},{24,72},{28,76},{32,8... | collective-permute-start | bytes 98312
  927.5 21.6 %collective-permute-start.12 = (f32[8,1024]{1,0:T(8,128)S(1)}, f32[8,1024]{1,0:T(8,128)S(1)}, u32[]{:S(2)}, u32[]{:S(2)}) collective-permute-start(f32[8,1024]{1,0:T(8,128)S(1)} %fusion), channel_id=1, source_target_pairs={{0,52},{4,56},{8,60},{12,64},{16,68},{20,72},{24,76},{28,80},{32,8... | collective-permute-start | bytes 98312
  934.7 18.1 %collective-permute-start.13 = (f32[8,1024]{1,0:T(8,128)S(1)}, f32[8,1024]{1,0:T(8,128)S(1)}, u32[]{:S(2)}, u32[]{:S(2)}) collective-permute-start(f32[8,1024]{1,0:T(8,128)S(1)} %fusion), channel_id=1, source_target_pairs={{0,56},{4,60},{8,64},{12,68},{16,72},{20,76},{24,80},{28,84},{32,8... | collective-permute-start | bytes 98312
  936.0 22.1 %collective-permute-start.14 = (f32[8,1024]{1,0:T(8,128)S(1)}, f32[8,1024]{1,0:T(8,128)S(1)}, u32[]{:S(2)}, u32[]{:S(2)}) collective-permute-start(f32[8,1024]{1,0:T(8,128)S(1)} %fusion), channel_id=1, source_target_pairs={{0,60},{4,64},{8,68},{12,72},{16,76},{20,80},{24,84},{28,88},{32,9... | collective-permute-start | bytes 98312
  946.0 18.4 %collective-permute-start.15 = (f32[8,1024]{1,0:T(8,128)S(1)}, f32[8,1024]{1,0:T(8,128)S(1)}, u32[]{:S(2)}, u32[]{:S(2)}) collective-permute-start(f32[8,1024]{1,0:T(8,128)S(1)} %fusion), channel_id=1, source_target_pairs={{0,64},{4,68},{8,72},{12,76},{16,80},{20,84},{24,88},{28,92},{32,9... | collective-permute-start | bytes 98312
  947.3 20.5 %collective-permute-start.16 = (f32[8,1024]{1,0:T(8,128)S(1)}, f32[8,1024]{1,0:T(8,128)S(1)}, u32[]{:S(2)}, u32[]{:S(2)}) collective-permute-start(f32[8,1024]{1,0:T(8,128)S(1)} %fusion), channel_id=1, source_target_pairs={{0,68},{4,72},{8,76},{12,80},{16,84},{20,88},{24,92},{28,96},{32,1... | collective-permute-start | bytes 98312
  949.0 20.9 %collective-permute-start.17 = (f32[8,1024]{1,0:T(8,128)S(1)}, f32[8,1024]{1,0:T(8,128)S(1)}, u32[]{:S(2)}, u32[]{:S(2)}) collective-permute-start(f32[8,1024]{1,0:T(8,128)S(1)} %fusion), channel_id=1, source_target_pairs={{0,72},{4,76},{8,80},{12,84},{16,88},{20,92},{24,96},{28,100},{32,... | collective-permute-start | bytes 98312
  952.8 20.8 %collective-permute-start.18 = (f32[8,1024]{1,0:T(8,128)S(1)}, f32[8,1024]{1,0:T(8,128)S(1)}, u32[]{:S(2)}, u32[]{:S(2)}) collective-permute-start(f32[8,1024]{1,0:T(8,128)S(1)} %fusion), channel_id=1, source_target_pairs={{0,76},{4,80},{8,84},{12,88},{16,92},{20,96},{24,100},{28,104},{32... | collective-permute-start | bytes 98312
  958.1 21.3 %collective-permute-start.19 = (f32[8,1024]{1,0:T(8,128)S(1)}, f32[8,1024]{1,0:T(8,128)S(1)}, u32[]{:S(2)}, u32[]{:S(2)}) collective-permute-start(f32[8,1024]{1,0:T(8,128)S(1)} %fusion), channel_id=1, source_target_pairs={{0,80},{4,84},{8,88},{12,92},{16,96},{20,100},{24,104},{28,108},{3... | collective-permute-start | bytes 98312
  964.5 17.5 %collective-permute-start.2 = (f32[8,1024]{1,0:T(8,128)S(1)}, f32[8,1024]{1,0:T(8,128)S(1)}, u32[]{:S(2)}, u32[]{:S(2)}) collective-permute-start(f32[8,1024]{1,0:T(8,128)S(1)} %fusion), channel_id=1, source_target_pairs={{0,12},{4,16},{8,20},{12,24},{16,28},{20,32},{24,36},{28,40},{32,4... | collective-permute-start | bytes 98312
  967.9 16.9 %collective-permute-start.20 = (f32[8,1024]{1,0:T(8,128)S(1)}, f32[8,1024]{1,0:T(8,128)S(1)}, u32[]{:S(2)}, u32[]{:S(2)}) collective-permute-start(f32[8,1024]{1,0:T(8,128)S(1)} %fusion), channel_id=1, source_target_pairs={{0,84},{4,88},{8,92},{12,96},{16,100},{20,104},{24,108},{28,112},{... | collective-permute-start | bytes 98312
  969.9 19.3 %collective-permute-start.21 = (f32[8,1024]{1,0:T(8,128)S(1)}, f32[8,1024]{1,0:T(8,128)S(1)}, u32[]{:S(2)}, u32[]{:S(2)}) collective-permute-start(f32[8,1024]{1,0:T(8,128)S(1)} %fusion), channel_id=1, source_target_pairs={{0,88},{4,92},{8,96},{12,100},{16,104},{20,108},{24,112},{28,116},... | collective-permute-start | bytes 98312
  973.6 16.9 %collective-permute-start.22 = (f32[8,1024]{1,0:T(8,128)S(1)}, f32[8,1024]{1,0:T(8,128)S(1)}, u32[]{:S(2)}, u32[]{:S(2)}) collective-permute-start(f32[8,1024]{1,0:T(8,128)S(1)} %fusion), channel_id=1, source_target_pairs={{0,92},{4,96},{8,100},{12,104},{16,108},{20,112},{24,116},{28,120}... | collective-permute-start | bytes 98312
  979.4 12.4 %collective-permute-start.23 = (f32[8,1024]{1,0:T(8,128)S(1)}, f32[8,1024]{1,0:T(8,128)S(1)}, u32[]{:S(2)}, u32[]{:S(2)}) collective-permute-start(f32[8,1024]{1,0:T(8,128)S(1)} %fusion), channel_id=1, source_target_pairs={{0,96},{4,100},{8,104},{12,108},{16,112},{20,116},{24,120},{28,124... | collective-permute-start | bytes 98312
  982.0 11.1 collective-permute-start.24
  984.8 13.8 %collective-permute-start.25 = (f32[8,1024]{1,0:T(8,128)S(1)}, f32[8,1024]{1,0:T(8,128)S(1)}, u32[]{:S(2)}, u32[]{:S(2)}) collective-permute-start(f32[8,1024]{1,0:T(8,128)S(1)} %fusion), channel_id=1, source_target_pairs={{0,104},{4,108},{8,112},{12,116},{16,120},{20,124},{24,128},{28,13... | collective-permute-start | bytes 98312
  989.2 14.4 %collective-permute-start.26 = (f32[8,1024]{1,0:T(8,128)S(1)}, f32[8,1024]{1,0:T(8,128)S(1)}, u32[]{:S(2)}, u32[]{:S(2)}) collective-permute-start(f32[8,1024]{1,0:T(8,128)S(1)} %fusion), channel_id=1, source_target_pairs={{0,108},{4,112},{8,116},{12,120},{16,124},{20,128},{24,132},{28,13... | collective-permute-start | bytes 98312
  990.5 14.4 %collective-permute-start.27 = (f32[8,1024]{1,0:T(8,128)S(1)}, f32[8,1024]{1,0:T(8,128)S(1)}, u32[]{:S(2)}, u32[]{:S(2)}) collective-permute-start(f32[8,1024]{1,0:T(8,128)S(1)} %fusion), channel_id=1, source_target_pairs={{0,112},{4,116},{8,120},{12,124},{16,128},{20,132},{24,136},{28,14... | collective-permute-start | bytes 98312
  991.8 24.1 %collective-permute-start.28 = (f32[8,1024]{1,0:T(8,128)S(1)}, f32[8,1024]{1,0:T(8,128)S(1)}, u32[]{:S(2)}, u32[]{:S(2)}) collective-permute-start(f32[8,1024]{1,0:T(8,128)S(1)} %fusion), channel_id=1, source_target_pairs={{0,116},{4,120},{8,124},{12,128},{16,132},{20,136},{24,140},{28,14... | collective-permute-start | bytes 98312
  993.1 24.1 %collective-permute-start.29 = (f32[8,1024]{1,0:T(8,128)S(1)}, f32[8,1024]{1,0:T(8,128)S(1)}, u32[]{:S(2)}, u32[]{:S(2)}) collective-permute-start(f32[8,1024]{1,0:T(8,128)S(1)} %fusion), channel_id=1, source_target_pairs={{0,120},{4,124},{8,128},{12,132},{16,136},{20,140},{24,144},{28,14... | collective-permute-start | bytes 98312
  998.6 21.1 %collective-permute-start.3 = (f32[8,1024]{1,0:T(8,128)S(1)}, f32[8,1024]{1,0:T(8,128)S(1)}, u32[]{:S(2)}, u32[]{:S(2)}) collective-permute-start(f32[8,1024]{1,0:T(8,128)S(1)} %fusion), channel_id=1, source_target_pairs={{0,16},{4,20},{8,24},{12,28},{16,32},{20,36},{24,40},{28,44},{32,4... | collective-permute-start | bytes 98312
  1003.6 27.0 %collective-permute-start.30 = (f32[8,1024]{1,0:T(8,128)S(1)}, f32[8,1024]{1,0:T(8,128)S(1)}, u32[]{:S(2)}, u32[]{:S(2)}) collective-permute-start(f32[8,1024]{1,0:T(8,128)S(1)} %fusion), channel_id=1, source_target_pairs={{0,124},{4,128},{8,132},{12,136},{16,140},{20,144},{24,148},{28,15... | collective-permute-start | bytes 98312
  1004.9 34.9 %collective-permute-start.4 = (f32[8,1024]{1,0:T(8,128)S(1)}, f32[8,1024]{1,0:T(8,128)S(1)}, u32[]{:S(2)}, u32[]{:S(2)}) collective-permute-start(f32[8,1024]{1,0:T(8,128)S(1)} %fusion), channel_id=1, source_target_pairs={{0,20},{4,24},{8,28},{12,32},{16,36},{20,40},{24,44},{28,48},{32,5... | collective-permute-start | bytes 98312
  1015.9 30.3 %collective-permute-start.5 = (f32[8,1024]{1,0:T(8,128)S(1)}, f32[8,1024]{1,0:T(8,128)S(1)}, u32[]{:S(2)}, u32[]{:S(2)}) collective-permute-start(f32[8,1024]{1,0:T(8,128)S(1)} %fusion), channel_id=1, source_target_pairs={{0,24},{4,28},{8,32},{12,36},{16,40},{20,44},{24,48},{28,52},{32,5... | collective-permute-start | bytes 98312
  1017.2 29.0 %collective-permute-start.6 = (f32[8,1024]{1,0:T(8,128)S(1)}, f32[8,1024]{1,0:T(8,128)S(1)}, u32[]{:S(2)}, u32[]{:S(2)}) collective-permute-start(f32[8,1024]{1,0:T(8,128)S(1)} %fusion), channel_id=1, source_target_pairs={{0,28},{4,32},{8,36},{12,40},{16,44},{20,48},{24,52},{28,56},{32,6... | collective-permute-start | bytes 98312
  1019.7 26.6 %collective-permute-start.7 = (f32[8,1024]{1,0:T(8,128)S(1)}, f32[8,1024]{1,0:T(8,128)S(1)}, u32[]{:S(2)}, u32[]{:S(2)}) collective-permute-start(f32[8,1024]{1,0:T(8,128)S(1)} %fusion), channel_id=1, source_target_pairs={{0,32},{4,36},{8,40},{12,44},{16,48},{20,52},{24,56},{28,60},{32,6... | collective-permute-start | bytes 98312
  1030.6 15.7 %collective-permute-start.8 = (f32[8,1024]{1,0:T(8,128)S(1)}, f32[8,1024]{1,0:T(8,128)S(1)}, u32[]{:S(2)}, u32[]{:S(2)}) collective-permute-start(f32[8,1024]{1,0:T(8,128)S(1)} %fusion), channel_id=1, source_target_pairs={{0,36},{4,40},{8,44},{12,48},{16,52},{20,56},{24,60},{28,64},{32,6... | collective-permute-start | bytes 98312
  1039.8 6.4 collective-permute-start.9
Sparse Core Ops, SparseCore 0:
  10.1 523.7 all-gather.2
where the time goes:
time: 1130 us
  waiting for transfers between devices  500 us (44%)
  blocking collectives  461 us (41%)
  starting transfers between devices  118 us (10%)
  local copies, waits for them, and re-layouts  18.5 us (2%)
  between operations  15.3 us (1%)
    all_gather x1, waiting for transfers between devices, shards(): pooled = lax.all_gather(passages, 'batch', axis=0, tiled=True)  499 us
    unnamed x1, blocking collectives  274 us
    unnamed x32, starting transfers between devices  118 us
    all_gather x1, blocking collectives, shards(): group_weights = lax.all_gather(weights, 'rep', axis=0, tiled=True)  95 us
    all_gather x1, blocking collectives, shards(): passage_grad = lax.all_gather(owned, 'rep', axis=1, tiled=True)  67.8 us
    all_to_all x1, blocking collectives, shards(): lax.all_to_all(queries, 'rep', split_axis=1, concat_axis=0, tiled=True)  24.2 us
  transfers between devices with their start and end apart: 33, of which 1 were waited for; matrix products, arithmetic and copies ran while one was open for 1% of the time, Pallas kernels for 0%

commit v1 on v0

v1 whole, which is shorter than its diff:
```python
import functools

import jax
import jax.numpy as jnp
from jax import lax
from jax.experimental import pallas as pl
from jax.experimental.pallas import tpu as pltpu
from jax.sharding import Mesh
from jax.sharding import PartitionSpec as P

D = 4096
HALF = 2048
SLICE = 512
QDEV = 128
NP = 768
ROWS = 96
SIDE = 384
Y = ("yl", "yh")
VMEM_LIMIT = 60 * 1024 * 1024
F32, BF16 = jnp.float32, jnp.bfloat16


def shift(count, by):
    return [(i, (i + by) % count) for i in range(count)]


def along_y(by):
    place = lambda y: 2 * (y % 2) + y // 2
    return [(place(y), place((y + by) % 4)) for y in range(4)]


def call(kernel, outs, *args, smem=0, scratch=(), flops=0):
    in_specs = [pl.BlockSpec(memory_space=pltpu.SMEM)] * smem
    in_specs += [pl.BlockSpec(memory_space=pltpu.VMEM)] * (len(args) - smem)
    size = sum(a.size * a.dtype.itemsize for a in args) + sum(o.size * o.dtype.itemsize for o in outs)
    return pl.pallas_call(
        kernel,
        out_shape=outs,
        in_specs=in_specs,
        out_specs=[pl.BlockSpec(memory_space=pltpu.VMEM)] * len(outs),
        scratch_shapes=list(scratch),
        compiler_params=pltpu.CompilerParams(vmem_limit_bytes=VMEM_LIMIT),
        cost_estimate=pl.CostEstimate(flops=flops, bytes_accessed=size, transcendentals=0),
    )(*args)


def score_kernel(side_ref, qo, qx, *refs):
    pieces, (so, sx, pool), q2 = refs[:8], refs[8:11], refs[11]
    q2[:QDEV] = qo[...]
    q2[QDEV:] = qx[...]
    side = side_ref[0]
    for t in range(2):
        base = (side if t == 0 else 1 - side) * SIDE
        for s in range(4):
            pool[pl.ds(pl.multiple_of(base + ROWS * s, 32), ROWS), :] = pieces[4 * t + s][...]
    for n in range(3):
        cols = slice(256 * n, 256 * n + 256)
        part = lax.dot_general(q2[...], pool[cols, :], (((1,), (1,)), ((), ())), preferred_element_type=F32)
        so[:, cols] = part[:QDEV]
        sx[:, cols] = part[QDEV:]


def loss_kernel(so, sr, ids, pos, neg, w):
    scores = (so[...] + sr[...]) * 0.0625
    column = ids[...]
    count = jnp.ones(scores.shape, F32)
    for k in range(7):
        count += jnp.where(neg[:, k : k + 1] == column, 1.0, 0.0)
    top = jnp.max(scores, axis=1, keepdims=True)
    mass = jnp.exp(scores - top) * count
    total = jnp.sum(mass, axis=1, keepdims=True)
    w[...] = (mass / total - jnp.where(pos[...] == column, 1.0, 0.0)).astype(BF16)


def query_kernel(wo, wx, pool, go, gx, w2):
    w2[:QDEV] = wo[...]
    w2[QDEV:] = wx[...]
    for n in range(HALF // 512):
        cols = slice(512 * n, 512 * n + 512)
        part = jnp.dot(w2[...], pool[:, cols], preferred_element_type=F32) * 0.0625
        go[:, cols] = part[:QDEV]
        gx[:, cols] = part[QDEV:]


def pool_kernel(*refs):
    ws, qs, outs, w_all, q_all = refs[:8], refs[8:12], refs[12:16], refs[16], refs[17]
    for i in range(8):
        w_all[QDEV * i : QDEV * (i + 1), :] = ws[i][...]
    for i in range(4):
        q_all[2 * QDEV * i : 2 * QDEV * (i + 1), :] = qs[i][...]
    for n in range(3):
        part = lax.dot_general(
            w_all[:, 256 * n : 256 * n + 256], q_all[...], (((0,), (0,)), ((), ())), preferred_element_type=F32
        ) * 0.0625
        for lo in range(256 * n, 256 * n + 256, 32):
            side, rest = divmod(lo, SIDE)
            s, row = divmod(rest, ROWS)
            outs[s][ROWS * side + row : ROWS * side + row + 32, :] = part[lo - 256 * n : lo - 256 * n + 32]


def sum_kernel(a, b, c, d, out):
    out[...] = (a[...] + b[...]) + (c[...] + d[...])


def shards(queries, passages, positives, negatives):
    core = lax.axis_index("c")
    x = lax.axis_index("x")
    yl = lax.axis_index("yl")
    y = 2 * lax.axis_index("yh") + yl
    other = lambda a: lax.ppermute(a, "c", shift(2, 1))

    q_own = lax.dynamic_slice(queries, (0, core * HALF), (QDEV, HALF))
    q_out = lax.dynamic_slice(queries, (0, (1 - core) * HALF), (QDEV, HALF))
    q_oth = other(q_out)

    mine = lax.dynamic_slice(passages, (0, core * HALF), (6, HALF)).reshape(6, 16, 128)
    block = lax.all_gather(mine, "z", axis=0, tiled=True).reshape(ROWS, HALF)
    near = [block] + [lax.ppermute(block, "x", shift(4, s)) for s in range(1, 4)]
    far = [lax.ppermute(b, Y, along_y(1 if s in (0, 3) else -1)) for s, b in enumerate(near)]

    chip_queries = []
    for s in range(4):
        at = ((y + s) % 4) * SLICE
        part = jnp.concatenate([lax.dynamic_slice(q, (0, at), (QDEV, SLICE)) for q in (q_own, q_oth)])
        chip_queries.append(part if s == 0 else lax.ppermute(part, Y, along_y(s)))

    sd = jax.ShapeDtypeStruct
    s_own, s_out, pool = call(
        score_kernel,
        [sd((QDEV, NP), F32), sd((QDEV, NP), F32), sd((NP, HALF), BF16)],
        yl.reshape(1), q_own, q_oth, *near, *far,
        smem=1, scratch=[pltpu.VMEM((2 * QDEV, HALF), BF16)], flops=2 * 256 * NP * HALF,
    )
    s_oth = other(s_out)

    col = jnp.arange(NP, dtype=jnp.int32)
    side, s, z, r = col // SIDE, (col // ROWS) % 4, (col // 6) % 16, col % 6
    ids = ((side * 4 + (x - s) % 4) * 16 + z) * 6 + r
    w = call(
        loss_kernel, [sd((QDEV, NP), BF16)],
        s_own, s_oth, ids.reshape(1, NP), positives.reshape(QDEV, 1), negatives,
    )[0]

    ws = [w] + [lax.ppermute(w, Y, along_y(s)) for s in range(1, 4)]
    wx = [other(a) for a in ws]
    blocks = call(
        pool_kernel, [sd((2 * ROWS, SLICE), F32)] * 4,
        *[a for pair in zip(ws, wx) for a in pair], *chip_queries,
        scratch=[pltpu.VMEM((1024, NP), BF16), pltpu.VMEM((1024, SLICE), BF16)], flops=2 * 1024 * NP * SLICE,
    )
    got = [blocks[0]] + [lax.ppermute(blocks[s], "x", shift(4, -s)) for s in range(1, 4)]

    g_own, g_out = call(
        query_kernel, [sd((QDEV, HALF), F32)] * 2, w, wx[0], pool,
        scratch=[pltpu.VMEM((2 * QDEV, NP), BF16)], flops=2 * 256 * NP * HALF,
    )
    g_oth = other(g_out)
    low = jnp.where(core == 0, g_own, g_oth)
    high = jnp.where(core == 0, g_oth, g_own)
    query_grad = jnp.concatenate([low, high], axis=1)

    mid = call(sum_kernel, [sd((2 * ROWS, SLICE), F32)], *got)[0]
    spread = lax.all_to_all(mid.reshape(2, 16, 6, 4, 128), "z", 1, 0, tiled=False)
    owned = jnp.sum(spread, axis=0)
    full = lax.all_gather(owned.reshape(2, 6, SLICE), Y + ("c",), axis=0, tiled=False)
    full = jnp.where(yl == 0, full[:, 0], full[:, 1])
    passage_grad = full.reshape(2, 2, 2, 6, SLICE).transpose(3, 2, 1, 0, 4).reshape(6, D)
    return query_grad, passage_grad


def solution(mesh):
    fine = Mesh(mesh.devices.reshape(2, 4, 16, 2, 2), ("yl", "x", "z", "yh", "c"))
    every, pooled = ("yl", "x", "z", "yh", "c"), ("yl", "x", "z")
    return jax.shard_map(
        shards,
        mesh=fine,
        in_specs=(P(every, None), P(pooled, None), P(every), P(every, None)),
        out_specs=(P(every, None), P(pooled, None)),
        check_vma=False,
    )
```

time: 1130 us -> 214 us (0.19)
  waiting for transfers between devices: 500 us -> 45.1 us
  blocking collectives: 461 us -> 52.3 us
  starting transfers between devices: 118 us -> 81.5 us
  Pallas kernels: 0 us -> 18.2 us
  between operations: 15.3 us -> 1.32 us
    all_gather x1 -> x0, waiting for transfers between devices: 499 us -> none  [shards(): pooled = lax.all_gather(passages, 'batch', axis=0, tiled=True)]
    unnamed x1 -> x0, blocking collectives: 274 us -> none
    unnamed x32 -> x0, starting transfers between devices: 118 us -> none
    all_gather x2, blocking collectives: 163 us -> 52.3 us  [the longest x1 31.1 us: shards(): block = lax.all_gather(mine, 'z', axis=0, tiled=True).reshape(ROWS, HALF)]
    ppermute x0 -> x23, starting transfers between devices: none -> 75.1 us  [the longest x7 25.7 us: shards(): other = lambda a: lax.ppermute(a, 'c', shift(2, 1))]
    ppermute x0 -> x23, waiting for transfers between devices: none -> 29.2 us  [the longest x3 17.1 us: shards(): lax.ppermute(blocks[s], 'x', shift(4, -s))]
    all_to_all x1 -> x0, blocking collectives: 24.2 us -> none  [shards(): lax.all_to_all(queries, 'rep', split_axis=1, concat_axis=0, tiled=True)]
    pallas_call x0 -> x5, Pallas kernels: none -> 18.2 us  [call(): pl.pallas_call(kernel, out_shape=outs, in_specs=in_specs, out_specs=[pl.B...]
  transfers between devices with their start and end apart: 33 -> 24, of which waited for: 1 -> 7; matrix products, arithmetic and copies ran while one was open for 1% -> 5% of each run, Pallas kernels for 0% -> 6%
where the time goes in v1:
time: 214 us; the launch traced here: 213 us
  starting transfers between devices  81.5 us (38%)
  blocking collectives  52.3 us (24%)
  waiting for transfers between devices  45.1 us (21%)
  Pallas kernels  18.2 us (9%)
  local copies, waits for them, and re-layouts  11.1 us (5%)
  other arithmetic  3.23 us (2%)
    all_gather x1, blocking collectives, shards(): block = lax.all_gather(mine, 'z', axis=0, tiled=True).reshape(ROWS, HALF)  31.1 us
    ppermute x7, starting transfers between devices, shards(): other = lambda a: lax.ppermute(a, 'c', shift(2, 1))  25.7 us
    all_gather x1, blocking collectives, shards(): lax.all_gather(owned.reshape(2, 6, SLICE), Y + ('c',), axis=0, tiled=False)  21.2 us
    pallas_call x5, Pallas kernels, call(): pl.pallas_call(kernel, out_shape=outs, in_specs=in_specs, out_specs=[pl.B...  18.2 us
    ppermute x3, waiting for transfers between devices, shards(): lax.ppermute(blocks[s], 'x', shift(4, -s))  17.1 us
    all_to_all x1, waiting for transfers between devices, shards(): lax.all_to_all(mid.reshape(2, 16, 6, 4, 128), 'z', 1, 0, tiled=False)  15.9 us
    ppermute x4, waiting for transfers between devices, shards(): lax.ppermute(b, Y, along_y(1 if s in (0, 3) else -1))  12 us
    ppermute x4, starting transfers between devices, shards(): lax.ppermute(b, Y, along_y(1 if s in (0, 3) else -1))  11.8 us
  transfers between devices with their start and end apart: 24, of which 7 were waited for; matrix products, arithmetic and copies ran while one was open for 5% of the time, Pallas kernels for 6%

profile of v1, /device:TPU:1, one launch (start us, length us, event | category | flops | bytes accessed | tf_op | source)
XLA Modules:
  0.0 212.7 jit_solution(14741865169353192264)
XLA Ops:
  0.7 0.8 copy-done
  1.5 31.1 %all_gather.6 = bf16[96,16,128]{2,1,0:T(8,128)(2,1)S(1)} all-gather(bf16[6,16,128]{2,1,0:T(8,128)(2,1)S(1)} %bitcast.25), channel_id=1, replica_groups=mesh['yl'=2,'x'=4,'z'=16,'yh'=2,'c'=2] {'z'}, dimensions={0}, use_global_device_ids=true | all-gather | bytes 417792 | tf_op jit(solution)/shard_map/all_gather | solution.py:117
  32.7 3.1 %collective-permute-start.1 = (bf16[96,2048]{1,0:T(8,128)(2,1)S(1)}, bf16[96,2048]{1,0:T(8,128)(2,1)S(1)}, u32[]{:S(2)}, u32[]{:S(2)}) collective-permute-start(bf16[96,2048]{1,0:T(8,128)(2,1)S(1)} %bitcast.18), channel_id=1, source_target_pairs={{0,64},{64,128},{128,192},{192,0},{1,65},{65,129},{129,193},{193,1... | collective-permute-start | bytes 1179656 | tf_op jit(solution)/shard_map/ppermute | solution.py:118
  35.8 4.4 %collective-permute-start.2 = (bf16[96,2048]{1,0:T(8,128)(2,1)S(1)}, bf16[96,2048]{1,0:T(8,128)(2,1)S(1)}, u32[]{:S(2)}, u32[]{:S(2)}) collective-permute-start(bf16[96,2048]{1,0:T(8,128)(2,1)S(1)} %bitcast.19), channel_id=1, source_target_pairs={{0,128},{64,192},{128,0},{192,64},{1,129},{65,193},{129,1},{193,65... | collective-permute-start | bytes 1179656 | tf_op jit(solution)/shard_map/ppermute | solution.py:118
  40.2 3.1 %collective-permute-start.3 = (bf16[96,2048]{1,0:T(8,128)(2,1)S(1)}, bf16[96,2048]{1,0:T(8,128)(2,1)S(1)}, u32[]{:S(2)}, u32[]{:S(2)}) collective-permute-start(bf16[96,2048]{1,0:T(8,128)(2,1)S(1)} %bitcast.20), channel_id=1, source_target_pairs={{0,192},{64,0},{128,64},{192,128},{1,193},{65,1},{129,65},{193,129... | collective-permute-start | bytes 1179656 | tf_op jit(solution)/shard_map/ppermute | solution.py:118
  43.3 2.1 constant_dynamic-slice_fusion.8
  45.4 10.8 %collective-permute-start = (bf16[128,2048]{1,0:T(8,128)(2,1)S(1)}, bf16[128,2048]{1,0:T(8,128)(2,1)S(1)}, u32[]{:S(2)}, u32[]{:S(2)}) collective-permute-start(bf16[128,2048]{1,0:T(8,128)(2,1)S(1)} %get-tuple-element.26), channel_id=1, source_target_pairs={{0,1},{1,0},{2,3},{3,2},{4,5},{5,4},{6,7},{7,6},{8,9},{9,8},{10,11... | collective-permute-start | bytes 1572872 | tf_op jit(solution)/shard_map/ppermute | solution.py:110
  56.2 3.2 %collective-permute-start.4 = (bf16[96,2048]{1,0:T(8,128)(2,1)S(1)}, bf16[96,2048]{1,0:T(8,128)(2,1)S(1)}, u32[]{:S(2)}, u32[]{:S(2)}) collective-permute-start(bf16[96,2048]{1,0:T(8,128)(2,1)S(1)} %bitcast.21), channel_id=1, source_target_pairs={{0,256},{256,2},{2,258},{258,0},{1,257},{257,3},{3,259},{259,1},{4... | collective-permute-start | bytes 1179656 | tf_op jit(solution)/shard_map/ppermute | solution.py:119
  59.4 3.4 %collective-permute-start.5 = (bf16[96,2048]{1,0:T(8,128)(2,1)S(1)}, bf16[96,2048]{1,0:T(8,128)(2,1)}, u32[]{:S(2)}, u32[]{:S(2)}) collective-permute-start(bf16[96,2048]{1,0:T(8,128)(2,1)S(1)} %collective-permute-done.1.refs_1_), channel_id=1, source_target_pairs={{0,258},{256,0},{2,256},{258,2},{1,259},{257,1},{3,257},{259,3},{4... | collective-permute-start | bytes 1179656 | tf_op jit(solution)/shard_map/ppermute | solution.py:119
  62.8 3.4 %collective-permute-start.6 = (bf16[96,2048]{1,0:T(8,128)(2,1)S(1)}, bf16[96,2048]{1,0:T(8,128)(2,1)}, u32[]{:S(2)}, u32[]{:S(2)}) collective-permute-start(bf16[96,2048]{1,0:T(8,128)(2,1)S(1)} %collective-permute-done.2.refs_2_), channel_id=1, source_target_pairs={{0,258},{256,0},{2,256},{258,2},{1,259},{257,1},{3,257},{259,3},{4... | collective-permute-start | bytes 1179656 | tf_op jit(solution)/shard_map/ppermute | solution.py:119
  66.2 1.9 collective-permute-start.7
  68.2 2.0 collective-permute-done.4.refs_4_
  70.2 1.7 collective-permute-done.5.refs_5_
  71.9 8.4 %collective-permute-done.6.refs_6_ = bf16[96,2048]{1,0:T(8,128)(2,1)} collective-permute-done((bf16[96,2048]{1,0:T(8,128)(2,1)S(1)}, bf16[96,2048]{1,0:T(8,128)(2,1)}, u32[]{:S(2)}, u32[]{:S(2)}) %collective-permute-start.6) | collective-permute-done | bytes 393248 | tf_op jit(solution)/shard_map/ppermute | solution.py:119
  80.3 5.3 %shard_map.59 = (f32[128,768]{1,0:T(8,128)}, f32[128,768]{1,0:T(8,128)}, bf16[768,2048]{1,0:T(8,128)(2,1)}) custom-call(s32[1]{0:T(128)} %bitcast.side_ref, bf16[128,2048]{1,0:T(8,128)(2,1)} %get-tuple-element.27.qo, bf16[128,2048]{1,0:T(8,128)(2,1)} %copy-done.2, bf16[96,2048]{1,0:T(8,128)(2,1)} %bitcast.22, bf16[96,2048]{1,0:T(8,128)(2,1)} %copy-done.5, ...), custom_call_target="tpu_custom_call" | custom-call | flops 805306368 | bytes 8126468 | tf_op jit(solution)/shard_map/pallas_call | solution.py:36
  85.6 3.2 %collective-permute-start.8 = (f32[128,768]{1,0:T(8,128)}, f32[128,768]{1,0:T(8,128)S(1)}, u32[]{:S(2)}, u32[]{:S(2)}) collective-permute-start(f32[128,768]{1,0:T(8,128)} %get-tuple-element.12), channel_id=1, source_target_pairs={{0,1},{1,0},{2,3},{3,2},{4,5},{5,4},{6,7},{7,6},{8,9},{9,8},{10,11... | collective-permute-start | bytes 1179656 | tf_op jit(solution)/shard_map/ppermute | solution.py:110
  89.1 1.1 constant_dynamic-slice_fusion
  90.3 3.2 %collective-permute-start.17 = (bf16[256,512]{1,0:T(8,128)(2,1)S(1)}, bf16[256,512]{1,0:T(8,128)(2,1)S(1)}, u32[]{:S(2)}, u32[]{:S(2)}) collective-permute-start(bf16[256,512]{1,0:T(8,128)(2,1)S(1)} %pad_maximum_fusion.2), channel_id=1, source_target_pairs={{0,256},{256,2},{2,258},{258,0},{1,257},{257,3},{3,259},{259,1},{4... | collective-permute-start | bytes 786440 | tf_op jit(solution)/shard_map/ppermute | solution.py:125
  93.5 0.7 copy.15.pos
  95.6 0.7 copy-done.9
  96.4 2.4 %shard_map.60.wo.refs_0_ = bf16[128,768]{1,0:T(8,128)(2,1)} custom-call(f32[128,768]{1,0:T(8,128)} %get-tuple-element.11.so, f32[128,768]{1,0:T(8,128)} %copy-done.9, s32[1,768]{1,0:T(1,128)} %fusion.ids, s32[128,1]{1,0:T(8,128)} %copy.15.pos, s32[128,7]{1,0:T(8,128)} %copy.16.neg), custom_call_target="tpu_custom_call" | custom-call | bytes 990208 | tf_op jit(solution)/shard_map/pallas_call | solution.py:36
  98.8 2.9 %collective-permute-start.11 = (bf16[128,768]{1,0:T(8,128)(2,1)}, bf16[128,768]{1,0:T(8,128)(2,1)S(1)}, u32[]{:S(2)}, u32[]{:S(2)}) collective-permute-start(bf16[128,768]{1,0:T(8,128)(2,1)} %shard_map.60.wo.refs_0_), channel_id=1, source_target_pairs={{0,256},{256,2},{2,258},{258,0},{1,257},{257,3},{3,259},{259,1},{4... | collective-permute-start | bytes 589832 | tf_op jit(solution)/shard_map/ppermute | solution.py:144
  101.7 3.5 %collective-permute-start.13 = (bf16[128,768]{1,0:T(8,128)(2,1)}, bf16[128,768]{1,0:T(8,128)(2,1)S(1)}, u32[]{:S(2)}, u32[]{:S(2)}) collective-permute-start(bf16[128,768]{1,0:T(8,128)(2,1)} %shard_map.60.wo.refs_0_), channel_id=1, source_target_pairs={{0,2},{256,258},{2,0},{258,256},{1,3},{257,259},{3,1},{259,257},{4... | collective-permute-start | bytes 589832 | tf_op jit(solution)/shard_map/ppermute | solution.py:144
  105.2 4.0 %collective-permute-start.15 = (bf16[128,768]{1,0:T(8,128)(2,1)}, bf16[128,768]{1,0:T(8,128)(2,1)S(1)}, u32[]{:S(2)}, u32[]{:S(2)}) collective-permute-start(bf16[128,768]{1,0:T(8,128)(2,1)} %shard_map.60.wo.refs_0_), channel_id=1, source_target_pairs={{0,258},{256,0},{2,256},{258,2},{1,259},{257,1},{3,257},{259,3},{4... | collective-permute-start | bytes 589832 | tf_op jit(solution)/shard_map/ppermute | solution.py:144
  109.2 3.0 %collective-permute-start.9 = (bf16[128,768]{1,0:T(8,128)(2,1)}, bf16[128,768]{1,0:T(8,128)(2,1)S(1)}, u32[]{:S(2)}, u32[]{:S(2)}) collective-permute-start(bf16[128,768]{1,0:T(8,128)(2,1)} %shard_map.60.wo.refs_0_), channel_id=1, source_target_pairs={{0,1},{1,0},{2,3},{3,2},{4,5},{5,4},{6,7},{7,6},{8,9},{9,8},{10,11... | collective-permute-start | bytes 589832 | tf_op jit(solution)/shard_map/ppermute | solution.py:110
  112.3 2.3 %collective-permute-start.18 = (bf16[256,512]{1,0:T(8,128)(2,1)S(1)}, bf16[256,512]{1,0:T(8,128)(2,1)S(1)}, u32[]{:S(2)}, u32[]{:S(2)}) collective-permute-start(bf16[256,512]{1,0:T(8,128)(2,1)S(1)} %pad_maximum_fusion.3), channel_id=1, source_target_pairs={{0,2},{256,258},{2,0},{258,256},{1,3},{257,259},{3,1},{259,257},{4... | collective-permute-start | bytes 786440 | tf_op jit(solution)/shard_map/ppermute | solution.py:125
  114.7 3.3 %collective-permute-start.19 = (bf16[256,512]{1,0:T(8,128)(2,1)S(1)}, bf16[256,512]{1,0:T(8,128)(2,1)S(1)}, u32[]{:S(2)}, u32[]{:S(2)}) collective-permute-start(bf16[256,512]{1,0:T(8,128)(2,1)S(1)} %pad_maximum_fusion.4), channel_id=1, source_target_pairs={{0,258},{256,0},{2,256},{258,2},{1,259},{257,1},{3,257},{259,3},{4... | collective-permute-start | bytes 786440 | tf_op jit(solution)/shard_map/ppermute | solution.py:125
  118.0 2.5 %collective-permute-start.12 = (bf16[128,768]{1,0:T(8,128)(2,1)S(1)}, bf16[128,768]{1,0:T(8,128)(2,1)S(1)}, u32[]{:S(2)}, u32[]{:S(2)}) collective-permute-start(bf16[128,768]{1,0:T(8,128)(2,1)S(1)} %collective-permute-done.11.refs_2_), channel_id=1, source_target_pairs={{0,1},{1,0},{2,3},{3,2},{4,5},{5,4},{6,7},{7,6},{8,9},{9,8},{10,11... | collective-permute-start | bytes 589832 | tf_op jit(solution)/shard_map/ppermute | solution.py:110
  120.5 1.9 collective-permute-start.14
  122.4 2.4 %collective-permute-start.16 = (bf16[128,768]{1,0:T(8,128)(2,1)S(1)}, bf16[128,768]{1,0:T(8,128)(2,1)}, u32[]{:S(2)}, u32[]{:S(2)}) collective-permute-start(bf16[128,768]{1,0:T(8,128)(2,1)S(1)} %collective-permute-done.15.refs_6_), channel_id=1, source_target_pairs={{0,1},{1,0},{2,3},{3,2},{4,5},{5,4},{6,7},{7,6},{8,9},{9,8},{10,11... | collective-permute-start | bytes 589832 | tf_op jit(solution)/shard_map/ppermute | solution.py:110
  124.9 4.4 %shard_map.61 = (f32[128,2048]{1,0:T(8,128)}, f32[128,2048]{1,0:T(8,128)}) custom-call(bf16[128,768]{1,0:T(8,128)(2,1)} %shard_map.60.wo.refs_0_, bf16[128,768]{1,0:T(8,128)(2,1)} %copy-done.13, bf16[768,2048]{1,0:T(8,128)(2,1)} %get-tuple-element.13.pool), custom_call_target="tpu_custom_call" | custom-call | flops 805306368 | bytes 5636096 | tf_op jit(solution)/shard_map/pallas_call | solution.py:36
  129.3 1.9 collective-permute-start.10
  132.7 3.8 %shard_map.62 = (f32[192,512]{1,0:T(8,128)}, f32[192,512]{1,0:T(8,128)}, f32[192,512]{1,0:T(8,128)}, f32[192,512]{1,0:T(8,128)}) custom-call(bf16[128,768]{1,0:T(8,128)(2,1)} %shard_map.60.wo.refs_0_, bf16[128,768]{1,0:T(8,128)(2,1)} %copy-done.13, bf16[128,768]{1,0:T(8,128)(2,1)} %copy-done.19, bf16[128,768]{1,0:T(8,128)(2,1)} %copy-done.22, ...), custom_call_target="tpu_custom_call" | custom-call | flops 805306368 | bytes 4194304 | tf_op jit(solution)/shard_map/pallas_call | solution.py:36
  136.5 1.9 collective-permute-start.20
  138.5 4.0 %collective-permute-start.21 = (f32[192,512]{1,0:T(8,128)}, f32[192,512]{1,0:T(8,128)S(1)}, u32[]{:S(2)}, u32[]{:S(2)}) collective-permute-start(f32[192,512]{1,0:T(8,128)} %get-tuple-element.18), channel_id=1, source_target_pairs={{0,128},{64,192},{128,0},{192,64},{1,129},{65,193},{129,1},{193,65... | collective-permute-start | bytes 1179656 | tf_op jit(solution)/shard_map/ppermute | solution.py:151
  142.5 1.9 collective-permute-start.22
  144.4 4.4 %collective-permute-done.20.b = f32[192,512]{1,0:T(8,128)S(1)} collective-permute-done((f32[192,512]{1,0:T(8,128)}, f32[192,512]{1,0:T(8,128)S(1)}, u32[]{:S(2)}, u32[]{:S(2)}) %collective-permute-start.20) | collective-permute-done | bytes 393248 | tf_op jit(solution)/shard_map/ppermute | solution.py:151
  148.8 3.5 %collective-permute-done.21.c = f32[192,512]{1,0:T(8,128)S(1)} collective-permute-done((f32[192,512]{1,0:T(8,128)}, f32[192,512]{1,0:T(8,128)S(1)}, u32[]{:S(2)}, u32[]{:S(2)}) %collective-permute-start.21) | collective-permute-done | bytes 393248 | tf_op jit(solution)/shard_map/ppermute | solution.py:151
  152.3 9.2 %collective-permute-done.22.d = f32[192,512]{1,0:T(8,128)S(1)} collective-permute-done((f32[192,512]{1,0:T(8,128)}, f32[192,512]{1,0:T(8,128)S(1)}, u32[]{:S(2)}, u32[]{:S(2)}) %collective-permute-start.22) | collective-permute-done | bytes 393248 | tf_op jit(solution)/shard_map/ppermute | solution.py:151
  161.5 0.8 copy-done.12
  162.3 2.3 %shard_map.63 = f32[192,512]{1,0:T(8,128)} custom-call(f32[192,512]{1,0:T(8,128)} %get-tuple-element.16.a, f32[192,512]{1,0:T(8,128)} %copy-done.10, f32[192,512]{1,0:T(8,128)} %copy-done.11, f32[192,512]{1,0:T(8,128)} %copy-done.12), custom_call_target="tpu_custom_call" | custom-call | bytes 1966080 | tf_op jit(solution)/shard_map/pallas_call | solution.py:36
  164.5 1.1 broadcast_in_dim_reshape.3
  165.7 0.8 copy.17
  166.4 6.4 %all-to-all-start = ((f32[1,2,16,6,4,128]{5,4,3,1,0,2:T(4,128)}), f32[1,2,16,6,4,128]{5,4,3,1,0,2:T(4,128)S(1)}, u32[]{:S(2)}, u32[]{:S(2)}) async-start(f32[1,2,16,6,4,128]{5,4,3,1,0,2:T(4,128)} %copy.17), calls=%async_computation | async-start | bytes 786432 | tf_op jit(solution)/shard_map/all_to_all | solution.py:163
  173.0 1.5 pad_maximum_fusion
  174.5 15.9 %all-to-all-done = f32[1,2,16,6,4,128]{5,4,3,1,0,2:T(4,128)S(1)} async-done(((f32[1,2,16,6,4,128]{5,4,3,1,0,2:T(4,128)}), f32[1,2,16,6,4,128]{5,4,3,1,0,2:T(4,128)S(1)}, u32[]{:S(2)}, u32[]{:S(2)}) %all-to-all-start) | async-done | bytes 393248 | tf_op jit(solution)/shard_map/all_to_all | solution.py:163
  190.5 21.2 %all_gather.7 = f32[8,2,6,512]{3,1,2,0:T(2,128)S(1)} all-gather(f32[1,2,6,512]{3,1,2,0:T(2,128)S(1)} %all_gather_reshape.3), channel_id=1, replica_groups=mesh['yl'=2,'x'=4,'z'=16,'yh'=2,'c'=2] {'yl','yh','c'}, dimensions={0}, use_global_device_ids=true | all-gather | bytes 221184 | tf_op jit(solution)/shard_map/all_gather | solution.py:165
  212.0 0.7 reshape.244
  (80 shorter events, 4.0 us)
Async XLA Ops:
  0.6 0.8 copy-start
  32.7 47.6 %copy-start.3 = (bf16[12,8,16,128]{3,1,2,0:T(8,128)(2,1)}, bf16[12,8,16,128]{3,1,2,0:T(8,128)(2,1)S(1)}, u32[]{:S(2)}) copy-start(bf16[12,8,16,128]{3,1,2,0:T(8,128)(2,1)S(1)} %copy.27) | copy-start | bytes 1179652
  32.7 26.7 %collective-permute-start.1 = (bf16[96,2048]{1,0:T(8,128)(2,1)S(1)}, bf16[96,2048]{1,0:T(8,128)(2,1)S(1)}, u32[]{:S(2)}, u32[]{:S(2)}) collective-permute-start(bf16[96,2048]{1,0:T(8,128)(2,1)S(1)} %bitcast.18), channel_id=1, source_target_pairs={{0,64},{64,128},{128,192},{192,0},{1,65},{65,129},{129,193},{193,1... | collective-permute-start | bytes 1179656 | tf_op jit(solution)/shard_map/ppermute | solution.py:118
  35.8 27.0 %collective-permute-start.2 = (bf16[96,2048]{1,0:T(8,128)(2,1)S(1)}, bf16[96,2048]{1,0:T(8,128)(2,1)S(1)}, u32[]{:S(2)}, u32[]{:S(2)}) collective-permute-start(bf16[96,2048]{1,0:T(8,128)(2,1)S(1)} %bitcast.19), channel_id=1, source_target_pairs={{0,128},{64,192},{128,0},{192,64},{1,129},{65,193},{129,1},{193,65... | collective-permute-start | bytes 1179656 | tf_op jit(solution)/shard_map/ppermute | solution.py:118
  40.2 26.0 %collective-permute-start.3 = (bf16[96,2048]{1,0:T(8,128)(2,1)S(1)}, bf16[96,2048]{1,0:T(8,128)(2,1)S(1)}, u32[]{:S(2)}, u32[]{:S(2)}) collective-permute-start(bf16[96,2048]{1,0:T(8,128)(2,1)S(1)} %bitcast.20), channel_id=1, source_target_pairs={{0,192},{64,0},{128,64},{192,128},{1,193},{65,1},{129,65},{193,129... | collective-permute-start | bytes 1179656 | tf_op jit(solution)/shard_map/ppermute | solution.py:118
  45.4 24.8 %collective-permute-start = (bf16[128,2048]{1,0:T(8,128)(2,1)S(1)}, bf16[128,2048]{1,0:T(8,128)(2,1)S(1)}, u32[]{:S(2)}, u32[]{:S(2)}) collective-permute-start(bf16[128,2048]{1,0:T(8,128)(2,1)S(1)} %get-tuple-element.26), channel_id=1, source_target_pairs={{0,1},{1,0},{2,3},{3,2},{4,5},{5,4},{6,7},{7,6},{8,9},{9,8},{10,11... | collective-permute-start | bytes 1572872 | tf_op jit(solution)/shard_map/ppermute | solution.py:110
  56.2 14.0 %collective-permute-start.4 = (bf16[96,2048]{1,0:T(8,128)(2,1)S(1)}, bf16[96,2048]{1,0:T(8,128)(2,1)S(1)}, u32[]{:S(2)}, u32[]{:S(2)}) collective-permute-start(bf16[96,2048]{1,0:T(8,128)(2,1)S(1)} %bitcast.21), channel_id=1, source_target_pairs={{0,256},{256,2},{2,258},{258,0},{1,257},{257,3},{3,259},{259,1},{4... | collective-permute-start | bytes 1179656 | tf_op jit(solution)/shard_map/ppermute | solution.py:119
  59.4 20.9 %copy-start.5 = (bf16[96,2048]{1,0:T(8,128)(2,1)}, bf16[96,2048]{1,0:T(8,128)(2,1)S(1)}, u32[]{:S(2)}) copy-start(bf16[96,2048]{1,0:T(8,128)(2,1)S(1)} %collective-permute-done.1.refs_1_) | copy-start | bytes 1179652
  59.4 12.4 %collective-permute-start.5 = (bf16[96,2048]{1,0:T(8,128)(2,1)S(1)}, bf16[96,2048]{1,0:T(8,128)(2,1)}, u32[]{:S(2)}, u32[]{:S(2)}) collective-permute-start(bf16[96,2048]{1,0:T(8,128)(2,1)S(1)} %collective-permute-done.1.refs_1_), channel_id=1, source_target_pairs={{0,258},{256,0},{2,256},{258,2},{1,259},{257,1},{3,257},{259,3},{4... | collective-permute-start | bytes 1179656 | tf_op jit(solution)/shard_map/ppermute | solution.py:119
  62.8 17.5 %copy-start.6 = (bf16[96,2048]{1,0:T(8,128)(2,1)}, bf16[96,2048]{1,0:T(8,128)(2,1)S(1)}, u32[]{:S(2)}) copy-start(bf16[96,2048]{1,0:T(8,128)(2,1)S(1)} %collective-permute-done.2.refs_2_) | copy-start | bytes 1179652
  62.8 17.5 %collective-permute-start.6 = (bf16[96,2048]{1,0:T(8,128)(2,1)S(1)}, bf16[96,2048]{1,0:T(8,128)(2,1)}, u32[]{:S(2)}, u32[]{:S(2)}) collective-permute-start(bf16[96,2048]{1,0:T(8,128)(2,1)S(1)} %collective-permute-done.2.refs_2_), channel_id=1, source_target_pairs={{0,258},{256,0},{2,256},{258,2},{1,259},{257,1},{3,257},{259,3},{4... | collective-permute-start | bytes 1179656 | tf_op jit(solution)/shard_map/ppermute | solution.py:119
  66.2 14.1 %copy-start.7 = (bf16[96,2048]{1,0:T(8,128)(2,1)}, bf16[96,2048]{1,0:T(8,128)(2,1)S(1)}, u32[]{:S(2)}) copy-start(bf16[96,2048]{1,0:T(8,128)(2,1)S(1)} %collective-permute-done.3.refs_3_) | copy-start | bytes 1179652
  66.2 14.1 %collective-permute-start.7 = (bf16[96,2048]{1,0:T(8,128)(2,1)S(1)}, bf16[96,2048]{1,0:T(8,128)(2,1)}, u32[]{:S(2)}, u32[]{:S(2)}) collective-permute-start(bf16[96,2048]{1,0:T(8,128)(2,1)S(1)} %collective-permute-done.3.refs_3_), channel_id=1, source_target_pairs={{0,256},{256,2},{2,258},{258,0},{1,257},{257,3},{3,259},{259,1},{4... | collective-permute-start | bytes 1179656 | tf_op jit(solution)/shard_map/ppermute | solution.py:119
  70.2 10.1 %copy-start.8 = (bf16[96,2048]{1,0:T(8,128)(2,1)}, bf16[96,2048]{1,0:T(8,128)(2,1)S(1)}, u32[]{:S(2)}) copy-start(bf16[96,2048]{1,0:T(8,128)(2,1)S(1)} %collective-permute-done.4.refs_4_) | copy-start | bytes 1179652
  70.2 10.1 %copy-start.2 = (bf16[128,2048]{1,0:T(8,128)(2,1)}, bf16[128,2048]{1,0:T(8,128)(2,1)S(1)}, u32[]{:S(2)}) copy-start(bf16[128,2048]{1,0:T(8,128)(2,1)S(1)} %collective-permute-done.qx) | copy-start | bytes 1572868
  80.3 8.5 %copy-start.1 = (bf16[128,4096]{1,0:T(8,128)(2,1)S(1)}, bf16[128,4096]{1,0:T(8,128)(2,1)}, u32[]{:S(2)}) copy-start(bf16[128,4096]{1,0:T(8,128)(2,1)} %param.4) | copy-start | bytes 3145732
  85.6 7.9 %copy-start.15 = (s32[128]{0:T(128)S(1)}, s32[128]{0:T(128)}, u32[]{:S(2)}) copy-start(s32[128]{0:T(128)} %param.6) | copy-start | bytes 1540
  85.6 8.6 %copy-start.14 = (s32[128,7]{0,1:T(8,128)S(1)}, s32[128,7]{0,1:T(8,128)}, u32[]{:S(2)}) copy-start(s32[128,7]{0,1:T(8,128)} %param.7) | copy-start | bytes 10756
  85.6 10.0 %collective-permute-start.8 = (f32[128,768]{1,0:T(8,128)}, f32[128,768]{1,0:T(8,128)S(1)}, u32[]{:S(2)}, u32[]{:S(2)}) collective-permute-start(f32[128,768]{1,0:T(8,128)} %get-tuple-element.12), channel_id=1, source_target_pairs={{0,1},{1,0},{2,3},{3,2},{4,5},{5,4},{6,7},{7,6},{8,9},{9,8},{10,11... | collective-permute-start | bytes 1179656 | tf_op jit(solution)/shard_map/ppermute | solution.py:110
  90.3 22.0 %collective-permute-start.17 = (bf16[256,512]{1,0:T(8,128)(2,1)S(1)}, bf16[256,512]{1,0:T(8,128)(2,1)S(1)}, u32[]{:S(2)}, u32[]{:S(2)}) collective-permute-start(bf16[256,512]{1,0:T(8,128)(2,1)S(1)} %pad_maximum_fusion.2), channel_id=1, source_target_pairs={{0,256},{256,2},{2,258},{258,0},{1,257},{257,3},{3,259},{259,1},{4... | collective-permute-start | bytes 786440 | tf_op jit(solution)/shard_map/ppermute | solution.py:125
  95.6 0.7 copy-start.9
  98.8 15.8 %collective-permute-start.11 = (bf16[128,768]{1,0:T(8,128)(2,1)}, bf16[128,768]{1,0:T(8,128)(2,1)S(1)}, u32[]{:S(2)}, u32[]{:S(2)}) collective-permute-start(bf16[128,768]{1,0:T(8,128)(2,1)} %shard_map.60.wo.refs_0_), channel_id=1, source_target_pairs={{0,256},{256,2},{2,258},{258,0},{1,257},{257,3},{3,259},{259,1},{4... | collective-permute-start | bytes 589832 | tf_op jit(solution)/shard_map/ppermute | solution.py:144
  101.7 16.2 %collective-permute-start.13 = (bf16[128,768]{1,0:T(8,128)(2,1)}, bf16[128,768]{1,0:T(8,128)(2,1)S(1)}, u32[]{:S(2)}, u32[]{:S(2)}) collective-permute-start(bf16[128,768]{1,0:T(8,128)(2,1)} %shard_map.60.wo.refs_0_), channel_id=1, source_target_pairs={{0,2},{256,258},{2,0},{258,256},{1,3},{257,259},{3,1},{259,257},{4... | collective-permute-start | bytes 589832 | tf_op jit(solution)/shard_map/ppermute | solution.py:144
  105.2 15.3 %collective-permute-start.15 = (bf16[128,768]{1,0:T(8,128)(2,1)}, bf16[128,768]{1,0:T(8,128)(2,1)S(1)}, u32[]{:S(2)}, u32[]{:S(2)}) collective-permute-start(bf16[128,768]{1,0:T(8,128)(2,1)} %shard_map.60.wo.refs_0_), channel_id=1, source_target_pairs={{0,258},{256,0},{2,256},{258,2},{1,259},{257,1},{3,257},{259,3},{4... | collective-permute-start | bytes 589832 | tf_op jit(solution)/shard_map/ppermute | solution.py:144
  109.2 13.2 %collective-permute-start.9 = (bf16[128,768]{1,0:T(8,128)(2,1)}, bf16[128,768]{1,0:T(8,128)(2,1)S(1)}, u32[]{:S(2)}, u32[]{:S(2)}) collective-permute-start(bf16[128,768]{1,0:T(8,128)(2,1)} %shard_map.60.wo.refs_0_), channel_id=1, source_target_pairs={{0,1},{1,0},{2,3},{3,2},{4,5},{5,4},{6,7},{7,6},{8,9},{9,8},{10,11... | collective-permute-start | bytes 589832 | tf_op jit(solution)/shard_map/ppermute | solution.py:110
  112.3 19.6 %copy-start.16 = (bf16[256,512]{1,0:T(8,128)(2,1)}, bf16[256,512]{1,0:T(8,128)(2,1)S(1)}, u32[]{:S(2)}) copy-start(bf16[256,512]{1,0:T(8,128)(2,1)S(1)} %collective-permute-done.17.refs_9_) | copy-start | bytes 786436
  112.3 17.0 %collective-permute-start.18 = (bf16[256,512]{1,0:T(8,128)(2,1)S(1)}, bf16[256,512]{1,0:T(8,128)(2,1)S(1)}, u32[]{:S(2)}, u32[]{:S(2)}) collective-permute-start(bf16[256,512]{1,0:T(8,128)(2,1)S(1)} %pad_maximum_fusion.3), channel_id=1, source_target_pairs={{0,2},{256,258},{2,0},{258,256},{1,3},{257,259},{3,1},{259,257},{4... | collective-permute-start | bytes 786440 | tf_op jit(solution)/shard_map/ppermute | solution.py:125
  114.7 17.3 %copy-start.19 = (bf16[128,768]{1,0:T(8,128)(2,1)}, bf16[128,768]{1,0:T(8,128)(2,1)S(1)}, u32[]{:S(2)}) copy-start(bf16[128,768]{1,0:T(8,128)(2,1)S(1)} %collective-permute-done.11.refs_2_) | copy-start | bytes 589828
  114.7 17.2 %collective-permute-start.19 = (bf16[256,512]{1,0:T(8,128)(2,1)S(1)}, bf16[256,512]{1,0:T(8,128)(2,1)S(1)}, u32[]{:S(2)}, u32[]{:S(2)}) collective-permute-start(bf16[256,512]{1,0:T(8,128)(2,1)S(1)} %pad_maximum_fusion.4), channel_id=1, source_target_pairs={{0,258},{256,0},{2,256},{258,2},{1,259},{257,1},{3,257},{259,3},{4... | collective-permute-start | bytes 786440 | tf_op jit(solution)/shard_map/ppermute | solution.py:125
  118.0 14.0 %copy-start.20 = (bf16[128,768]{1,0:T(8,128)(2,1)}, bf16[128,768]{1,0:T(8,128)(2,1)S(1)}, u32[]{:S(2)}) copy-start(bf16[128,768]{1,0:T(8,128)(2,1)S(1)} %collective-permute-done.13.refs_4_) | copy-start | bytes 589828
  118.0 13.9 %collective-permute-start.12 = (bf16[128,768]{1,0:T(8,128)(2,1)S(1)}, bf16[128,768]{1,0:T(8,128)(2,1)S(1)}, u32[]{:S(2)}, u32[]{:S(2)}) collective-permute-start(bf16[128,768]{1,0:T(8,128)(2,1)S(1)} %collective-permute-done.11.refs_2_), channel_id=1, source_target_pairs={{0,1},{1,0},{2,3},{3,2},{4,5},{5,4},{6,7},{7,6},{8,9},{9,8},{10,11... | collective-permute-start | bytes 589832 | tf_op jit(solution)/shard_map/ppermute | solution.py:110
  120.5 11.5 %copy-start.21 = (bf16[128,768]{1,0:T(8,128)(2,1)}, bf16[128,768]{1,0:T(8,128)(2,1)S(1)}, u32[]{:S(2)}) copy-start(bf16[128,768]{1,0:T(8,128)(2,1)S(1)} %collective-permute-done.15.refs_6_) | copy-start | bytes 589828
  120.5 11.4 %collective-permute-start.14 = (bf16[128,768]{1,0:T(8,128)(2,1)S(1)}, bf16[128,768]{1,0:T(8,128)(2,1)S(1)}, u32[]{:S(2)}, u32[]{:S(2)}) collective-permute-start(bf16[128,768]{1,0:T(8,128)(2,1)S(1)} %collective-permute-done.13.refs_4_), channel_id=1, source_target_pairs={{0,1},{1,0},{2,3},{3,2},{4,5},{5,4},{6,7},{7,6},{8,9},{9,8},{10,11... | collective-permute-start | bytes 589832 | tf_op jit(solution)/shard_map/ppermute | solution.py:110
  122.4 2.4 %copy-start.13 = (bf16[128,768]{1,0:T(8,128)(2,1)}, bf16[128,768]{1,0:T(8,128)(2,1)S(1)}, u32[]{:S(2)}) copy-start(bf16[128,768]{1,0:T(8,128)(2,1)S(1)} %collective-permute-done.9.wx.refs_1_) | copy-start | bytes 589828
  122.4 9.5 %collective-permute-start.16 = (bf16[128,768]{1,0:T(8,128)(2,1)S(1)}, bf16[128,768]{1,0:T(8,128)(2,1)}, u32[]{:S(2)}, u32[]{:S(2)}) collective-permute-start(bf16[128,768]{1,0:T(8,128)(2,1)S(1)} %collective-permute-done.15.refs_6_), channel_id=1, source_target_pairs={{0,1},{1,0},{2,3},{3,2},{4,5},{5,4},{6,7},{7,6},{8,9},{9,8},{10,11... | collective-permute-start | bytes 589832 | tf_op jit(solution)/shard_map/ppermute | solution.py:110
  129.3 2.7 %copy-start.17 = (bf16[256,512]{1,0:T(8,128)(2,1)}, bf16[256,512]{1,0:T(8,128)(2,1)S(1)}, u32[]{:S(2)}) copy-start(bf16[256,512]{1,0:T(8,128)(2,1)S(1)} %collective-permute-done.18.refs_10_) | copy-start | bytes 786436
  129.3 43.6 %collective-permute-start.10 = (f32[128,2048]{1,0:T(8,128)}, f32[128,2048]{1,0:T(8,128)S(1)}, u32[]{:S(2)}, u32[]{:S(2)}) collective-permute-start(f32[128,2048]{1,0:T(8,128)} %get-tuple-element.15), channel_id=1, source_target_pairs={{0,1},{1,0},{2,3},{3,2},{4,5},{5,4},{6,7},{7,6},{8,9},{9,8},{10,11... | collective-permute-start | bytes 3145736 | tf_op jit(solution)/shard_map/ppermute | solution.py:110
  131.9 0.7 copy-start.18
  131.9 0.8 copy-start.22
  131.9 0.8 copy-start.23
  136.5 12.3 %collective-permute-start.20 = (f32[192,512]{1,0:T(8,128)}, f32[192,512]{1,0:T(8,128)S(1)}, u32[]{:S(2)}, u32[]{:S(2)}) collective-permute-start(f32[192,512]{1,0:T(8,128)} %get-tuple-element.17), channel_id=1, source_target_pairs={{0,192},{64,0},{128,64},{192,128},{1,193},{65,1},{129,65},{193,129... | collective-permute-start | bytes 1179656 | tf_op jit(solution)/shard_map/ppermute | solution.py:151
  138.5 13.8 %collective-permute-start.21 = (f32[192,512]{1,0:T(8,128)}, f32[192,512]{1,0:T(8,128)S(1)}, u32[]{:S(2)}, u32[]{:S(2)}) collective-permute-start(f32[192,512]{1,0:T(8,128)} %get-tuple-element.18), channel_id=1, source_target_pairs={{0,128},{64,192},{128,0},{192,64},{1,129},{65,193},{129,1},{193,65... | collective-permute-start | bytes 1179656 | tf_op jit(solution)/shard_map/ppermute | solution.py:151
  142.5 19.1 %collective-permute-start.22 = (f32[192,512]{1,0:T(8,128)}, f32[192,512]{1,0:T(8,128)S(1)}, u32[]{:S(2)}, u32[]{:S(2)}) collective-permute-start(f32[192,512]{1,0:T(8,128)} %get-tuple-element.19), channel_id=1, source_target_pairs={{0,64},{64,128},{128,192},{192,0},{1,65},{65,129},{129,193},{193,1... | collective-permute-start | bytes 1179656 | tf_op jit(solution)/shard_map/ppermute | solution.py:151
  148.8 12.7 %copy-start.10 = (f32[192,512]{1,0:T(8,128)}, f32[192,512]{1,0:T(8,128)S(1)}, u32[]{:S(2)}) copy-start(f32[192,512]{1,0:T(8,128)S(1)} %collective-permute-done.20.b) | copy-start | bytes 1179652
  152.3 9.2 %copy-start.11 = (f32[192,512]{1,0:T(8,128)}, f32[192,512]{1,0:T(8,128)S(1)}, u32[]{:S(2)}) copy-start(f32[192,512]{1,0:T(8,128)S(1)} %collective-permute-done.21.c) | copy-start | bytes 1179652
  161.5 0.8 copy-start.12
  162.3 10.6 %copy-start.4 = (f32[128,2048]{1,0:T(8,128)S(1)}, f32[128,2048]{1,0:T(8,128)}, u32[]{:S(2)}) copy-start(f32[128,2048]{1,0:T(8,128)} %get-tuple-element.14) | copy-start | bytes 3145732
  166.4 24.0 %all-to-all-start = ((f32[1,2,16,6,4,128]{5,4,3,1,0,2:T(4,128)}), f32[1,2,16,6,4,128]{5,4,3,1,0,2:T(4,128)S(1)}, u32[]{:S(2)}, u32[]{:S(2)}) async-start(f32[1,2,16,6,4,128]{5,4,3,1,0,2:T(4,128)} %copy.17), calls=%async_computation | async-start | bytes 786432 | tf_op jit(solution)/shard_map/all_to_all | solution.py:163

commit v2 on v1

v2 whole, which is shorter than its diff:
```python
import jax
import jax.numpy as jnp
from jax import lax
from jax.experimental import pallas as pl
from jax.experimental.pallas import tpu as pltpu
from jax.sharding import Mesh
from jax.sharding import PartitionSpec as P

D = 4096
HALF = 2048
SLICE = 512
QDEV = 128
NP = 768
ROWS = 96
SIDE = 384
Y = ("yl", "yh")
VMEM_LIMIT = 60 * 1024 * 1024
F32, BF16 = jnp.float32, jnp.bfloat16


def shift(count, by):
    return [(i, (i + by) % count) for i in range(count)]


def along_y(by):
    place = lambda y: 2 * (y % 2) + y // 2
    return [(place(y), place((y + by) % 4)) for y in range(4)]


def call(kernel, outs, *args, smem=0, after=0, scratch=(), flops=0):
    count = len(args)
    in_specs = [pl.BlockSpec(memory_space=pltpu.SMEM)] * smem
    in_specs += [pl.BlockSpec(memory_space=pltpu.VMEM)] * (count - smem - after)
    in_specs += [pl.BlockSpec(memory_space=pl.ANY)] * after
    body = kernel
    if after:
        body = lambda *refs: kernel(*refs[: count - after], *refs[count:])
    size = sum(a.size * a.dtype.itemsize for a in args) + sum(o.size * o.dtype.itemsize for o in outs)
    return pl.pallas_call(
        body,
        out_shape=outs,
        in_specs=in_specs,
        out_specs=[pl.BlockSpec(memory_space=pltpu.VMEM)] * len(outs),
        scratch_shapes=list(scratch),
        compiler_params=pltpu.CompilerParams(vmem_limit_bytes=VMEM_LIMIT),
        cost_estimate=pl.CostEstimate(flops=flops, bytes_accessed=size, transcendentals=0),
    )(*args)


def score_kernel(side_ref, qo, qx, *refs):
    pieces, (so, sx, pool), q2 = refs[:8], refs[8:11], refs[11]
    q2[:QDEV] = qo[...]
    q2[QDEV:] = qx[...]
    side = side_ref[0]
    for t in range(2):
        base = (side if t == 0 else 1 - side) * SIDE
        for s in range(4):
            pool[pl.ds(pl.multiple_of(base + ROWS * s, 32), ROWS), :] = pieces[4 * t + s][...]
    for n in range(3):
        cols = slice(256 * n, 256 * n + 256)
        part = lax.dot_general(q2[...], pool[cols, :], (((1,), (1,)), ((), ())), preferred_element_type=F32)
        so[:, cols] = part[:QDEV]
        sx[:, cols] = part[QDEV:]


def loss_kernel(so, sr, ids, pos, neg, w):
    scores = (so[...] + sr[...]) * 0.0625
    column = ids[...]
    count = jnp.ones(scores.shape, F32)
    for k in range(7):
        count += jnp.where(neg[:, k : k + 1] == column, 1.0, 0.0)
    top = jnp.max(scores, axis=1, keepdims=True)
    mass = jnp.exp(scores - top) * count
    total = jnp.sum(mass, axis=1, keepdims=True)
    rounded = (mass / total - jnp.where(pos[...] == column, 1.0, 0.0)).astype(BF16)
    for i in range(4):
        w[i] = rounded


def query_kernel(here_ref, wo, wx, pool, go, gx, w2):
    here = here_ref[0]
    w2[:QDEV] = wo[here]
    w2[QDEV:] = wx[here]
    for n in range(HALF // 512):
        cols = slice(512 * n, 512 * n + 512)
        part = jnp.dot(w2[...], pool[:, cols], preferred_element_type=F32) * 0.0625
        go[:, cols] = part[:QDEV]
        gx[:, cols] = part[QDEV:]


def pool_kernel(at_ref, w_own, w_oth, qs, out, w_all):
    core, x = at_ref[0], at_ref[1]
    for i in range(4):
        for own, w in ((core, w_own), (1 - core, w_oth)):
            w_all[pl.ds(pl.multiple_of((2 * i + own) * QDEV, QDEV), QDEV), :] = w[i]
    for n in range(3):
        part = lax.dot_general(
            w_all[:, 256 * n : 256 * n + 256], qs[...], (((0,), (0,)), ((), ())), preferred_element_type=F32
        ) * 0.0625
        for lo in range(256 * n, 256 * n + 256, 32):
            side, rest = divmod(lo, SIDE)
            s, row = divmod(rest, ROWS)
            at = (x + 4 - s) % 4
            out[at, ROWS * side + row : ROWS * side + row + 32, :] = part[lo - 256 * n : lo - 256 * n + 32]


def x_sum_kernel(parts, out):
    total = (parts[0] + parts[1]) + (parts[2] + parts[3])
    for z in range(16):
        for side in range(2):
            rows = total[ROWS * side + 6 * z : ROWS * side + 6 * z + 6]
            for j in range(4):
                at = (4 * side + j) * 6
                out[z, at : at + 6, :] = rows[:, 128 * j : 128 * j + 128]


def z_sum_kernel(parts, out):
    total = parts[0]
    for z in range(1, 16):
        total = total + parts[z]
    for i in range(8):
        side = i // 4
        out[i] = total[24 * side : 24 * side + 24]


def last_kernel(parts, out):
    for i in range(8):
        yl, yh, core = i // 4, (i // 2) % 2, i % 2
        for j in range(4):
            at = core * HALF + (2 * yh + yl) * SLICE + 128 * j
            out[:, at : at + 128] = parts[i, 6 * j : 6 * j + 6, :]


def shards(queries, passages, positives, negatives):
    core = lax.axis_index("c")
    x = lax.axis_index("x")
    yl = lax.axis_index("yl")
    other = lambda a: lax.ppermute(a, "c", shift(2, 1))
    swap = lambda a, axes: lax.all_to_all(a, axes, 0, 0, tiled=True)
    sd = jax.ShapeDtypeStruct

    mine = lax.dynamic_slice(passages, (0, core * HALF), (6, HALF)).reshape(6, 16, 128)
    block = swap(jnp.broadcast_to(mine[None], (16, 6, 16, 128)), "z").reshape(ROWS, HALF)
    near = [block] + [lax.ppermute(block, "x", shift(4, s)) for s in range(1, 4)]
    far = [lax.ppermute(b, Y, along_y(1 if s in (0, 3) else -1)) for s, b in enumerate(near)]

    q_own = lax.dynamic_slice(queries, (0, core * HALF), (QDEV, HALF))
    q_oth = other(lax.dynamic_slice(queries, (0, (1 - core) * HALF), (QDEV, HALF)))
    slices = queries.reshape(QDEV, 2, 2, 2, SLICE).transpose(3, 2, 1, 0, 4)
    group = swap(slices.reshape(8, QDEV, SLICE), Y + ("c",))

    s_own, s_out, pool = call(
        score_kernel,
        [sd((QDEV, NP), F32), sd((QDEV, NP), F32), sd((NP, HALF), BF16)],
        yl.reshape(1), q_own, q_oth, *near, *far, group,
        smem=1, after=1, scratch=[pltpu.VMEM((2 * QDEV, HALF), BF16)], flops=2 * 256 * NP * HALF,
    )
    s_oth = other(s_out)

    col = jnp.arange(NP, dtype=jnp.int32)
    side, s, z, r = col // SIDE, (col // ROWS) % 4, (col // 6) % 16, col % 6
    ids = ((side * 4 + (x - s) % 4) * 16 + z) * 6 + r
    w4 = call(
        loss_kernel, [sd((4, QDEV, NP), BF16)],
        s_own, s_oth, ids.reshape(1, NP), positives.reshape(QDEV, 1), negatives,
    )[0]
    w_own = swap(w4, Y)
    w_oth = other(w_own)
    blocks = call(
        pool_kernel, [sd((4, 2 * ROWS, SLICE), F32)],
        jnp.stack([core, x]), w_own, w_oth, group.reshape(8 * QDEV, SLICE),
        smem=1, scratch=[pltpu.VMEM((1024, NP), BF16)], flops=2 * 1024 * NP * SLICE,
    )[0]
    by_x = swap(blocks, "x")

    here = 2 * yl + lax.axis_index("yh")
    g_own, g_out = call(
        query_kernel, [sd((QDEV, HALF), F32)] * 2, here.reshape(1), w_own, w_oth, pool, blocks,
        smem=1, after=1, scratch=[pltpu.VMEM((2 * QDEV, NP), BF16)], flops=2 * 256 * NP * HALF,
    )
    g_oth = other(g_out)
    low = jnp.where(core == 0, g_own, g_oth)
    high = jnp.where(core == 0, g_oth, g_own)
    query_grad = jnp.concatenate([low, high], axis=1)

    by_z = swap(call(x_sum_kernel, [sd((16, 48, 128), F32)], by_x)[0], "z")
    by_y = swap(call(z_sum_kernel, [sd((8, 24, 128), F32)], by_z)[0], Y + ("c",))
    passage_grad = call(last_kernel, [sd((6, D), F32)], by_y)[0]
    return query_grad, passage_grad


def solution(mesh):
    fine = Mesh(mesh.devices.reshape(2, 4, 16, 2, 2), ("yl", "x", "z", "yh", "c"))
    every, pooled = ("yl", "x", "z", "yh", "c"), ("yl", "x", "z")
    return jax.shard_map(
        shards,
        mesh=fine,
        in_specs=(P(every, None), P(pooled, None), P(every), P(every, None)),
        out_specs=(P(every, None), P(pooled, None)),
        check_vma=False,
    )
```

time: 214 us -> 199 us (0.930)
  blocking collectives: 52.3 us -> 15.4 us
  waiting for transfers between devices: 45.1 us -> 61.8 us
  Pallas kernels: 18.2 us -> 22 us
    all_gather x2 -> x0, blocking collectives: 52.3 us -> none  [the longest x1 31.1 us: shards(): block = lax.all_gather(mine, 'z', axis=0, tiled=True).reshape(ROWS, HALF)]
    all_to_all x1 -> x5, starting transfers between devices: 6.39 us -> 46.2 us  [shards(): swap = lambda a, axes: lax.all_to_all(a, axes, 0, 0, tiled=True)]
    all_to_all x1 -> x5, waiting for transfers between devices: 15.9 us -> 47.6 us  [shards(): swap = lambda a, axes: lax.all_to_all(a, axes, 0, 0, tiled=True)]
    ppermute x9 -> x0, starting transfers between devices: 27 us -> none  [the longest x3 10.3 us: shards(): ws = [w] + [lax.ppermute(w, Y, along_y(s)) for s in range(1, 4)]]
    ppermute x9 -> x0, waiting for transfers between devices: 17.2 us -> none  [the longest x3 17.1 us: shards(): lax.ppermute(blocks[s], 'x', shift(4, -s))]
    all_to_all x0 -> x1, blocking collectives: none -> 15.4 us  [shards(): swap = lambda a, axes: lax.all_to_all(a, axes, 0, 0, tiled=True)]
    ppermute x7 -> x4, starting transfers between devices: 25.7 us -> 12.2 us  [shards(): other = lambda a: lax.ppermute(a, 'c', shift(2, 1))]
    pallas_call x5 -> x7, Pallas kernels: 18.2 us -> 22 us  [call(): pl.pallas_call(body, out_shape=outs, in_specs=in_specs, out_specs=[pl.Blo...]
  transfers between devices with their start and end apart: 24 -> 16, of which waited for: 7 -> 9; matrix products, arithmetic and copies ran while one was open for 5% -> 5% of each run, Pallas kernels for 6% -> 3%
where the time goes in v2:
time: 199 us; the launch traced here: 198 us
  starting transfers between devices  81.7 us (41%)
  waiting for transfers between devices  61.8 us (31%)
  Pallas kernels  22 us (11%)
  blocking collectives  15.4 us (8%)
  local copies, waits for them, and re-layouts  11.5 us (6%)
  other arithmetic  4.38 us (2%)
    all_to_all x5, waiting for transfers between devices, shards(): swap = lambda a, axes: lax.all_to_all(a, axes, 0, 0, tiled=True)  47.6 us
    all_to_all x5, starting transfers between devices, shards(): swap = lambda a, axes: lax.all_to_all(a, axes, 0, 0, tiled=True)  46.2 us
    pallas_call x7, Pallas kernels, call(): pl.pallas_call(body, out_shape=outs, in_specs=in_specs, out_specs=[pl.Blo...  22 us
    all_to_all x1, blocking collectives, shards(): swap = lambda a, axes: lax.all_to_all(a, axes, 0, 0, tiled=True)  15.4 us
    ppermute x4, starting transfers between devices, shards(): lax.ppermute(b, Y, along_y(1 if s in (0, 3) else -1))  12.8 us
    ppermute x4, starting transfers between devices, shards(): other = lambda a: lax.ppermute(a, 'c', shift(2, 1))  12.2 us
    ppermute x4, waiting for transfers between devices, shards(): lax.ppermute(b, Y, along_y(1 if s in (0, 3) else -1))  10.6 us
    ppermute x3, starting transfers between devices, shards(): lax.ppermute(block, 'x', shift(4, s))  10.5 us
  transfers between devices with their start and end apart: 16, of which 9 were waited for; matrix products, arithmetic and copies ran while one was open for 5% of the time, Pallas kernels for 3%

profile of v2, /device:TPU:1, one launch (start us, length us, event | category | flops | bytes accessed | tf_op | source)
XLA Modules:
  0.0 197.6 jit_solution(9898729090095728982)
XLA Ops:
  0.6 0.8 copy-done
  1.5 0.8 broadcast_in_dim.8
  2.3 15.7 %all-to-all-start = ((bf16[16,6,16,128]{3,2,1,0:T(8,128)(2,1)}), bf16[16,6,16,128]{3,2,1,0:T(8,128)(2,1)S(1)}, u32[]{:S(2)}, u32[]{:S(2)}) async-start(bf16[16,6,16,128]{3,2,1,0:T(8,128)(2,1)} %broadcast_in_dim.8), calls=%async_computation | async-start | bytes 786432 | tf_op jit(solution)/shard_map/all_to_all | solution.py:139
  18.0 1.8 reshape.244
  19.9 1.3 copy.6
  21.2 14.9 %all-to-all-done = bf16[16,6,16,128]{3,2,1,0:T(8,128)(2,1)S(1)} async-done(((bf16[16,6,16,128]{3,2,1,0:T(8,128)(2,1)}), bf16[16,6,16,128]{3,2,1,0:T(8,128)(2,1)S(1)}, u32[]{:S(2)}, u32[]{:S(2)}) %all-to-all-start) | async-done | bytes 393248 | tf_op jit(solution)/shard_map/all_to_all | solution.py:139
  36.1 11.2 %all-to-all-start.1 = ((bf16[8,128,512]{2,1,0:T(8,128)(2,1)}), bf16[8,128,512]{2,1,0:T(8,128)(2,1)S(1)}, u32[]{:S(2)}, u32[]{:S(2)}) async-start(bf16[8,128,512]{2,1,0:T(8,128)(2,1)} %bitcast.3), calls=%async_computation.1 | async-start | bytes 2097152 | tf_op jit(solution)/shard_map/all_to_all | solution.py:139
  47.4 3.1 %collective-permute-start.1 = (bf16[96,2048]{1,0:T(8,128)(2,1)S(1)}, bf16[96,2048]{1,0:T(8,128)(2,1)S(1)}, u32[]{:S(2)}, u32[]{:S(2)}) collective-permute-start(bf16[96,2048]{1,0:T(8,128)(2,1)S(1)} %bitcast.21), channel_id=1, source_target_pairs={{0,64},{64,128},{128,192},{192,0},{1,65},{65,129},{129,193},{193,1... | collective-permute-start | bytes 1179656 | tf_op jit(solution)/shard_map/ppermute | solution.py:144
  50.5 4.4 %collective-permute-start.2 = (bf16[96,2048]{1,0:T(8,128)(2,1)S(1)}, bf16[96,2048]{1,0:T(8,128)(2,1)}, u32[]{:S(2)}, u32[]{:S(2)}) collective-permute-start(bf16[96,2048]{1,0:T(8,128)(2,1)S(1)} %bitcast.22), channel_id=1, source_target_pairs={{0,128},{64,192},{128,0},{192,64},{1,129},{65,193},{129,1},{193,65... | collective-permute-start | bytes 1179656 | tf_op jit(solution)/shard_map/ppermute | solution.py:144
  54.9 3.1 %collective-permute-start.3 = (bf16[96,2048]{1,0:T(8,128)(2,1)S(1)}, bf16[96,2048]{1,0:T(8,128)(2,1)}, u32[]{:S(2)}, u32[]{:S(2)}) collective-permute-start(bf16[96,2048]{1,0:T(8,128)(2,1)S(1)} %bitcast.23), channel_id=1, source_target_pairs={{0,192},{64,0},{128,64},{192,128},{1,193},{65,1},{129,65},{193,129... | collective-permute-start | bytes 1179656 | tf_op jit(solution)/shard_map/ppermute | solution.py:144
  57.9 0.9 constant_dynamic-slice_fusion
  58.8 2.7 %collective-permute-start = (bf16[128,2048]{1,0:T(8,128)(2,1)S(1)}, bf16[128,2048]{1,0:T(8,128)(2,1)S(1)}, u32[]{:S(2)}, u32[]{:S(2)}) collective-permute-start(bf16[128,2048]{1,0:T(8,128)(2,1)S(1)} %get-tuple-element.14), channel_id=1, source_target_pairs={{0,1},{1,0},{2,3},{3,2},{4,5},{5,4},{6,7},{7,6},{8,9},{9,8},{10,11... | collective-permute-start | bytes 1572872 | tf_op jit(solution)/shard_map/ppermute | solution.py:138
  61.6 3.7 %collective-permute-start.4 = (bf16[96,2048]{1,0:T(8,128)(2,1)S(1)}, bf16[96,2048]{1,0:T(8,128)(2,1)S(1)}, u32[]{:S(2)}, u32[]{:S(2)}) collective-permute-start(bf16[96,2048]{1,0:T(8,128)(2,1)S(1)} %bitcast.24), channel_id=1, source_target_pairs={{0,256},{256,2},{2,258},{258,0},{1,257},{257,3},{3,259},{259,1},{4... | collective-permute-start | bytes 1179656 | tf_op jit(solution)/shard_map/ppermute | solution.py:145
  65.3 3.1 %collective-permute-start.5 = (bf16[96,2048]{1,0:T(8,128)(2,1)S(1)}, bf16[96,2048]{1,0:T(8,128)(2,1)}, u32[]{:S(2)}, u32[]{:S(2)}) collective-permute-start(bf16[96,2048]{1,0:T(8,128)(2,1)S(1)} %collective-permute-done.1.refs_4_), channel_id=1, source_target_pairs={{0,258},{256,0},{2,256},{258,2},{1,259},{257,1},{3,257},{259,3},{4... | collective-permute-start | bytes 1179656 | tf_op jit(solution)/shard_map/ppermute | solution.py:145
  68.4 2.3 %collective-permute-done.2.refs_5_ = bf16[96,2048]{1,0:T(8,128)(2,1)} collective-permute-done((bf16[96,2048]{1,0:T(8,128)(2,1)S(1)}, bf16[96,2048]{1,0:T(8,128)(2,1)}, u32[]{:S(2)}, u32[]{:S(2)}) %collective-permute-start.2) | collective-permute-done | bytes 393248 | tf_op jit(solution)/shard_map/ppermute | solution.py:144
  70.7 4.1 %collective-permute-start.6 = (bf16[96,2048]{1,0:T(8,128)(2,1)}, bf16[96,2048]{1,0:T(8,128)(2,1)}, u32[]{:S(2)}, u32[]{:S(2)}) collective-permute-start(bf16[96,2048]{1,0:T(8,128)(2,1)} %collective-permute-done.2.refs_5_), channel_id=1, source_target_pairs={{0,258},{256,0},{2,256},{258,2},{1,259},{257,1},{3,257},{259,3},{4... | collective-permute-start | bytes 1179656 | tf_op jit(solution)/shard_map/ppermute | solution.py:145
  74.8 1.9 collective-permute-start.7
  76.8 0.8 collective-permute-done.5.refs_8_
  77.7 8.4 %collective-permute-done.6.refs_9_ = bf16[96,2048]{1,0:T(8,128)(2,1)} collective-permute-done((bf16[96,2048]{1,0:T(8,128)(2,1)}, bf16[96,2048]{1,0:T(8,128)(2,1)}, u32[]{:S(2)}, u32[]{:S(2)}) %collective-permute-start.6) | collective-permute-done | bytes 393248 | tf_op jit(solution)/shard_map/ppermute | solution.py:145
  86.1 1.3 collective-permute-done.7.refs_10_
  87.4 5.2 %shard_map.59 = (f32[128,768]{1,0:T(8,128)}, f32[128,768]{1,0:T(8,128)}, bf16[768,2048]{1,0:T(8,128)(2,1)}) custom-call(s32[1]{0:T(128)} %bitcast.1.refs_0_, bf16[128,2048]{1,0:T(8,128)(2,1)} %get-tuple-element.15.refs_1_, bf16[128,2048]{1,0:T(8,128)(2,1)} %copy-done.8, bf16[96,2048]{1,0:T(8,128)(2,1)} %bitcast.25, bf16[96,2048]{1,0:T(8,128)(2,1)} %copy-done.11, ...), custom_call_target="tpu_custom_call" | custom-call | flops 805306368 | bytes 9175044 | tf_op jit(solution)/shard_map/pallas_call | solution.py:39
  92.7 4.3 %collective-permute-start.8 = (f32[128,768]{1,0:T(8,128)}, f32[128,768]{1,0:T(8,128)S(1)}, u32[]{:S(2)}, u32[]{:S(2)}) collective-permute-start(f32[128,768]{1,0:T(8,128)} %get-tuple-element.8), channel_id=1, source_target_pairs={{0,1},{1,0},{2,3},{3,2},{4,5},{5,4},{6,7},{7,6},{8,9},{9,8},{10,11... | collective-permute-start | bytes 1179656 | tf_op jit(solution)/shard_map/ppermute | solution.py:138
  97.0 0.7 copy.7.pos
  97.7 0.7 copy.8.neg
  98.5 0.6 fusion.ids
  99.1 0.8 copy-done.10
  99.9 2.6 %shard_map.60 = bf16[4,128,768]{2,1,0:T(8,128)(2,1)} custom-call(f32[128,768]{1,0:T(8,128)} %get-tuple-element.7.so, f32[128,768]{1,0:T(8,128)} %copy-done.10, s32[1,768]{1,0:T(1,128)} %fusion.ids, s32[128,1]{1,0:T(8,128)} %copy.7.pos, s32[128,7]{1,0:T(8,128)} %copy.8.neg), custom_call_target="tpu_custom_call" | custom-call | bytes 1580032 | tf_op jit(solution)/shard_map/pallas_call | solution.py:39
  102.5 15.4 %all_to_all.30.w_own.refs_1_ = bf16[4,128,768]{2,1,0:T(8,128)(2,1)S(1)} all-to-all(bf16[4,128,768]{2,1,0:T(8,128)(2,1)} %shard_map.60), channel_id=1, replica_groups=mesh['yl'=2,'x'=4,'z'=16,'yh'=2,'c'=2] {'yl','yh'}, dimensions={0} | all-to-all | bytes 1572864 | tf_op jit(solution)/shard_map/all_to_all | solution.py:139
  117.9 2.9 %collective-permute-start.9 = (bf16[4,128,768]{2,1,0:T(8,128)(2,1)S(1)}, bf16[4,128,768]{2,1,0:T(8,128)(2,1)S(1)}, u32[]{:S(2)}, u32[]{:S(2)}) collective-permute-start(bf16[4,128,768]{2,1,0:T(8,128)(2,1)S(1)} %all_to_all.30.w_own.refs_1_), channel_id=1, source_target_pairs={{0,1},{1,0},{2,3},{3,2},{4,5},{5,4},{6,7},{7,6},{8,9},{9,8},{10,11... | collective-permute-start | bytes 2359304 | tf_op jit(solution)/shard_map/ppermute | solution.py:138
  121.4 1.3 collective-permute-done.9.w_oth.refs_2_
  122.7 0.9 copy-done.5
  123.6 4.0 %shard_map.61.refs_4_ = f32[4,192,512]{2,1,0:T(8,128)} custom-call(s32[2]{0:T(128)} %pad_add_fusion.at_ref, bf16[4,128,768]{2,1,0:T(8,128)(2,1)} %copy-done.2, bf16[4,128,768]{2,1,0:T(8,128)(2,1)} %copy-done.5, bf16[1024,512]{1,0:T(8,128)(2,1)} %bitcast.19), custom_call_target="tpu_custom_call" | custom-call | flops 805306368 | bytes 4194312 | tf_op jit(solution)/shard_map/pallas_call | solution.py:39
  127.6 3.6 %all-to-all-start.3 = ((f32[4,192,512]{2,1,0:T(8,128)}), f32[4,192,512]{2,1,0:T(8,128)S(1)}, u32[]{:S(2)}, u32[]{:S(2)}) async-start(f32[4,192,512]{2,1,0:T(8,128)} %shard_map.61.refs_4_), calls=%async_computation.3 | async-start | bytes 3145728 | tf_op jit(solution)/shard_map/all_to_all | solution.py:139
  131.2 4.7 %shard_map.62 = (f32[128,2048]{1,0:T(8,128)}, f32[128,2048]{1,0:T(8,128)}) custom-call(s32[1]{0:T(128)} %bitcast.refs_0_, bf16[4,128,768]{2,1,0:T(8,128)(2,1)} %copy-done.2, bf16[4,128,768]{2,1,0:T(8,128)(2,1)} %copy-done.5, bf16[768,2048]{1,0:T(8,128)(2,1)} %get-tuple-element.9.refs_3_, f32[4,192,512]{2,1,0:T(8,128)} %shard_map.61.refs_4_), custom_call_target="tpu_custom_call" | custom-call | flops 805306368 | bytes 8388612 | tf_op jit(solution)/shard_map/pallas_call | solution.py:39
  135.8 2.3 %collective-permute-start.10 = (f32[128,2048]{1,0:T(8,128)}, f32[128,2048]{1,0:T(8,128)}, u32[]{:S(2)}, u32[]{:S(2)}) collective-permute-start(f32[128,2048]{1,0:T(8,128)} %get-tuple-element.11), channel_id=1, source_target_pairs={{0,1},{1,0},{2,3},{3,2},{4,5},{5,4},{6,7},{7,6},{8,9},{9,8},{10,11... | collective-permute-start | bytes 3145736 | tf_op jit(solution)/shard_map/ppermute | solution.py:138
  138.1 13.5 %all-to-all-done.3.parts = f32[4,192,512]{2,1,0:T(8,128)S(1)} async-done(((f32[4,192,512]{2,1,0:T(8,128)}), f32[4,192,512]{2,1,0:T(8,128)S(1)}, u32[]{:S(2)}, u32[]{:S(2)}) %all-to-all-start.3) | async-done | bytes 1572896 | tf_op jit(solution)/shard_map/all_to_all | solution.py:139
  151.6 1.1 copy-done.3
  152.7 2.2 %shard_map.63 = f32[16,48,128]{2,1,0:T(8,128)} custom-call(f32[4,192,512]{2,1,0:T(8,128)} %copy-done.3), custom_call_target="tpu_custom_call" | custom-call | bytes 1966080 | tf_op jit(solution)/shard_map/pallas_call | solution.py:39
  155.0 5.7 %all-to-all-start.4 = ((f32[16,48,128]{2,1,0:T(8,128)}), f32[16,48,128]{2,1,0:T(8,128)S(1)}, u32[]{:S(2)}, u32[]{:S(2)}) async-start(f32[16,48,128]{2,1,0:T(8,128)} %shard_map.63), calls=%async_computation.4 | async-start | bytes 786432 | tf_op jit(solution)/shard_map/all_to_all | solution.py:139
  160.7 1.7 broadcast_select_fusion.1
  162.4 15.8 %all-to-all-done.4.parts = f32[16,48,128]{2,1,0:T(8,128)S(1)} async-done(((f32[16,48,128]{2,1,0:T(8,128)}), f32[16,48,128]{2,1,0:T(8,128)S(1)}, u32[]{:S(2)}, u32[]{:S(2)}) %all-to-all-start.4) | async-done | bytes 393248 | tf_op jit(solution)/shard_map/all_to_all | solution.py:139
  178.2 0.7 copy-done.6
  178.9 1.7 shard_map.64
  180.6 10.0 %all-to-all-start.5 = ((f32[8,24,128]{2,1,0:T(8,128)}), f32[8,24,128]{2,1,0:T(8,128)S(1)}, u32[]{:S(2)}, u32[]{:S(2)}) async-start(f32[8,24,128]{2,1,0:T(8,128)} %shard_map.64), calls=%async_computation.5 | async-start | bytes 196608 | tf_op jit(solution)/shard_map/all_to_all | solution.py:139
  190.6 1.5 pad_maximum_fusion
  192.0 3.4 %all-to-all-done.5.parts = f32[8,24,128]{2,1,0:T(8,128)S(1)} async-done(((f32[8,24,128]{2,1,0:T(8,128)}), f32[8,24,128]{2,1,0:T(8,128)S(1)}, u32[]{:S(2)}, u32[]{:S(2)}) %all-to-all-start.5) | async-done | bytes 98336 | tf_op jit(solution)/shard_map/all_to_all | solution.py:139
  195.4 0.6 copy-done.9
  196.1 1.6 shard_map.65
  (35 shorter events, 0.8 us)
Async XLA Ops:
  0.6 0.8 copy-start
  2.3 33.8 %all-to-all-start = ((bf16[16,6,16,128]{3,2,1,0:T(8,128)(2,1)}), bf16[16,6,16,128]{3,2,1,0:T(8,128)(2,1)S(1)}, u32[]{:S(2)}, u32[]{:S(2)}) async-start(bf16[16,6,16,128]{3,2,1,0:T(8,128)(2,1)} %broadcast_in_dim.8), calls=%async_computation | async-start | bytes 786432 | tf_op jit(solution)/shard_map/all_to_all | solution.py:139
  19.9 38.0 %copy-start.4 = (bf16[128,4096]{1,0:T(8,128)(2,1)S(1)}, bf16[128,4096]{1,0:T(8,128)(2,1)}, u32[]{:S(2)}) copy-start(bf16[128,4096]{1,0:T(8,128)(2,1)} %param.4) | copy-start | bytes 3145732
  36.1 40.7 %all-to-all-start.1 = ((bf16[8,128,512]{2,1,0:T(8,128)(2,1)}), bf16[8,128,512]{2,1,0:T(8,128)(2,1)S(1)}, u32[]{:S(2)}, u32[]{:S(2)}) async-start(bf16[8,128,512]{2,1,0:T(8,128)(2,1)} %bitcast.3), calls=%async_computation.1 | async-start | bytes 2097152 | tf_op jit(solution)/shard_map/all_to_all | solution.py:139
  47.3 40.0 %copy-start.7 = (bf16[12,8,16,128]{3,1,2,0:T(8,128)(2,1)}, bf16[12,8,16,128]{3,1,2,0:T(8,128)(2,1)S(1)}, u32[]{:S(2)}) copy-start(bf16[12,8,16,128]{3,1,2,0:T(8,128)(2,1)S(1)} %copy.13) | copy-start | bytes 1179652
  47.4 17.9 %collective-permute-start.1 = (bf16[96,2048]{1,0:T(8,128)(2,1)S(1)}, bf16[96,2048]{1,0:T(8,128)(2,1)S(1)}, u32[]{:S(2)}, u32[]{:S(2)}) collective-permute-start(bf16[96,2048]{1,0:T(8,128)(2,1)S(1)} %bitcast.21), channel_id=1, source_target_pairs={{0,64},{64,128},{128,192},{192,0},{1,65},{65,129},{129,193},{193,1... | collective-permute-start | bytes 1179656 | tf_op jit(solution)/shard_map/ppermute | solution.py:144
  50.5 20.2 %collective-permute-start.2 = (bf16[96,2048]{1,0:T(8,128)(2,1)S(1)}, bf16[96,2048]{1,0:T(8,128)(2,1)}, u32[]{:S(2)}, u32[]{:S(2)}) collective-permute-start(bf16[96,2048]{1,0:T(8,128)(2,1)S(1)} %bitcast.22), channel_id=1, source_target_pairs={{0,128},{64,192},{128,0},{192,64},{1,129},{65,193},{129,1},{193,65... | collective-permute-start | bytes 1179656 | tf_op jit(solution)/shard_map/ppermute | solution.py:144
  54.9 20.0 %collective-permute-start.3 = (bf16[96,2048]{1,0:T(8,128)(2,1)S(1)}, bf16[96,2048]{1,0:T(8,128)(2,1)}, u32[]{:S(2)}, u32[]{:S(2)}) collective-permute-start(bf16[96,2048]{1,0:T(8,128)(2,1)S(1)} %bitcast.23), channel_id=1, source_target_pairs={{0,192},{64,0},{128,64},{192,128},{1,193},{65,1},{129,65},{193,129... | collective-permute-start | bytes 1179656 | tf_op jit(solution)/shard_map/ppermute | solution.py:144
  58.8 17.9 %collective-permute-start = (bf16[128,2048]{1,0:T(8,128)(2,1)S(1)}, bf16[128,2048]{1,0:T(8,128)(2,1)S(1)}, u32[]{:S(2)}, u32[]{:S(2)}) collective-permute-start(bf16[128,2048]{1,0:T(8,128)(2,1)S(1)} %get-tuple-element.14), channel_id=1, source_target_pairs={{0,1},{1,0},{2,3},{3,2},{4,5},{5,4},{6,7},{7,6},{8,9},{9,8},{10,11... | collective-permute-start | bytes 1572872 | tf_op jit(solution)/shard_map/ppermute | solution.py:138
  61.6 15.2 %collective-permute-start.4 = (bf16[96,2048]{1,0:T(8,128)(2,1)S(1)}, bf16[96,2048]{1,0:T(8,128)(2,1)S(1)}, u32[]{:S(2)}, u32[]{:S(2)}) collective-permute-start(bf16[96,2048]{1,0:T(8,128)(2,1)S(1)} %bitcast.24), channel_id=1, source_target_pairs={{0,256},{256,2},{2,258},{258,0},{1,257},{257,3},{3,259},{259,1},{4... | collective-permute-start | bytes 1179656 | tf_op jit(solution)/shard_map/ppermute | solution.py:145
  65.3 22.1 %copy-start.11 = (bf16[96,2048]{1,0:T(8,128)(2,1)}, bf16[96,2048]{1,0:T(8,128)(2,1)S(1)}, u32[]{:S(2)}) copy-start(bf16[96,2048]{1,0:T(8,128)(2,1)S(1)} %collective-permute-done.1.refs_4_) | copy-start | bytes 1179652
  65.3 12.4 %collective-permute-start.5 = (bf16[96,2048]{1,0:T(8,128)(2,1)S(1)}, bf16[96,2048]{1,0:T(8,128)(2,1)}, u32[]{:S(2)}, u32[]{:S(2)}) collective-permute-start(bf16[96,2048]{1,0:T(8,128)(2,1)S(1)} %collective-permute-done.1.refs_4_), channel_id=1, source_target_pairs={{0,258},{256,0},{2,256},{258,2},{1,259},{257,1},{3,257},{259,3},{4... | collective-permute-start | bytes 1179656 | tf_op jit(solution)/shard_map/ppermute | solution.py:145
  70.7 15.4 %collective-permute-start.6 = (bf16[96,2048]{1,0:T(8,128)(2,1)}, bf16[96,2048]{1,0:T(8,128)(2,1)}, u32[]{:S(2)}, u32[]{:S(2)}) collective-permute-start(bf16[96,2048]{1,0:T(8,128)(2,1)} %collective-permute-done.2.refs_5_), channel_id=1, source_target_pairs={{0,258},{256,0},{2,256},{258,2},{1,259},{257,1},{3,257},{259,3},{4... | collective-permute-start | bytes 1179656 | tf_op jit(solution)/shard_map/ppermute | solution.py:145
  74.8 12.6 %collective-permute-start.7 = (bf16[96,2048]{1,0:T(8,128)(2,1)}, bf16[96,2048]{1,0:T(8,128)(2,1)}, u32[]{:S(2)}, u32[]{:S(2)}) collective-permute-start(bf16[96,2048]{1,0:T(8,128)(2,1)} %collective-permute-done.3.refs_6_), channel_id=1, source_target_pairs={{0,256},{256,2},{2,258},{258,0},{1,257},{257,3},{3,259},{259,1},{4... | collective-permute-start | bytes 1179656 | tf_op jit(solution)/shard_map/ppermute | solution.py:145
  76.8 10.6 %copy-start.8 = (bf16[128,2048]{1,0:T(8,128)(2,1)}, bf16[128,2048]{1,0:T(8,128)(2,1)S(1)}, u32[]{:S(2)}) copy-start(bf16[128,2048]{1,0:T(8,128)(2,1)S(1)} %collective-permute-done.refs_2_) | copy-start | bytes 1572868
  76.8 10.6 %copy-start.1 = (bf16[8,128,512]{2,1,0:T(8,128)(2,1)}, bf16[8,128,512]{2,1,0:T(8,128)(2,1)S(1)}, u32[]{:S(2)}) copy-start(bf16[8,128,512]{2,1,0:T(8,128)(2,1)S(1)} %all-to-all-done.1.refs_11_) | copy-start | bytes 3145732
  76.8 10.6 %copy-start.12 = (bf16[96,2048]{1,0:T(8,128)(2,1)}, bf16[96,2048]{1,0:T(8,128)(2,1)S(1)}, u32[]{:S(2)}) copy-start(bf16[96,2048]{1,0:T(8,128)(2,1)S(1)} %collective-permute-done.4.refs_7_) | copy-start | bytes 1179652
  87.4 9.5 %copy-start.14 = (s32[128]{0:T(128)S(1)}, s32[128]{0:T(128)}, u32[]{:S(2)}) copy-start(s32[128]{0:T(128)} %param.6) | copy-start | bytes 1540
  87.4 10.3 %copy-start.13 = (s32[128,7]{0,1:T(8,128)S(1)}, s32[128,7]{0,1:T(8,128)}, u32[]{:S(2)}) copy-start(s32[128,7]{0,1:T(8,128)} %param.7) | copy-start | bytes 10756
  92.7 6.4 %collective-permute-start.8 = (f32[128,768]{1,0:T(8,128)}, f32[128,768]{1,0:T(8,128)S(1)}, u32[]{:S(2)}, u32[]{:S(2)}) collective-permute-start(f32[128,768]{1,0:T(8,128)} %get-tuple-element.8), channel_id=1, source_target_pairs={{0,1},{1,0},{2,3},{3,2},{4,5},{5,4},{6,7},{7,6},{8,9},{9,8},{10,11... | collective-permute-start | bytes 1179656 | tf_op jit(solution)/shard_map/ppermute | solution.py:138
  99.1 0.8 copy-start.10
  117.9 4.8 %copy-start.2 = (bf16[4,128,768]{2,1,0:T(8,128)(2,1)}, bf16[4,128,768]{2,1,0:T(8,128)(2,1)S(1)}, u32[]{:S(2)}) copy-start(bf16[4,128,768]{2,1,0:T(8,128)(2,1)S(1)} %all_to_all.30.w_own.refs_1_) | copy-start | bytes 2359300
  117.9 4.8 %collective-permute-start.9 = (bf16[4,128,768]{2,1,0:T(8,128)(2,1)S(1)}, bf16[4,128,768]{2,1,0:T(8,128)(2,1)S(1)}, u32[]{:S(2)}, u32[]{:S(2)}) collective-permute-start(bf16[4,128,768]{2,1,0:T(8,128)(2,1)S(1)} %all_to_all.30.w_own.refs_1_), channel_id=1, source_target_pairs={{0,1},{1,0},{2,3},{3,2},{4,5},{5,4},{6,7},{7,6},{8,9},{9,8},{10,11... | collective-permute-start | bytes 2359304 | tf_op jit(solution)/shard_map/ppermute | solution.py:138
  122.7 0.9 copy-start.5
  127.6 24.0 %all-to-all-start.3 = ((f32[4,192,512]{2,1,0:T(8,128)}), f32[4,192,512]{2,1,0:T(8,128)S(1)}, u32[]{:S(2)}, u32[]{:S(2)}) async-start(f32[4,192,512]{2,1,0:T(8,128)} %shard_map.61.refs_4_), calls=%async_computation.3 | async-start | bytes 3145728 | tf_op jit(solution)/shard_map/all_to_all | solution.py:139
  135.8 24.9 %collective-permute-start.10 = (f32[128,2048]{1,0:T(8,128)}, f32[128,2048]{1,0:T(8,128)}, u32[]{:S(2)}, u32[]{:S(2)}) collective-permute-start(f32[128,2048]{1,0:T(8,128)} %get-tuple-element.11), channel_id=1, source_target_pairs={{0,1},{1,0},{2,3},{3,2},{4,5},{5,4},{6,7},{7,6},{8,9},{9,8},{10,11... | collective-permute-start | bytes 3145736 | tf_op jit(solution)/shard_map/ppermute | solution.py:138
  151.6 1.1 copy-start.3
  155.0 23.2 %all-to-all-start.4 = ((f32[16,48,128]{2,1,0:T(8,128)}), f32[16,48,128]{2,1,0:T(8,128)S(1)}, u32[]{:S(2)}, u32[]{:S(2)}) async-start(f32[16,48,128]{2,1,0:T(8,128)} %shard_map.63), calls=%async_computation.4 | async-start | bytes 786432 | tf_op jit(solution)/shard_map/all_to_all | solution.py:139
  178.2 0.7 copy-start.6
  180.6 14.8 %all-to-all-start.5 = ((f32[8,24,128]{2,1,0:T(8,128)}), f32[8,24,128]{2,1,0:T(8,128)S(1)}, u32[]{:S(2)}, u32[]{:S(2)}) async-start(f32[8,24,128]{2,1,0:T(8,128)} %shard_map.64), calls=%async_computation.5 | async-start | bytes 196608 | tf_op jit(solution)/shard_map/all_to_all | solution.py:139
  195.4 0.6 copy-start.9

commit v3 on v2

v3 whole, which is shorter than its diff:
```python
import jax
import jax.numpy as jnp
from jax import lax
from jax.experimental import pallas as pl
from jax.experimental.pallas import tpu as pltpu
from jax.sharding import Mesh
from jax.sharding import PartitionSpec as P

D = 4096
HALF = 2048
SLICE = 512
QDEV = 128
NP = 768
ROWS = 96
SIDE = 384
Y = ("yl", "yh")
MIB = 1024 * 1024
F32, BF16 = jnp.float32, jnp.bfloat16


def shift(count, by):
    return [(i, (i + by) % count) for i in range(count)]


def along_y(by):
    place = lambda y: 2 * (y % 2) + y // 2
    return [(place(y), place((y + by) % 4)) for y in range(4)]


def call(kernel, outs, *args, smem=0, after=0, limit=16, scratch=(), flops=0):
    count = len(args)
    in_specs = [pl.BlockSpec(memory_space=pltpu.SMEM)] * smem
    in_specs += [pl.BlockSpec(memory_space=pltpu.VMEM)] * (count - smem - after)
    in_specs += [pl.BlockSpec(memory_space=pl.ANY)] * after
    body = kernel
    if after:
        body = lambda *refs: kernel(*refs[: count - after], *refs[count:])
    size = sum(a.size * a.dtype.itemsize for a in args) + sum(o.size * o.dtype.itemsize for o in outs)
    return pl.pallas_call(
        body,
        out_shape=outs,
        in_specs=in_specs,
        out_specs=[pl.BlockSpec(memory_space=pltpu.VMEM)] * len(outs),
        scratch_shapes=list(scratch),
        compiler_params=pltpu.CompilerParams(vmem_limit_bytes=limit * MIB),
        cost_estimate=pl.CostEstimate(flops=flops, bytes_accessed=size, transcendentals=0),
    )(*args)


def prep_kernel(at_ref, queries, q_oth, q2, *parts):
    core, y = at_ref[0], at_ref[1]
    q2[:QDEV] = queries[:, pl.ds(pl.multiple_of(core * HALF, 128), HALF)]
    q2[QDEV:] = q_oth[...]
    for s, part in enumerate(parts):
        part[...] = q2[:, pl.ds(pl.multiple_of((y + s) % 4 * SLICE, 128), SLICE)]


def hold_kernel(block, out):
    out[...] = block[...]


def mask_kernel(ids, pos, neg, count, target):
    column = ids[...]
    total = jnp.ones(count.shape, F32)
    for k in range(7):
        total += jnp.where(neg[:, k : k + 1] == column, 1.0, 0.0)
    count[...] = total
    target[...] = jnp.where(pos[...] == column, 1.0, 0.0)


def near_kernel(q2, *refs):
    pieces, (part, pool) = refs[:4], refs[4:]
    for s in range(4):
        pool[ROWS * s : ROWS * s + ROWS, :] = pieces[s][...]
    part[...] = lax.dot_general(q2[...], pool[...], (((1,), (1,)), ((), ())), preferred_element_type=F32)


def far_kernel(side_ref, q2, near, *refs):
    pieces, (so, sx, pool) = refs[:4], refs[4:]
    for s in range(4):
        pool[ROWS * s : ROWS * s + ROWS, :] = pieces[s][...]
    far = lax.dot_general(q2[...], pool[...], (((1,), (1,)), ((), ())), preferred_element_type=F32)
    for side, part in ((side_ref[0], near[...]), (1 - side_ref[0], far)):
        cols = pl.ds(pl.multiple_of(side * SIDE, 128), SIDE)
        so[:, cols] = part[:QDEV]
        sx[:, cols] = part[QDEV:]


def loss_kernel(so, sr, count, target, w):
    scores = (so[...] + sr[...]) * 0.0625
    top = jnp.max(scores, axis=1, keepdims=True)
    mass = jnp.exp(scores - top) * count[...]
    total = jnp.sum(mass, axis=1, keepdims=True)
    rounded = (mass / total - target[...]).astype(BF16)
    for i in range(4):
        w[i] = rounded


def query_kernel(at_ref, wo, wx, near, far, go, gx, w2):
    here, side = at_ref[0], at_ref[1]
    w2[:QDEV] = wo[here]
    w2[QDEV:] = wx[here]
    w_near = w2[:, pl.ds(pl.multiple_of(side * SIDE, 128), SIDE)]
    w_far = w2[:, pl.ds(pl.multiple_of((1 - side) * SIDE, 128), SIDE)]
    for n in range(HALF // 512):
        cols = slice(512 * n, 512 * n + 512)
        part = jnp.dot(w_near, near[:, cols], preferred_element_type=F32)
        part = (part + jnp.dot(w_far, far[:, cols], preferred_element_type=F32)) * 0.0625
        go[:, cols] = part[:QDEV]
        gx[:, cols] = part[QDEV:]


def join_kernel(core_ref, go, gx, out):
    core = core_ref[0]
    out[:, pl.ds(pl.multiple_of(core * HALF, 128), HALF)] = go[...]
    out[:, pl.ds(pl.multiple_of((1 - core) * HALF, 128), HALF)] = gx[...]


def pool_kernel(at_ref, w_own, w_oth, q0, q1, q2, q3, out, w_all, q_all):
    x, y, core = at_ref[0], at_ref[1], at_ref[2]
    for s, q in enumerate((q0, q1, q2, q3)):
        src = (y + 4 - s) % 4
        at = 2 * (src % 2) + src // 2
        q_all[2 * QDEV * s : 2 * QDEV * s + 2 * QDEV, :] = q[...]
        w_all[2 * QDEV * s : 2 * QDEV * s + QDEV, :] = w_own[at]
        w_all[2 * QDEV * s + QDEV : 2 * QDEV * s + 2 * QDEV, :] = w_oth[at]
    for n in range(3):
        part = lax.dot_general(
            w_all[:, 256 * n : 256 * n + 256], q_all[...], (((0,), (0,)), ((), ())), preferred_element_type=F32
        ) * 0.0625
        for lo in range(256 * n, 256 * n + 256, 32):
            side, rest = divmod(lo, SIDE)
            s, row = divmod(rest, ROWS)
            at = (x + 4 - s) % 4
            out[at, ROWS * side + row : ROWS * side + row + 32, :] = part[lo - 256 * n : lo - 256 * n + 32]


def x_sum_kernel(parts, out):
    total = (parts[0] + parts[1]) + (parts[2] + parts[3])
    for z in range(16):
        for side in range(2):
            rows = total[ROWS * side + 6 * z : ROWS * side + 6 * z + 6]
            for j in range(4):
                at = (4 * side + j) * 6
                out[z, at : at + 6, :] = rows[:, 128 * j : 128 * j + 128]


def z_sum_kernel(parts, out):
    total = parts[0]
    for z in range(1, 16):
        total = total + parts[z]
    for i in range(8):
        side = i // 4
        out[i] = total[24 * side : 24 * side + 24]


def last_kernel(parts, out):
    for i in range(8):
        yl, yh, core = i // 4, (i // 2) % 2, i % 2
        for j in range(4):
            at = core * HALF + (2 * yh + yl) * SLICE + 128 * j
            out[:, at : at + 128] = parts[i, 6 * j : 6 * j + 6, :]


def shards(queries, passages, positives, negatives):
    core = lax.axis_index("c")
    x = lax.axis_index("x")
    yl = lax.axis_index("yl")
    other = lambda a: lax.ppermute(a, "c", shift(2, 1))
    swap = lambda a, axes: lax.all_to_all(a, axes, 0, 0, tiled=True)
    sd = jax.ShapeDtypeStruct

    y = 2 * lax.axis_index("yh") + yl
    mine = lax.dynamic_slice(passages, (0, core * HALF), (6, HALF)).reshape(6, 16, 128)
    block = swap(jnp.broadcast_to(mine[None], (16, 6, 16, 128)), "z").reshape(ROWS, HALF)

    q_oth = other(lax.dynamic_slice(queries, (0, (1 - core) * HALF), (QDEV, HALF)))
    q2, *parts = call(
        prep_kernel, [sd((2 * QDEV, HALF), BF16)] + [sd((2 * QDEV, SLICE), BF16)] * 4,
        jnp.stack([core, y]), queries, q_oth, smem=1,
    )
    group = [parts[0]] + [lax.ppermute(parts[s], Y, along_y(s)) for s in range(1, 4)]
    col = jnp.arange(NP, dtype=jnp.int32)
    side, s, z, r = col // SIDE, (col // ROWS) % 4, (col // 6) % 16, col % 6
    ids = ((side * 4 + (x - s) % 4) * 16 + z) * 6 + r
    count, target = call(
        mask_kernel, [sd((QDEV, NP), F32)] * 2, ids.reshape(1, NP), positives.reshape(QDEV, 1), negatives
    )

    block = call(hold_kernel, [sd((ROWS, HALF), BF16)], block, q2, *group, count, target, after=7)[0]
    near = [block, lax.ppermute(block, "x", shift(4, 1)), None, lax.ppermute(block, "x", shift(4, 3))]
    near[2] = lax.ppermute(near[1], "x", shift(4, 1))
    far = [lax.ppermute(b, Y, along_y(by)) for b, by in zip(near, (1, -1, -1, 1))]

    s_near, pool_near = call(
        near_kernel, [sd((2 * QDEV, SIDE), F32), sd((SIDE, HALF), BF16)], q2, *near, flops=256 * NP * HALF
    )
    s_own, s_out, pool_far = call(
        far_kernel,
        [sd((QDEV, NP), F32), sd((QDEV, NP), F32), sd((SIDE, HALF), BF16)],
        yl.reshape(1), q2, s_near, *far, smem=1, flops=256 * NP * HALF,
    )
    s_oth = other(s_out)

    w4 = call(loss_kernel, [sd((4, QDEV, NP), BF16)], s_own, s_oth, count, target)[0]
    w_own = swap(w4, Y)
    w_oth = other(w_own)
    blocks = call(
        pool_kernel, [sd((4, 2 * ROWS, SLICE), F32)],
        jnp.stack([x, y, core]), w_own, w_oth, *group, smem=1,
        scratch=[pltpu.VMEM((1024, NP), BF16), pltpu.VMEM((1024, SLICE), BF16)], flops=2 * 1024 * NP * SLICE,
    )[0]
    sums = call(x_sum_kernel, [sd((16, 48, 128), F32)], swap(blocks, "x"))[0]
    by_z = swap(sums, "z")

    here = 2 * yl + lax.axis_index("yh")
    g_own, g_out = call(
        query_kernel, [sd((QDEV, HALF), F32)] * 2,
        jnp.stack([here, yl]), w_own, w_oth, pool_near, pool_far, sums,
        smem=1, after=1, scratch=[pltpu.VMEM((2 * QDEV, NP), BF16)], flops=2 * 256 * NP * HALF,
    )
    query_grad = call(join_kernel, [sd((QDEV, D), F32)], core.reshape(1), g_own, other(g_out), smem=1)[0]

    by_y = swap(call(z_sum_kernel, [sd((8, 24, 128), F32)], by_z, query_grad, after=1)[0], Y + ("c",))
    passage_grad = call(last_kernel, [sd((6, D), F32)], by_y)[0]
    return query_grad, passage_grad


def solution(mesh):
    fine = Mesh(mesh.devices.reshape(2, 4, 16, 2, 2), ("yl", "x", "z", "yh", "c"))
    every, pooled = ("yl", "x", "z", "yh", "c"), ("yl", "x", "z")
    return jax.shard_map(
        shards,
        mesh=fine,
        in_specs=(P(every, None), P(pooled, None), P(every), P(every, None)),
        out_specs=(P(every, None), P(pooled, None)),
        check_vma=False,
    )
```

time: 199 us -> 181 us (0.910)
  blocking collectives: 15.4 us -> 52.6 us
  waiting for transfers between devices: 61.8 us -> 31.4 us
  Pallas kernels: 22 us -> 9.98 us
  starting transfers between devices: 81.7 us -> 76.5 us
  other arithmetic: 4.38 us -> 0.28 us
  local copies, waits for them, and re-layouts: 11.5 us -> 8.56 us
    all_to_all x5 -> x2, waiting for transfers between devices: 47.6 us -> 4.85 us  [shards(): swap = lambda a, axes: lax.all_to_all(a, axes, 0, 0, tiled=True)]
    all_to_all x1 -> x3, blocking collectives: 15.4 us -> 52.6 us  [shards(): swap = lambda a, axes: lax.all_to_all(a, axes, 0, 0, tiled=True)]
    all_to_all x5 -> x2, starting transfers between devices: 46.2 us -> 27.6 us  [shards(): swap = lambda a, axes: lax.all_to_all(a, axes, 0, 0, tiled=True)]
    pallas_call x7 -> x12, Pallas kernels: 22 us -> 9.98 us  [call(): pl.pallas_call(body, out_shape=outs, in_specs=in_specs, out_specs=[pl.Blo...]
    ppermute x7 -> x10, starting transfers between devices: 23.3 us -> 35 us  [the longest x4 15.9 us: shards(): lax.ppermute(b, Y, along_y(by))]
    ppermute x7 -> x10, waiting for transfers between devices: 12.9 us -> 19.7 us  [the longest x4 8.44 us: shards(): lax.ppermute(b, Y, along_y(by))]
    ppermute x4, waiting for transfers between devices: 1.31 us -> 6.83 us  [shards(): other = lambda a: lax.ppermute(a, 'c', shift(2, 1))]
    reshape x2 -> x0, local copies, waits for them, and re-layouts: 3.12 us -> none  [shards(): slices = queries.reshape(QDEV, 2, 2, 2, SLICE).transpose(3, 2, 1, 0, 4)]
  transfers between devices with their start and end apart: 16 -> 16, of which waited for: 9 -> 11; matrix products, arithmetic and copies ran while one was open for 5% -> 1% of each run, Pallas kernels for 3% -> 3%
where the time goes in v3:
time: 181 us; the launch traced here: 180 us
  starting transfers between devices  76.5 us (42%)
  blocking collectives  52.6 us (29%)
  waiting for transfers between devices  31.4 us (17%)
  Pallas kernels  9.98 us (6%)
  local copies, waits for them, and re-layouts  8.56 us (5%)
    all_to_all x3, blocking collectives, shards(): swap = lambda a, axes: lax.all_to_all(a, axes, 0, 0, tiled=True)  52.6 us
    all_to_all x2, starting transfers between devices, shards(): swap = lambda a, axes: lax.all_to_all(a, axes, 0, 0, tiled=True)  27.6 us
    ppermute x4, starting transfers between devices, shards(): lax.ppermute(b, Y, along_y(by))  15.9 us
    ppermute x4, starting transfers between devices, shards(): other = lambda a: lax.ppermute(a, 'c', shift(2, 1))  13.9 us
    ppermute x3, starting transfers between devices, shards(): lax.ppermute(parts[s], Y, along_y(s))  10.7 us
    pallas_call x12, Pallas kernels, call(): pl.pallas_call(body, out_shape=outs, in_specs=in_specs, out_specs=[pl.Blo...  9.98 us
    ppermute x4, waiting for transfers between devices, shards(): lax.ppermute(b, Y, along_y(by))  8.44 us
    unnamed x22, local copies, waits for them, and re-layouts  7.61 us
  transfers between devices with their start and end apart: 16, of which 11 were waited for; matrix products, arithmetic and copies ran while one was open for 1% of the time, Pallas kernels for 3%

profile of v3, /device:TPU:1, one launch (start us, length us, event | category | flops | bytes accessed | tf_op | source)
XLA Modules:
  0.0 180.3 jit_solution(1752376979782255973)
XLA Ops:
  0.7 0.8 copy-done
  1.5 0.8 broadcast_in_dim.8
  2.3 15.9 %all-to-all-start = ((bf16[16,6,16,128]{3,2,1,0:T(8,128)(2,1)}), bf16[16,6,16,128]{3,2,1,0:T(8,128)(2,1)}, u32[]{:S(2)}, u32[]{:S(2)}) async-start(bf16[16,6,16,128]{3,2,1,0:T(8,128)(2,1)} %broadcast_in_dim.8), calls=%async_computation | async-start | bytes 786432 | tf_op jit(solution)/shard_map/all_to_all | solution.py:170
  18.3 2.9 %collective-permute-start = (bf16[128,2048]{1,0:T(8,128)(2,1)S(1)}, bf16[128,2048]{1,0:T(8,128)(2,1)S(1)}, u32[]{:S(2)}, u32[]{:S(2)}) collective-permute-start(bf16[128,2048]{1,0:T(8,128)(2,1)S(1)} %constant_dynamic-slice_fusion), channel_id=1, source_target_pairs={{0,1},{1,0},{2,3},{3,2},{4,5},{5,4},{6,7},{7,6},{8,9},{9,8},{10,11... | collective-permute-start | bytes 1572872 | tf_op jit(solution)/shard_map/ppermute | solution.py:169
  21.2 1.4 collective-permute-done.q_oth
  22.7 1.5 shard_map.59
  24.2 3.2 %collective-permute-start.1 = (bf16[256,512]{1,0:T(8,128)(2,1)}, bf16[256,512]{1,0:T(8,128)(2,1)S(1)}, u32[]{:S(2)}, u32[]{:S(2)}) collective-permute-start(bf16[256,512]{1,0:T(8,128)(2,1)} %get-tuple-element.18), channel_id=1, source_target_pairs={{0,256},{256,2},{2,258},{258,0},{1,257},{257,3},{3,259},{259,1},{4... | collective-permute-start | bytes 786440 | tf_op jit(solution)/shard_map/ppermute | solution.py:182
  27.4 4.5 %collective-permute-start.2 = (bf16[256,512]{1,0:T(8,128)(2,1)}, bf16[256,512]{1,0:T(8,128)(2,1)S(1)}, u32[]{:S(2)}, u32[]{:S(2)}) collective-permute-start(bf16[256,512]{1,0:T(8,128)(2,1)} %get-tuple-element.19), channel_id=1, source_target_pairs={{0,2},{256,258},{2,0},{258,256},{1,3},{257,259},{3,1},{259,257},{4... | collective-permute-start | bytes 786440 | tf_op jit(solution)/shard_map/ppermute | solution.py:182
  31.9 3.0 %collective-permute-start.3 = (bf16[256,512]{1,0:T(8,128)(2,1)S(1)}, bf16[256,512]{1,0:T(8,128)(2,1)S(1)}, u32[]{:S(2)}, u32[]{:S(2)}) collective-permute-start(bf16[256,512]{1,0:T(8,128)(2,1)S(1)} %get-tuple-element.20), channel_id=1, source_target_pairs={{0,258},{256,0},{2,256},{258,2},{1,259},{257,1},{3,257},{259,3},{4... | collective-permute-start | bytes 786440 | tf_op jit(solution)/shard_map/ppermute | solution.py:182
  34.9 0.1 copy.6.pos
  35.2 0.4 shard_map.60
  35.6 0.7 all-to-all-done
  36.3 1.1 copy.12
  37.4 4.5 %collective-permute-done.2.refs_4_.q2 = bf16[256,512]{1,0:T(8,128)(2,1)S(1)} collective-permute-done((bf16[256,512]{1,0:T(8,128)(2,1)}, bf16[256,512]{1,0:T(8,128)(2,1)S(1)}, u32[]{:S(2)}, u32[]{:S(2)}) %collective-permute-start.2) | collective-permute-done | bytes 262176 | tf_op jit(solution)/shard_map/ppermute | solution.py:182
  41.9 1.0 collective-permute-done.3.refs_5_.q3
  42.9 3.1 %collective-permute-start.4 = (bf16[96,2048]{1,0:T(8,128)(2,1)S(1)}, bf16[96,2048]{1,0:T(8,128)(2,1)S(1)}, u32[]{:S(2)}, u32[]{:S(2)}) collective-permute-start(bf16[96,2048]{1,0:T(8,128)(2,1)S(1)} %shard_map.61.refs_0_), channel_id=1, source_target_pairs={{0,64},{64,128},{128,192},{192,0},{1,65},{65,129},{129,193},{193,1... | collective-permute-start | bytes 1179656 | tf_op jit(solution)/shard_map/ppermute | solution.py:191
  46.1 3.4 %collective-permute-start.6 = (bf16[96,2048]{1,0:T(8,128)(2,1)S(1)}, bf16[96,2048]{1,0:T(8,128)(2,1)S(1)}, u32[]{:S(2)}, u32[]{:S(2)}) collective-permute-start(bf16[96,2048]{1,0:T(8,128)(2,1)S(1)} %shard_map.61.refs_0_), channel_id=1, source_target_pairs={{0,192},{64,0},{128,64},{192,128},{1,193},{65,1},{129,65},{193,129... | collective-permute-start | bytes 1179656 | tf_op jit(solution)/shard_map/ppermute | solution.py:191
  49.5 5.8 %collective-permute-done.4.refs_1_ = bf16[96,2048]{1,0:T(8,128)(2,1)S(1)} collective-permute-done((bf16[96,2048]{1,0:T(8,128)(2,1)S(1)}, bf16[96,2048]{1,0:T(8,128)(2,1)S(1)}, u32[]{:S(2)}, u32[]{:S(2)}) %collective-permute-start.4) | collective-permute-done | bytes 393248 | tf_op jit(solution)/shard_map/ppermute | solution.py:191
  55.2 1.9 %collective-permute-start.5 = (bf16[96,2048]{1,0:T(8,128)(2,1)S(1)}, bf16[96,2048]{1,0:T(8,128)(2,1)S(1)}, u32[]{:S(2)}, u32[]{:S(2)}) collective-permute-start(bf16[96,2048]{1,0:T(8,128)(2,1)S(1)} %collective-permute-done.4.refs_1_), channel_id=1, source_target_pairs={{0,64},{64,128},{128,192},{192,0},{1,65},{65,129},{129,193},{193,1... | collective-permute-start | bytes 1179656 | tf_op jit(solution)/shard_map/ppermute | solution.py:192
  57.1 6.1 %collective-permute-start.7 = (bf16[96,2048]{1,0:T(8,128)(2,1)S(1)}, bf16[96,2048]{1,0:T(8,128)(2,1)S(1)}, u32[]{:S(2)}, u32[]{:S(2)}) collective-permute-start(bf16[96,2048]{1,0:T(8,128)(2,1)S(1)} %shard_map.61.refs_0_), channel_id=1, source_target_pairs={{0,256},{256,2},{2,258},{258,0},{1,257},{257,3},{3,259},{259,1},{4... | collective-permute-start | bytes 1179656 | tf_op jit(solution)/shard_map/ppermute | solution.py:193
  63.3 1.9 %collective-permute-start.8 = (bf16[96,2048]{1,0:T(8,128)(2,1)S(1)}, bf16[96,2048]{1,0:T(8,128)(2,1)S(1)}, u32[]{:S(2)}, u32[]{:S(2)}) collective-permute-start(bf16[96,2048]{1,0:T(8,128)(2,1)S(1)} %collective-permute-done.4.refs_1_), channel_id=1, source_target_pairs={{0,258},{256,0},{2,256},{258,2},{1,259},{257,1},{3,257},{259,3},{4... | collective-permute-start | bytes 1179656 | tf_op jit(solution)/shard_map/ppermute | solution.py:193
  65.2 3.4 %collective-permute-start.10 = (bf16[96,2048]{1,0:T(8,128)(2,1)S(1)}, bf16[96,2048]{1,0:T(8,128)(2,1)S(1)}, u32[]{:S(2)}, u32[]{:S(2)}) collective-permute-start(bf16[96,2048]{1,0:T(8,128)(2,1)S(1)} %collective-permute-done.6.refs_3_), channel_id=1, source_target_pairs={{0,256},{256,2},{2,258},{258,0},{1,257},{257,3},{3,259},{259,1},{4... | collective-permute-start | bytes 1179656 | tf_op jit(solution)/shard_map/ppermute | solution.py:193
  68.6 4.5 %collective-permute-start.9 = (bf16[96,2048]{1,0:T(8,128)(2,1)S(1)}, bf16[96,2048]{1,0:T(8,128)(2,1)S(1)}, u32[]{:S(2)}, u32[]{:S(2)}) collective-permute-start(bf16[96,2048]{1,0:T(8,128)(2,1)S(1)} %collective-permute-done.5.refs_2_), channel_id=1, source_target_pairs={{0,258},{256,0},{2,256},{258,2},{1,259},{257,1},{3,257},{259,3},{4... | collective-permute-start | bytes 1179656 | tf_op jit(solution)/shard_map/ppermute | solution.py:193
  73.1 0.7 shard_map.62
  73.8 1.1 copy-done.3
  75.0 4.5 %collective-permute-done.10.refs_3_ = bf16[96,2048]{1,0:T(8,128)(2,1)S(1)} collective-permute-done((bf16[96,2048]{1,0:T(8,128)(2,1)S(1)}, bf16[96,2048]{1,0:T(8,128)(2,1)S(1)}, u32[]{:S(2)}, u32[]{:S(2)}) %collective-permute-start.10) | collective-permute-done | bytes 393248 | tf_op jit(solution)/shard_map/ppermute | solution.py:193
  79.5 3.9 %collective-permute-done.9.refs_2_ = bf16[96,2048]{1,0:T(8,128)(2,1)S(1)} collective-permute-done((bf16[96,2048]{1,0:T(8,128)(2,1)S(1)}, bf16[96,2048]{1,0:T(8,128)(2,1)S(1)}, u32[]{:S(2)}, u32[]{:S(2)}) %collective-permute-start.9) | collective-permute-done | bytes 393248 | tf_op jit(solution)/shard_map/ppermute | solution.py:193
  83.4 0.7 shard_map.63
  84.2 3.6 %collective-permute-start.11 = (f32[128,768]{1,0:T(8,128)S(1)}, f32[128,768]{1,0:T(8,128)S(1)}, u32[]{:S(2)}, u32[]{:S(2)}) collective-permute-start(f32[128,768]{1,0:T(8,128)S(1)} %get-tuple-element.25), channel_id=1, source_target_pairs={{0,1},{1,0},{2,3},{3,2},{4,5},{5,4},{6,7},{7,6},{8,9},{9,8},{10,11... | collective-permute-start | bytes 1179656 | tf_op jit(solution)/shard_map/ppermute | solution.py:169
  87.8 1.3 collective-permute-done.11.sr
  89.1 0.3 shard_map.64
  89.4 13.8 %all_to_all.25.w_own.refs_1_ = bf16[4,128,768]{2,1,0:T(8,128)(2,1)S(1)} all-to-all(bf16[4,128,768]{2,1,0:T(8,128)(2,1)S(1)} %shard_map.64), channel_id=1, replica_groups=mesh['yl'=2,'x'=4,'z'=16,'yh'=2,'c'=2] {'yl','yh'}, dimensions={0} | all-to-all | bytes 1572864 | tf_op jit(solution)/shard_map/all_to_all | solution.py:170
  103.2 3.4 %collective-permute-start.12 = (bf16[4,128,768]{2,1,0:T(8,128)(2,1)S(1)}, bf16[4,128,768]{2,1,0:T(8,128)(2,1)S(1)}, u32[]{:S(2)}, u32[]{:S(2)}) collective-permute-start(bf16[4,128,768]{2,1,0:T(8,128)(2,1)S(1)} %all_to_all.25.w_own.refs_1_), channel_id=1, source_target_pairs={{0,1},{1,0},{2,3},{3,2},{4,5},{5,4},{6,7},{7,6},{8,9},{9,8},{10,11... | collective-permute-start | bytes 2359304 | tf_op jit(solution)/shard_map/ppermute | solution.py:169
  106.7 1.8 %collective-permute-done.12.w_oth.refs_2_ = bf16[4,128,768]{2,1,0:T(8,128)(2,1)S(1)} collective-permute-done((bf16[4,128,768]{2,1,0:T(8,128)(2,1)S(1)}, bf16[4,128,768]{2,1,0:T(8,128)(2,1)S(1)}, u32[]{:S(2)}, u32[]{:S(2)}) %collective-permute-start.12) | collective-permute-done | bytes 786464 | tf_op jit(solution)/shard_map/ppermute | solution.py:169
  108.5 1.6 shard_map.65
  110.1 23.6 %all_to_all.26.parts = f32[4,192,512]{2,1,0:T(8,128)S(1)} all-to-all(f32[4,192,512]{2,1,0:T(8,128)S(1)} %shard_map.65), channel_id=1, replica_groups=mesh['yl'=2,'x'=4,'z'=16,'yh'=2,'c'=2] {'x'}, dimensions={0} | all-to-all | bytes 3145728 | tf_op jit(solution)/shard_map/all_to_all | solution.py:170
  133.7 0.8 shard_map.66.refs_5_
  134.6 11.7 %all-to-all-start.3 = ((f32[16,48,128]{2,1,0:T(8,128)}), f32[16,48,128]{2,1,0:T(8,128)S(1)}, u32[]{:S(2)}, u32[]{:S(2)}) async-start(f32[16,48,128]{2,1,0:T(8,128)} %shard_map.66.refs_5_), calls=%async_computation.3 | async-start | bytes 786432 | tf_op jit(solution)/shard_map/all_to_all | solution.py:170
  146.3 1.4 copy-done.4
  147.7 1.4 copy-done.6
  149.2 1.8 shard_map.67
  151.0 4.0 %collective-permute-start.13 = (f32[128,2048]{1,0:T(8,128)S(1)}, f32[128,2048]{1,0:T(8,128)S(1)}, u32[]{:S(2)}, u32[]{:S(2)}) collective-permute-start(f32[128,2048]{1,0:T(8,128)S(1)} %get-tuple-element.29), channel_id=1, source_target_pairs={{0,1},{1,0},{2,3},{3,2},{4,5},{5,4},{6,7},{7,6},{8,9},{9,8},{10,11... | collective-permute-start | bytes 3145736 | tf_op jit(solution)/shard_map/ppermute | solution.py:169
  155.0 2.3 %collective-permute-done.13.gx = f32[128,2048]{1,0:T(8,128)S(1)} collective-permute-done((f32[128,2048]{1,0:T(8,128)S(1)}, f32[128,2048]{1,0:T(8,128)S(1)}, u32[]{:S(2)}, u32[]{:S(2)}) %collective-permute-start.13) | collective-permute-done | bytes 1048608 | tf_op jit(solution)/shard_map/ppermute | solution.py:169
  157.2 1.5 shard_map.68.refs_1_
  158.7 4.1 %all-to-all-done.3.refs_0_ = f32[16,48,128]{2,1,0:T(8,128)S(1)} async-done(((f32[16,48,128]{2,1,0:T(8,128)}), f32[16,48,128]{2,1,0:T(8,128)S(1)}, u32[]{:S(2)}, u32[]{:S(2)}) %all-to-all-start.3) | async-done | bytes 393248 | tf_op jit(solution)/shard_map/all_to_all | solution.py:170
  162.8 1.6 copy-done.1
  164.4 15.2 %all_to_all.27.parts = f32[8,24,128]{2,1,0:T(8,128)S(1)} all-to-all(f32[8,24,128]{2,1,0:T(8,128)S(1)} %shard_map.69), channel_id=1, replica_groups=mesh['yl'=2,'x'=4,'z'=16,'yh'=2,'c'=2] {'yl','yh','c'}, dimensions={0} | all-to-all | bytes 196608 | tf_op jit(solution)/shard_map/all_to_all | solution.py:170
  179.7 0.7 shard_map.70
  (28 shorter events, 0.6 us)
Async XLA Ops:
  0.6 0.8 copy-start
  0.6 17.6 %copy-start.2 = (bf16[128,4096]{1,0:T(8,128)(2,1)S(1)}, bf16[128,4096]{1,0:T(8,128)(2,1)}, u32[]{:S(2)}) copy-start(bf16[128,4096]{1,0:T(8,128)(2,1)} %queries.1) | copy-start | bytes 3145732
  2.3 32.6 %copy-start.8 = (s32[128]{0:T(128)S(1)}, s32[128]{0:T(128)}, u32[]{:S(2)}) copy-start(s32[128]{0:T(128)} %param.6) | copy-start | bytes 1540
  2.3 32.7 %copy-start.7 = (s32[128,7]{0,1:T(8,128)S(1)}, s32[128,7]{0,1:T(8,128)}, u32[]{:S(2)}) copy-start(s32[128,7]{0,1:T(8,128)} %param.7) | copy-start | bytes 10756
  2.3 34.0 %all-to-all-start = ((bf16[16,6,16,128]{3,2,1,0:T(8,128)(2,1)}), bf16[16,6,16,128]{3,2,1,0:T(8,128)(2,1)}, u32[]{:S(2)}, u32[]{:S(2)}) async-start(bf16[16,6,16,128]{3,2,1,0:T(8,128)(2,1)} %broadcast_in_dim.8), calls=%async_computation | async-start | bytes 786432 | tf_op jit(solution)/shard_map/all_to_all | solution.py:170
  18.3 4.4 %collective-permute-start = (bf16[128,2048]{1,0:T(8,128)(2,1)S(1)}, bf16[128,2048]{1,0:T(8,128)(2,1)S(1)}, u32[]{:S(2)}, u32[]{:S(2)}) collective-permute-start(bf16[128,2048]{1,0:T(8,128)(2,1)S(1)} %constant_dynamic-slice_fusion), channel_id=1, source_target_pairs={{0,1},{1,0},{2,3},{3,2},{4,5},{5,4},{6,7},{7,6},{8,9},{9,8},{10,11... | collective-permute-start | bytes 1572872 | tf_op jit(solution)/shard_map/ppermute | solution.py:169
  24.2 13.2 %collective-permute-start.1 = (bf16[256,512]{1,0:T(8,128)(2,1)}, bf16[256,512]{1,0:T(8,128)(2,1)S(1)}, u32[]{:S(2)}, u32[]{:S(2)}) collective-permute-start(bf16[256,512]{1,0:T(8,128)(2,1)} %get-tuple-element.18), channel_id=1, source_target_pairs={{0,256},{256,2},{2,258},{258,0},{1,257},{257,3},{3,259},{259,1},{4... | collective-permute-start | bytes 786440 | tf_op jit(solution)/shard_map/ppermute | solution.py:182
  27.4 14.6 %collective-permute-start.2 = (bf16[256,512]{1,0:T(8,128)(2,1)}, bf16[256,512]{1,0:T(8,128)(2,1)S(1)}, u32[]{:S(2)}, u32[]{:S(2)}) collective-permute-start(bf16[256,512]{1,0:T(8,128)(2,1)} %get-tuple-element.19), channel_id=1, source_target_pairs={{0,2},{256,258},{2,0},{258,256},{1,3},{257,259},{3,1},{259,257},{4... | collective-permute-start | bytes 786440 | tf_op jit(solution)/shard_map/ppermute | solution.py:182
  31.9 11.0 %collective-permute-start.3 = (bf16[256,512]{1,0:T(8,128)(2,1)S(1)}, bf16[256,512]{1,0:T(8,128)(2,1)S(1)}, u32[]{:S(2)}, u32[]{:S(2)}) collective-permute-start(bf16[256,512]{1,0:T(8,128)(2,1)S(1)} %get-tuple-element.20), channel_id=1, source_target_pairs={{0,258},{256,0},{2,256},{258,2},{1,259},{257,1},{3,257},{259,3},{4... | collective-permute-start | bytes 786440 | tf_op jit(solution)/shard_map/ppermute | solution.py:182
  42.9 12.3 %collective-permute-start.4 = (bf16[96,2048]{1,0:T(8,128)(2,1)S(1)}, bf16[96,2048]{1,0:T(8,128)(2,1)S(1)}, u32[]{:S(2)}, u32[]{:S(2)}) collective-permute-start(bf16[96,2048]{1,0:T(8,128)(2,1)S(1)} %shard_map.61.refs_0_), channel_id=1, source_target_pairs={{0,64},{64,128},{128,192},{192,0},{1,65},{65,129},{129,193},{193,1... | collective-permute-start | bytes 1179656 | tf_op jit(solution)/shard_map/ppermute | solution.py:191
  46.1 19.1 %collective-permute-start.6 = (bf16[96,2048]{1,0:T(8,128)(2,1)S(1)}, bf16[96,2048]{1,0:T(8,128)(2,1)S(1)}, u32[]{:S(2)}, u32[]{:S(2)}) collective-permute-start(bf16[96,2048]{1,0:T(8,128)(2,1)S(1)} %shard_map.61.refs_0_), channel_id=1, source_target_pairs={{0,192},{64,0},{128,64},{192,128},{1,193},{65,1},{129,65},{193,129... | collective-permute-start | bytes 1179656 | tf_op jit(solution)/shard_map/ppermute | solution.py:191
  55.2 13.4 %collective-permute-start.5 = (bf16[96,2048]{1,0:T(8,128)(2,1)S(1)}, bf16[96,2048]{1,0:T(8,128)(2,1)S(1)}, u32[]{:S(2)}, u32[]{:S(2)}) collective-permute-start(bf16[96,2048]{1,0:T(8,128)(2,1)S(1)} %collective-permute-done.4.refs_1_), channel_id=1, source_target_pairs={{0,64},{64,128},{128,192},{192,0},{1,65},{65,129},{129,193},{193,1... | collective-permute-start | bytes 1179656 | tf_op jit(solution)/shard_map/ppermute | solution.py:192
  57.1 17.9 %collective-permute-start.7 = (bf16[96,2048]{1,0:T(8,128)(2,1)S(1)}, bf16[96,2048]{1,0:T(8,128)(2,1)S(1)}, u32[]{:S(2)}, u32[]{:S(2)}) collective-permute-start(bf16[96,2048]{1,0:T(8,128)(2,1)S(1)} %shard_map.61.refs_0_), channel_id=1, source_target_pairs={{0,256},{256,2},{2,258},{258,0},{1,257},{257,3},{3,259},{259,1},{4... | collective-permute-start | bytes 1179656 | tf_op jit(solution)/shard_map/ppermute | solution.py:193
  63.3 16.2 %collective-permute-start.8 = (bf16[96,2048]{1,0:T(8,128)(2,1)S(1)}, bf16[96,2048]{1,0:T(8,128)(2,1)S(1)}, u32[]{:S(2)}, u32[]{:S(2)}) collective-permute-start(bf16[96,2048]{1,0:T(8,128)(2,1)S(1)} %collective-permute-done.4.refs_1_), channel_id=1, source_target_pairs={{0,258},{256,0},{2,256},{258,2},{1,259},{257,1},{3,257},{259,3},{4... | collective-permute-start | bytes 1179656 | tf_op jit(solution)/shard_map/ppermute | solution.py:193
  65.2 14.3 %collective-permute-start.10 = (bf16[96,2048]{1,0:T(8,128)(2,1)S(1)}, bf16[96,2048]{1,0:T(8,128)(2,1)S(1)}, u32[]{:S(2)}, u32[]{:S(2)}) collective-permute-start(bf16[96,2048]{1,0:T(8,128)(2,1)S(1)} %collective-permute-done.6.refs_3_), channel_id=1, source_target_pairs={{0,256},{256,2},{2,258},{258,0},{1,257},{257,3},{3,259},{259,1},{4... | collective-permute-start | bytes 1179656 | tf_op jit(solution)/shard_map/ppermute | solution.py:193
  68.6 14.8 %collective-permute-start.9 = (bf16[96,2048]{1,0:T(8,128)(2,1)S(1)}, bf16[96,2048]{1,0:T(8,128)(2,1)S(1)}, u32[]{:S(2)}, u32[]{:S(2)}) collective-permute-start(bf16[96,2048]{1,0:T(8,128)(2,1)S(1)} %collective-permute-done.5.refs_2_), channel_id=1, source_target_pairs={{0,258},{256,0},{2,256},{258,2},{1,259},{257,1},{3,257},{259,3},{4... | collective-permute-start | bytes 1179656 | tf_op jit(solution)/shard_map/ppermute | solution.py:193
  73.8 1.1 copy-start.3
  84.2 19.0 %copy-start.5 = (bf16[384,2048]{1,0:T(8,128)(2,1)}, bf16[384,2048]{1,0:T(8,128)(2,1)S(1)}, u32[]{:S(2)}) copy-start(bf16[384,2048]{1,0:T(8,128)(2,1)S(1)} %get-tuple-element.27.refs_4_) | copy-start | bytes 4718596
  84.2 4.9 %collective-permute-start.11 = (f32[128,768]{1,0:T(8,128)S(1)}, f32[128,768]{1,0:T(8,128)S(1)}, u32[]{:S(2)}, u32[]{:S(2)}) collective-permute-start(f32[128,768]{1,0:T(8,128)S(1)} %get-tuple-element.25), channel_id=1, source_target_pairs={{0,1},{1,0},{2,3},{3,2},{4,5},{5,4},{6,7},{7,6},{8,9},{9,8},{10,11... | collective-permute-start | bytes 1179656 | tf_op jit(solution)/shard_map/ppermute | solution.py:169
  103.2 5.3 %collective-permute-start.12 = (bf16[4,128,768]{2,1,0:T(8,128)(2,1)S(1)}, bf16[4,128,768]{2,1,0:T(8,128)(2,1)S(1)}, u32[]{:S(2)}, u32[]{:S(2)}) collective-permute-start(bf16[4,128,768]{2,1,0:T(8,128)(2,1)S(1)} %all_to_all.25.w_own.refs_1_), channel_id=1, source_target_pairs={{0,1},{1,0},{2,3},{3,2},{4,5},{5,4},{6,7},{7,6},{8,9},{9,8},{10,11... | collective-permute-start | bytes 2359304 | tf_op jit(solution)/shard_map/ppermute | solution.py:169
  134.6 28.3 %all-to-all-start.3 = ((f32[16,48,128]{2,1,0:T(8,128)}), f32[16,48,128]{2,1,0:T(8,128)S(1)}, u32[]{:S(2)}, u32[]{:S(2)}) async-start(f32[16,48,128]{2,1,0:T(8,128)} %shard_map.66.refs_5_), calls=%async_computation.3 | async-start | bytes 786432 | tf_op jit(solution)/shard_map/all_to_all | solution.py:170
  146.3 1.4 copy-start.4
  147.7 1.4 copy-start.6
  151.0 6.3 %collective-permute-start.13 = (f32[128,2048]{1,0:T(8,128)S(1)}, f32[128,2048]{1,0:T(8,128)S(1)}, u32[]{:S(2)}, u32[]{:S(2)}) collective-permute-start(f32[128,2048]{1,0:T(8,128)S(1)} %get-tuple-element.29), channel_id=1, source_target_pairs={{0,1},{1,0},{2,3},{3,2},{4,5},{5,4},{6,7},{7,6},{8,9},{9,8},{10,11... | collective-permute-start | bytes 3145736 | tf_op jit(solution)/shard_map/ppermute | solution.py:169
  162.8 1.6 copy-start.1

commit v4 on v3

--- a/solution.py
+++ b/solution.py
@@ -27,7 +27,7 @@
     return [(place(y), place((y + by) % 4)) for y in range(4)]
 
 
-def call(kernel, outs, *args, smem=0, after=0, limit=16, scratch=(), flops=0):
+def call(kernel, outs, *args, smem=0, after=0, out_spaces=None, limit=16, scratch=(), flops=0):
     count = len(args)
     in_specs = [pl.BlockSpec(memory_space=pltpu.SMEM)] * smem
     in_specs += [pl.BlockSpec(memory_space=pltpu.VMEM)] * (count - smem - after)
@@ -40,7 +40,7 @@
         body,
         out_shape=outs,
         in_specs=in_specs,
-        out_specs=[pl.BlockSpec(memory_space=pltpu.VMEM)] * len(outs),
+        out_specs=[pl.BlockSpec(memory_space=space) for space in out_spaces or [pltpu.VMEM] * len(outs)],
         scratch_shapes=list(scratch),
         compiler_params=pltpu.CompilerParams(vmem_limit_bytes=limit * MIB),
         cost_estimate=pl.CostEstimate(flops=flops, bytes_accessed=size, transcendentals=0),
@@ -110,10 +110,16 @@
         gx[:, cols] = part[QDEV:]
 
 
-def join_kernel(core_ref, go, gx, out):
+def join_kernel(core_ref, go, gx, out, token, done):
     core = core_ref[0]
-    out[:, pl.ds(pl.multiple_of(core * HALF, 128), HALF)] = go[...]
-    out[:, pl.ds(pl.multiple_of((1 - core) * HALF, 128), HALF)] = gx[...]
+    copies = []
+    for i, (part, at) in enumerate(((go, core), (gx, 1 - core))):
+        cols = pl.ds(pl.multiple_of(at * HALF, 128), HALF)
+        copies.append(pltpu.make_async_copy(part, out.at[:, cols], done.at[i]))
+        copies[i].start()
+    token[...] = jnp.zeros(token.shape, F32)
+    for copy in copies:
+        copy.wait()
 
 
 def pool_kernel(at_ref, w_own, w_oth, q0, q1, q2, q3, out, w_all, q_all):
@@ -188,9 +194,14 @@
     )
 
     block = call(hold_kernel, [sd((ROWS, HALF), BF16)], block, q2, *group, count, target, after=7)[0]
-    near = [block, lax.ppermute(block, "x", shift(4, 1)), None, lax.ppermute(block, "x", shift(4, 3))]
-    near[2] = lax.ppermute(near[1], "x", shift(4, 1))
-    far = [lax.ppermute(b, Y, along_y(by)) for b, by in zip(near, (1, -1, -1, 1))]
+    far0 = lax.ppermute(block, Y, along_y(1))
+    near = [block] + [lax.ppermute(block, "x", shift(4, by)) for by in (1, 2, 3)]
+    far = [
+        far0,
+        lax.ppermute(far0, "x", shift(4, 1)),
+        lax.ppermute(near[2], Y, along_y(1)),
+        lax.ppermute(far0, "x", shift(4, 3)),
+    ]
 
     s_near, pool_near = call(
         near_kernel, [sd((2 * QDEV, SIDE), F32), sd((SIDE, HALF), BF16)], q2, *near, flops=256 * NP * HALF
@@ -219,9 +230,12 @@
         jnp.stack([here, yl]), w_own, w_oth, pool_near, pool_far, sums,
         smem=1, after=1, scratch=[pltpu.VMEM((2 * QDEV, NP), BF16)], flops=2 * 256 * NP * HALF,
     )
-    query_grad = call(join_kernel, [sd((QDEV, D), F32)], core.reshape(1), g_own, other(g_out), smem=1)[0]
-
-    by_y = swap(call(z_sum_kernel, [sd((8, 24, 128), F32)], by_z, query_grad, after=1)[0], Y + ("c",))
+    query_grad, token = call(
+        join_kernel, [sd((QDEV, D), F32), sd((8, 128), F32)], core.reshape(1), g_own, other(g_out),
+        smem=1, out_spaces=(pltpu.HBM, pltpu.VMEM), scratch=[pltpu.SemaphoreType.DMA((2,))],
+    )
+
+    by_y = swap(call(z_sum_kernel, [sd((8, 24, 128), F32)], by_z, token, after=1)[0], Y + ("c",))
     passage_grad = call(last_kernel, [sd((6, D), F32)], by_y)[0]
     return query_grad, passage_grad
 

time: 181 us -> 174 us (0.961)
  waiting for transfers between devices: 31.4 us -> 27.4 us
    ppermute x7, waiting for transfers between devices: 14.2 us -> 10.1 us  [the longest x1 6.46 us: shards(): lax.ppermute(far0, 'x', shift(4, 3))]
    unnamed x22 -> x20, local copies, waits for them, and re-layouts: 7.61 us -> 6.01 us
  transfers between devices with their start and end apart: 16 -> 16, of which waited for: 11 -> 12; matrix products, arithmetic and copies ran while one was open for 1% -> 1% of each run, Pallas kernels for 3% -> 3%
where the time goes in v4:
time: 174 us
  starting transfers between devices  75.4 us (43%)
  blocking collectives  52.6 us (30%)
  waiting for transfers between devices  27.4 us (16%)
  Pallas kernels  9.85 us (6%)
  local copies, waits for them, and re-layouts  6.97 us (4%)
    all_to_all x3, blocking collectives, shards(): swap = lambda a, axes: lax.all_to_all(a, axes, 0, 0, tiled=True)  52.6 us
    all_to_all x2, starting transfers between devices, shards(): swap = lambda a, axes: lax.all_to_all(a, axes, 0, 0, tiled=True)  27.6 us
    ppermute x4, starting transfers between devices, shards(): other = lambda a: lax.ppermute(a, 'c', shift(2, 1))  13.6 us
    ppermute x3, starting transfers between devices, shards(): lax.ppermute(parts[s], Y, along_y(s))  10.7 us
    ppermute x3, starting transfers between devices, shards(): lax.ppermute(block, 'x', shift(4, by))  9.93 us
    pallas_call x12, Pallas kernels, call(): pl.pallas_call(body, out_shape=outs, in_specs=in_specs, out_specs=[pl.Blo...  9.85 us
    ppermute x4, waiting for transfers between devices, shards(): other = lambda a: lax.ppermute(a, 'c', shift(2, 1))  6.83 us
    ppermute x1, waiting for transfers between devices, shards(): lax.ppermute(far0, 'x', shift(4, 3))  6.46 us
  transfers between devices with their start and end apart: 16, of which 12 were waited for; matrix products, arithmetic and copies ran while one was open for 1% of the time, Pallas kernels for 3%

profile of v4, /device:TPU:1, one launch (start us, length us, event | category | flops | bytes accessed | tf_op | source)
XLA Modules:
  0.0 173.5 jit_solution(2493566879701114789)
XLA Ops:
  0.7 0.8 copy-done
  1.5 0.8 broadcast_in_dim.8
  2.3 15.9 %all-to-all-start = ((bf16[16,6,16,128]{3,2,1,0:T(8,128)(2,1)}), bf16[16,6,16,128]{3,2,1,0:T(8,128)(2,1)}, u32[]{:S(2)}, u32[]{:S(2)}) async-start(bf16[16,6,16,128]{3,2,1,0:T(8,128)(2,1)} %broadcast_in_dim.8), calls=%async_computation | async-start | bytes 786432 | tf_op jit(solution)/shard_map/all_to_all | solution.py:176
  18.3 2.9 %collective-permute-start = (bf16[128,2048]{1,0:T(8,128)(2,1)S(1)}, bf16[128,2048]{1,0:T(8,128)(2,1)S(1)}, u32[]{:S(2)}, u32[]{:S(2)}) collective-permute-start(bf16[128,2048]{1,0:T(8,128)(2,1)S(1)} %constant_dynamic-slice_fusion), channel_id=1, source_target_pairs={{0,1},{1,0},{2,3},{3,2},{4,5},{5,4},{6,7},{7,6},{8,9},{9,8},{10,11... | collective-permute-start | bytes 1572872 | tf_op jit(solution)/shard_map/ppermute | solution.py:175
  21.2 1.4 collective-permute-done.q_oth
  22.7 1.5 shard_map.59
  24.2 3.2 %collective-permute-start.1 = (bf16[256,512]{1,0:T(8,128)(2,1)}, bf16[256,512]{1,0:T(8,128)(2,1)S(1)}, u32[]{:S(2)}, u32[]{:S(2)}) collective-permute-start(bf16[256,512]{1,0:T(8,128)(2,1)} %get-tuple-element.20), channel_id=1, source_target_pairs={{0,256},{256,2},{2,258},{258,0},{1,257},{257,3},{3,259},{259,1},{4... | collective-permute-start | bytes 786440 | tf_op jit(solution)/shard_map/ppermute | solution.py:188
  27.4 4.5 %collective-permute-start.2 = (bf16[256,512]{1,0:T(8,128)(2,1)}, bf16[256,512]{1,0:T(8,128)(2,1)S(1)}, u32[]{:S(2)}, u32[]{:S(2)}) collective-permute-start(bf16[256,512]{1,0:T(8,128)(2,1)} %get-tuple-element.21), channel_id=1, source_target_pairs={{0,2},{256,258},{2,0},{258,256},{1,3},{257,259},{3,1},{259,257},{4... | collective-permute-start | bytes 786440 | tf_op jit(solution)/shard_map/ppermute | solution.py:188
  31.9 3.0 %collective-permute-start.3 = (bf16[256,512]{1,0:T(8,128)(2,1)S(1)}, bf16[256,512]{1,0:T(8,128)(2,1)S(1)}, u32[]{:S(2)}, u32[]{:S(2)}) collective-permute-start(bf16[256,512]{1,0:T(8,128)(2,1)S(1)} %get-tuple-element.22), channel_id=1, source_target_pairs={{0,258},{256,0},{2,256},{258,2},{1,259},{257,1},{3,257},{259,3},{4... | collective-permute-start | bytes 786440 | tf_op jit(solution)/shard_map/ppermute | solution.py:188
  34.9 0.1 copy.6.pos
  35.0 0.1 copy.7.neg
  35.2 0.4 shard_map.60
  35.6 0.7 all-to-all-done
  36.3 1.1 copy.12
  37.4 4.5 %collective-permute-done.2.refs_4_.q2 = bf16[256,512]{1,0:T(8,128)(2,1)S(1)} collective-permute-done((bf16[256,512]{1,0:T(8,128)(2,1)}, bf16[256,512]{1,0:T(8,128)(2,1)S(1)}, u32[]{:S(2)}, u32[]{:S(2)}) %collective-permute-start.2) | collective-permute-done | bytes 262176 | tf_op jit(solution)/shard_map/ppermute | solution.py:188
  41.9 1.0 collective-permute-done.3.refs_5_.q3
  42.9 5.1 %collective-permute-start.7 = (bf16[96,2048]{1,0:T(8,128)(2,1)S(1)}, bf16[96,2048]{1,0:T(8,128)(2,1)S(1)}, u32[]{:S(2)}, u32[]{:S(2)}) collective-permute-start(bf16[96,2048]{1,0:T(8,128)(2,1)S(1)} %shard_map.61.refs_0_), channel_id=1, source_target_pairs={{0,256},{256,2},{2,258},{258,0},{1,257},{257,3},{3,259},{259,1},{4... | collective-permute-start | bytes 1179656 | tf_op jit(solution)/shard_map/ppermute | solution.py:197
  48.1 4.7 %collective-permute-start.5 = (bf16[96,2048]{1,0:T(8,128)(2,1)S(1)}, bf16[96,2048]{1,0:T(8,128)(2,1)S(1)}, u32[]{:S(2)}, u32[]{:S(2)}) collective-permute-start(bf16[96,2048]{1,0:T(8,128)(2,1)S(1)} %shard_map.61.refs_0_), channel_id=1, source_target_pairs={{0,128},{64,192},{128,0},{192,64},{1,129},{65,193},{129,1},{193,65... | collective-permute-start | bytes 1179656 | tf_op jit(solution)/shard_map/ppermute | solution.py:198
  52.7 2.8 %collective-permute-start.6 = (bf16[96,2048]{1,0:T(8,128)(2,1)S(1)}, bf16[96,2048]{1,0:T(8,128)(2,1)S(1)}, u32[]{:S(2)}, u32[]{:S(2)}) collective-permute-start(bf16[96,2048]{1,0:T(8,128)(2,1)S(1)} %shard_map.61.refs_0_), channel_id=1, source_target_pairs={{0,192},{64,0},{128,64},{192,128},{1,193},{65,1},{129,65},{193,129... | collective-permute-start | bytes 1179656 | tf_op jit(solution)/shard_map/ppermute | solution.py:198
  55.5 2.5 %collective-permute-start.4 = (bf16[96,2048]{1,0:T(8,128)(2,1)S(1)}, bf16[96,2048]{1,0:T(8,128)(2,1)S(1)}, u32[]{:S(2)}, u32[]{:S(2)}) collective-permute-start(bf16[96,2048]{1,0:T(8,128)(2,1)S(1)} %shard_map.61.refs_0_), channel_id=1, source_target_pairs={{0,64},{64,128},{128,192},{192,0},{1,65},{65,129},{129,193},{193,1... | collective-permute-start | bytes 1179656 | tf_op jit(solution)/shard_map/ppermute | solution.py:198
  58.0 4.0 %collective-permute-start.10 = (bf16[96,2048]{1,0:T(8,128)(2,1)S(1)}, bf16[96,2048]{1,0:T(8,128)(2,1)S(1)}, u32[]{:S(2)}, u32[]{:S(2)}) collective-permute-start(bf16[96,2048]{1,0:T(8,128)(2,1)S(1)} %collective-permute-done.7.refs_0_), channel_id=1, source_target_pairs={{0,192},{64,0},{128,64},{192,128},{1,193},{65,1},{129,65},{193,129... | collective-permute-start | bytes 1179656 | tf_op jit(solution)/shard_map/ppermute | solution.py:203
  62.0 1.9 %collective-permute-start.8 = (bf16[96,2048]{1,0:T(8,128)(2,1)S(1)}, bf16[96,2048]{1,0:T(8,128)(2,1)S(1)}, u32[]{:S(2)}, u32[]{:S(2)}) collective-permute-start(bf16[96,2048]{1,0:T(8,128)(2,1)S(1)} %collective-permute-done.7.refs_0_), channel_id=1, source_target_pairs={{0,64},{64,128},{128,192},{192,0},{1,65},{65,129},{129,193},{193,1... | collective-permute-start | bytes 1179656 | tf_op jit(solution)/shard_map/ppermute | solution.py:201
  63.9 2.5 %collective-permute-start.9 = (bf16[96,2048]{1,0:T(8,128)(2,1)S(1)}, bf16[96,2048]{1,0:T(8,128)(2,1)S(1)}, u32[]{:S(2)}, u32[]{:S(2)}) collective-permute-start(bf16[96,2048]{1,0:T(8,128)(2,1)S(1)} %collective-permute-done.5.refs_2_), channel_id=1, source_target_pairs={{0,256},{256,2},{2,258},{258,0},{1,257},{257,3},{3,259},{259,1},{4... | collective-permute-start | bytes 1179656 | tf_op jit(solution)/shard_map/ppermute | solution.py:202
  66.5 3.5 %collective-permute-done.6.refs_3_ = bf16[96,2048]{1,0:T(8,128)(2,1)S(1)} collective-permute-done((bf16[96,2048]{1,0:T(8,128)(2,1)S(1)}, bf16[96,2048]{1,0:T(8,128)(2,1)S(1)}, u32[]{:S(2)}, u32[]{:S(2)}) %collective-permute-start.6) | collective-permute-done | bytes 393248 | tf_op jit(solution)/shard_map/ppermute | solution.py:198
  70.1 0.7 shard_map.62
  70.8 1.1 copy-done.2
  72.0 6.5 %collective-permute-done.10.refs_3_ = bf16[96,2048]{1,0:T(8,128)(2,1)S(1)} collective-permute-done((bf16[96,2048]{1,0:T(8,128)(2,1)S(1)}, bf16[96,2048]{1,0:T(8,128)(2,1)S(1)}, u32[]{:S(2)}, u32[]{:S(2)}) %collective-permute-start.10) | collective-permute-done | bytes 393248 | tf_op jit(solution)/shard_map/ppermute | solution.py:203
  78.5 0.7 shard_map.63
  79.2 3.4 %collective-permute-start.11 = (f32[128,768]{1,0:T(8,128)S(1)}, f32[128,768]{1,0:T(8,128)S(1)}, u32[]{:S(2)}, u32[]{:S(2)}) collective-permute-start(f32[128,768]{1,0:T(8,128)S(1)} %get-tuple-element.27), channel_id=1, source_target_pairs={{0,1},{1,0},{2,3},{3,2},{4,5},{5,4},{6,7},{7,6},{8,9},{9,8},{10,11... | collective-permute-start | bytes 1179656 | tf_op jit(solution)/shard_map/ppermute | solution.py:175
  82.6 1.3 collective-permute-done.11.sr
  84.0 0.3 shard_map.64
  84.2 13.9 %all_to_all.25.w_own.refs_1_ = bf16[4,128,768]{2,1,0:T(8,128)(2,1)S(1)} all-to-all(bf16[4,128,768]{2,1,0:T(8,128)(2,1)S(1)} %shard_map.64), channel_id=1, replica_groups=mesh['yl'=2,'x'=4,'z'=16,'yh'=2,'c'=2] {'yl','yh'}, dimensions={0} | all-to-all | bytes 1572864 | tf_op jit(solution)/shard_map/all_to_all | solution.py:176
  98.1 3.4 %collective-permute-start.12 = (bf16[4,128,768]{2,1,0:T(8,128)(2,1)S(1)}, bf16[4,128,768]{2,1,0:T(8,128)(2,1)S(1)}, u32[]{:S(2)}, u32[]{:S(2)}) collective-permute-start(bf16[4,128,768]{2,1,0:T(8,128)(2,1)S(1)} %all_to_all.25.w_own.refs_1_), channel_id=1, source_target_pairs={{0,1},{1,0},{2,3},{3,2},{4,5},{5,4},{6,7},{7,6},{8,9},{9,8},{10,11... | collective-permute-start | bytes 2359304 | tf_op jit(solution)/shard_map/ppermute | solution.py:175
  101.5 0.1 pad_add_fusion.2.at_ref
  101.6 1.8 %collective-permute-done.12.w_oth.refs_2_ = bf16[4,128,768]{2,1,0:T(8,128)(2,1)S(1)} collective-permute-done((bf16[4,128,768]{2,1,0:T(8,128)(2,1)S(1)}, bf16[4,128,768]{2,1,0:T(8,128)(2,1)S(1)}, u32[]{:S(2)}, u32[]{:S(2)}) %collective-permute-start.12) | collective-permute-done | bytes 786464 | tf_op jit(solution)/shard_map/ppermute | solution.py:175
  103.4 1.6 shard_map.65
  105.0 23.5 %all_to_all.26.parts = f32[4,192,512]{2,1,0:T(8,128)S(1)} all-to-all(f32[4,192,512]{2,1,0:T(8,128)S(1)} %shard_map.65), channel_id=1, replica_groups=mesh['yl'=2,'x'=4,'z'=16,'yh'=2,'c'=2] {'x'}, dimensions={0} | all-to-all | bytes 3145728 | tf_op jit(solution)/shard_map/all_to_all | solution.py:176
  128.5 0.8 shard_map.66.refs_5_
  129.3 11.7 %all-to-all-start.3 = ((f32[16,48,128]{2,1,0:T(8,128)}), f32[16,48,128]{2,1,0:T(8,128)S(1)}, u32[]{:S(2)}, u32[]{:S(2)}) async-start(f32[16,48,128]{2,1,0:T(8,128)} %shard_map.66.refs_5_), calls=%async_computation.3 | async-start | bytes 786432 | tf_op jit(solution)/shard_map/all_to_all | solution.py:176
  141.1 1.4 copy-done.3
  142.5 1.4 copy-done.5
  143.9 1.8 %shard_map.67 = (f32[128,2048]{1,0:T(8,128)S(1)}, f32[128,2048]{1,0:T(8,128)S(1)}) custom-call(s32[2]{0:T(128)S(1)} %pad_add_fusion.refs_0_, bf16[4,128,768]{2,1,0:T(8,128)(2,1)S(1)} %all_to_all.25.w_own.refs_1_, bf16[4,128,768]{2,1,0:T(8,128)(2,1)S(1)} %collective-permute-done.12.w_oth.refs_2_, bf16[384,2048]{1,0:T(8,128)(2,1)S(1)} %copy-done.3, ...), custom_call_target="tpu_custom_call" | custom-call | flops 805306368 | bytes 7208968 | tf_op jit(solution)/shard_map/pallas_call | solution.py:39
  145.8 4.0 %collective-permute-start.13 = (f32[128,2048]{1,0:T(8,128)S(1)}, f32[128,2048]{1,0:T(8,128)S(1)}, u32[]{:S(2)}, u32[]{:S(2)}) collective-permute-start(f32[128,2048]{1,0:T(8,128)S(1)} %get-tuple-element.31), channel_id=1, source_target_pairs={{0,1},{1,0},{2,3},{3,2},{4,5},{5,4},{6,7},{7,6},{8,9},{9,8},{10,11... | collective-permute-start | bytes 3145736 | tf_op jit(solution)/shard_map/ppermute | solution.py:175
  149.8 2.3 %collective-permute-done.13.gx = f32[128,2048]{1,0:T(8,128)S(1)} collective-permute-done((f32[128,2048]{1,0:T(8,128)S(1)}, f32[128,2048]{1,0:T(8,128)S(1)}, u32[]{:S(2)}, u32[]{:S(2)}) %collective-permute-start.13) | collective-permute-done | bytes 1048608 | tf_op jit(solution)/shard_map/ppermute | solution.py:175
  152.0 1.3 shard_map.68
  153.4 4.2 %all-to-all-done.3.refs_0_ = f32[16,48,128]{2,1,0:T(8,128)S(1)} async-done(((f32[16,48,128]{2,1,0:T(8,128)}), f32[16,48,128]{2,1,0:T(8,128)S(1)}, u32[]{:S(2)}, u32[]{:S(2)}) %all-to-all-start.3) | async-done | bytes 393248 | tf_op jit(solution)/shard_map/all_to_all | solution.py:176
  157.6 15.2 %all_to_all.27.parts = f32[8,24,128]{2,1,0:T(8,128)S(1)} all-to-all(f32[8,24,128]{2,1,0:T(8,128)S(1)} %shard_map.69), channel_id=1, replica_groups=mesh['yl'=2,'x'=4,'z'=16,'yh'=2,'c'=2] {'yl','yh','c'}, dimensions={0} | all-to-all | bytes 196608 | tf_op jit(solution)/shard_map/all_to_all | solution.py:176
  172.9 0.7 shard_map.70
  (26 shorter events, 0.5 us)
Async XLA Ops:
  0.6 0.8 copy-start
  0.6 17.6 %copy-start.1 = (bf16[128,4096]{1,0:T(8,128)(2,1)S(1)}, bf16[128,4096]{1,0:T(8,128)(2,1)}, u32[]{:S(2)}) copy-start(bf16[128,4096]{1,0:T(8,128)(2,1)} %queries.1) | copy-start | bytes 3145732
  2.3 32.6 %copy-start.7 = (s32[128]{0:T(128)S(1)}, s32[128]{0:T(128)}, u32[]{:S(2)}) copy-start(s32[128]{0:T(128)} %param.6) | copy-start | bytes 1540
  2.3 32.7 %copy-start.6 = (s32[128,7]{0,1:T(8,128)S(1)}, s32[128,7]{0,1:T(8,128)}, u32[]{:S(2)}) copy-start(s32[128,7]{0,1:T(8,128)} %param.7) | copy-start | bytes 10756
  2.3 34.0 %all-to-all-start = ((bf16[16,6,16,128]{3,2,1,0:T(8,128)(2,1)}), bf16[16,6,16,128]{3,2,1,0:T(8,128)(2,1)}, u32[]{:S(2)}, u32[]{:S(2)}) async-start(bf16[16,6,16,128]{3,2,1,0:T(8,128)(2,1)} %broadcast_in_dim.8), calls=%async_computation | async-start | bytes 786432 | tf_op jit(solution)/shard_map/all_to_all | solution.py:176
  18.3 4.4 %collective-permute-start = (bf16[128,2048]{1,0:T(8,128)(2,1)S(1)}, bf16[128,2048]{1,0:T(8,128)(2,1)S(1)}, u32[]{:S(2)}, u32[]{:S(2)}) collective-permute-start(bf16[128,2048]{1,0:T(8,128)(2,1)S(1)} %constant_dynamic-slice_fusion), channel_id=1, source_target_pairs={{0,1},{1,0},{2,3},{3,2},{4,5},{5,4},{6,7},{7,6},{8,9},{9,8},{10,11... | collective-permute-start | bytes 1572872 | tf_op jit(solution)/shard_map/ppermute | solution.py:175
  24.2 13.2 %collective-permute-start.1 = (bf16[256,512]{1,0:T(8,128)(2,1)}, bf16[256,512]{1,0:T(8,128)(2,1)S(1)}, u32[]{:S(2)}, u32[]{:S(2)}) collective-permute-start(bf16[256,512]{1,0:T(8,128)(2,1)} %get-tuple-element.20), channel_id=1, source_target_pairs={{0,256},{256,2},{2,258},{258,0},{1,257},{257,3},{3,259},{259,1},{4... | collective-permute-start | bytes 786440 | tf_op jit(solution)/shard_map/ppermute | solution.py:188
  27.4 14.6 %collective-permute-start.2 = (bf16[256,512]{1,0:T(8,128)(2,1)}, bf16[256,512]{1,0:T(8,128)(2,1)S(1)}, u32[]{:S(2)}, u32[]{:S(2)}) collective-permute-start(bf16[256,512]{1,0:T(8,128)(2,1)} %get-tuple-element.21), channel_id=1, source_target_pairs={{0,2},{256,258},{2,0},{258,256},{1,3},{257,259},{3,1},{259,257},{4... | collective-permute-start | bytes 786440 | tf_op jit(solution)/shard_map/ppermute | solution.py:188
  31.9 11.0 %collective-permute-start.3 = (bf16[256,512]{1,0:T(8,128)(2,1)S(1)}, bf16[256,512]{1,0:T(8,128)(2,1)S(1)}, u32[]{:S(2)}, u32[]{:S(2)}) collective-permute-start(bf16[256,512]{1,0:T(8,128)(2,1)S(1)} %get-tuple-element.22), channel_id=1, source_target_pairs={{0,258},{256,0},{2,256},{258,2},{1,259},{257,1},{3,257},{259,3},{4... | collective-permute-start | bytes 786440 | tf_op jit(solution)/shard_map/ppermute | solution.py:188
  42.9 15.1 %collective-permute-start.7 = (bf16[96,2048]{1,0:T(8,128)(2,1)S(1)}, bf16[96,2048]{1,0:T(8,128)(2,1)S(1)}, u32[]{:S(2)}, u32[]{:S(2)}) collective-permute-start(bf16[96,2048]{1,0:T(8,128)(2,1)S(1)} %shard_map.61.refs_0_), channel_id=1, source_target_pairs={{0,256},{256,2},{2,258},{258,0},{1,257},{257,3},{3,259},{259,1},{4... | collective-permute-start | bytes 1179656 | tf_op jit(solution)/shard_map/ppermute | solution.py:197
  48.1 15.9 %collective-permute-start.5 = (bf16[96,2048]{1,0:T(8,128)(2,1)S(1)}, bf16[96,2048]{1,0:T(8,128)(2,1)S(1)}, u32[]{:S(2)}, u32[]{:S(2)}) collective-permute-start(bf16[96,2048]{1,0:T(8,128)(2,1)S(1)} %shard_map.61.refs_0_), channel_id=1, source_target_pairs={{0,128},{64,192},{128,0},{192,64},{1,129},{65,193},{129,1},{193,65... | collective-permute-start | bytes 1179656 | tf_op jit(solution)/shard_map/ppermute | solution.py:198
  52.7 17.3 %collective-permute-start.6 = (bf16[96,2048]{1,0:T(8,128)(2,1)S(1)}, bf16[96,2048]{1,0:T(8,128)(2,1)S(1)}, u32[]{:S(2)}, u32[]{:S(2)}) collective-permute-start(bf16[96,2048]{1,0:T(8,128)(2,1)S(1)} %shard_map.61.refs_0_), channel_id=1, source_target_pairs={{0,192},{64,0},{128,64},{192,128},{1,193},{65,1},{129,65},{193,129... | collective-permute-start | bytes 1179656 | tf_op jit(solution)/shard_map/ppermute | solution.py:198
  55.5 14.6 %collective-permute-start.4 = (bf16[96,2048]{1,0:T(8,128)(2,1)S(1)}, bf16[96,2048]{1,0:T(8,128)(2,1)S(1)}, u32[]{:S(2)}, u32[]{:S(2)}) collective-permute-start(bf16[96,2048]{1,0:T(8,128)(2,1)S(1)} %shard_map.61.refs_0_), channel_id=1, source_target_pairs={{0,64},{64,128},{128,192},{192,0},{1,65},{65,129},{129,193},{193,1... | collective-permute-start | bytes 1179656 | tf_op jit(solution)/shard_map/ppermute | solution.py:198
  58.0 20.4 %collective-permute-start.10 = (bf16[96,2048]{1,0:T(8,128)(2,1)S(1)}, bf16[96,2048]{1,0:T(8,128)(2,1)S(1)}, u32[]{:S(2)}, u32[]{:S(2)}) collective-permute-start(bf16[96,2048]{1,0:T(8,128)(2,1)S(1)} %collective-permute-done.7.refs_0_), channel_id=1, source_target_pairs={{0,192},{64,0},{128,64},{192,128},{1,193},{65,1},{129,65},{193,129... | collective-permute-start | bytes 1179656 | tf_op jit(solution)/shard_map/ppermute | solution.py:203
  62.0 16.5 %collective-permute-start.8 = (bf16[96,2048]{1,0:T(8,128)(2,1)S(1)}, bf16[96,2048]{1,0:T(8,128)(2,1)S(1)}, u32[]{:S(2)}, u32[]{:S(2)}) collective-permute-start(bf16[96,2048]{1,0:T(8,128)(2,1)S(1)} %collective-permute-done.7.refs_0_), channel_id=1, source_target_pairs={{0,64},{64,128},{128,192},{192,0},{1,65},{65,129},{129,193},{193,1... | collective-permute-start | bytes 1179656 | tf_op jit(solution)/shard_map/ppermute | solution.py:201
  63.9 14.5 %collective-permute-start.9 = (bf16[96,2048]{1,0:T(8,128)(2,1)S(1)}, bf16[96,2048]{1,0:T(8,128)(2,1)S(1)}, u32[]{:S(2)}, u32[]{:S(2)}) collective-permute-start(bf16[96,2048]{1,0:T(8,128)(2,1)S(1)} %collective-permute-done.5.refs_2_), channel_id=1, source_target_pairs={{0,256},{256,2},{2,258},{258,0},{1,257},{257,3},{3,259},{259,1},{4... | collective-permute-start | bytes 1179656 | tf_op jit(solution)/shard_map/ppermute | solution.py:202
  70.8 1.1 copy-start.2
  79.2 18.9 %copy-start.4 = (bf16[384,2048]{1,0:T(8,128)(2,1)}, bf16[384,2048]{1,0:T(8,128)(2,1)S(1)}, u32[]{:S(2)}) copy-start(bf16[384,2048]{1,0:T(8,128)(2,1)S(1)} %get-tuple-element.29.refs_4_) | copy-start | bytes 4718596
  79.2 4.7 %collective-permute-start.11 = (f32[128,768]{1,0:T(8,128)S(1)}, f32[128,768]{1,0:T(8,128)S(1)}, u32[]{:S(2)}, u32[]{:S(2)}) collective-permute-start(f32[128,768]{1,0:T(8,128)S(1)} %get-tuple-element.27), channel_id=1, source_target_pairs={{0,1},{1,0},{2,3},{3,2},{4,5},{5,4},{6,7},{7,6},{8,9},{9,8},{10,11... | collective-permute-start | bytes 1179656 | tf_op jit(solution)/shard_map/ppermute | solution.py:175
  98.1 5.3 %collective-permute-start.12 = (bf16[4,128,768]{2,1,0:T(8,128)(2,1)S(1)}, bf16[4,128,768]{2,1,0:T(8,128)(2,1)S(1)}, u32[]{:S(2)}, u32[]{:S(2)}) collective-permute-start(bf16[4,128,768]{2,1,0:T(8,128)(2,1)S(1)} %all_to_all.25.w_own.refs_1_), channel_id=1, source_target_pairs={{0,1},{1,0},{2,3},{3,2},{4,5},{5,4},{6,7},{7,6},{8,9},{9,8},{10,11... | collective-permute-start | bytes 2359304 | tf_op jit(solution)/shard_map/ppermute | solution.py:175
  129.3 28.2 %all-to-all-start.3 = ((f32[16,48,128]{2,1,0:T(8,128)}), f32[16,48,128]{2,1,0:T(8,128)S(1)}, u32[]{:S(2)}, u32[]{:S(2)}) async-start(f32[16,48,128]{2,1,0:T(8,128)} %shard_map.66.refs_5_), calls=%async_computation.3 | async-start | bytes 786432 | tf_op jit(solution)/shard_map/all_to_all | solution.py:176
  141.1 1.4 copy-start.3
  142.5 1.4 copy-start.5
  145.8 6.3 %collective-permute-start.13 = (f32[128,2048]{1,0:T(8,128)S(1)}, f32[128,2048]{1,0:T(8,128)S(1)}, u32[]{:S(2)}, u32[]{:S(2)}) collective-permute-start(f32[128,2048]{1,0:T(8,128)S(1)} %get-tuple-element.31), channel_id=1, source_target_pairs={{0,1},{1,0},{2,3},{3,2},{4,5},{5,4},{6,7},{7,6},{8,9},{9,8},{10,11... | collective-permute-start | bytes 3145736 | tf_op jit(solution)/shard_map/ppermute | solution.py:175

commit v5 on v4

--- a/solution.py
+++ b/solution.py
@@ -185,7 +185,8 @@
         prep_kernel, [sd((2 * QDEV, HALF), BF16)] + [sd((2 * QDEV, SLICE), BF16)] * 4,
         jnp.stack([core, y]), queries, q_oth, smem=1,
     )
-    group = [parts[0]] + [lax.ppermute(parts[s], Y, along_y(s)) for s in range(1, 4)]
+    sent = {s: lax.ppermute(parts[s], Y, along_y(s)) for s in (2, 1, 3)}
+    group = [parts[0]] + [sent[s] for s in (1, 2, 3)]
     col = jnp.arange(NP, dtype=jnp.int32)
     side, s, z, r = col // SIDE, (col // ROWS) % 4, (col // 6) % 16, col % 6
     ids = ((side * 4 + (x - s) % 4) * 16 + z) * 6 + r

time: 174 us -> 174 us (level)
  no operation moved by 1% of the time
where the time goes in v5:
time: 174 us
  starting transfers between devices  75.4 us (43%)
  blocking collectives  52.6 us (30%)
  waiting for transfers between devices  27.4 us (16%)
  Pallas kernels  9.85 us (6%)
  local copies, waits for them, and re-layouts  6.97 us (4%)
    all_to_all x3, blocking collectives, shards(): swap = lambda a, axes: lax.all_to_all(a, axes, 0, 0, tiled=True)  52.6 us
    all_to_all x2, starting transfers between devices, shards(): swap = lambda a, axes: lax.all_to_all(a, axes, 0, 0, tiled=True)  27.6 us
    ppermute x4, starting transfers between devices, shards(): other = lambda a: lax.ppermute(a, 'c', shift(2, 1))  13.6 us
    ppermute x3, starting transfers between devices, shards(): sent = {s: lax.ppermute(parts[s], Y, along_y(s)) for s in (2, 1, 3)}  10.7 us
    ppermute x3, starting transfers between devices, shards(): lax.ppermute(block, 'x', shift(4, by))  9.93 us
    pallas_call x12, Pallas kernels, call(): pl.pallas_call(body, out_shape=outs, in_specs=in_specs, out_specs=[pl.Blo...  9.85 us
    ppermute x4, waiting for transfers between devices, shards(): other = lambda a: lax.ppermute(a, 'c', shift(2, 1))  6.83 us
    ppermute x1, waiting for transfers between devices, shards(): lax.ppermute(far0, 'x', shift(4, 3))  6.46 us
  transfers between devices with their start and end apart: 16, of which 12 were waited for; matrix products, arithmetic and copies ran while one was open for 1% of the time, Pallas kernels for 3%

profile of v5, /device:TPU:1, one launch (start us, length us, event | category | flops | bytes accessed | tf_op | source)
XLA Modules:
  0.0 173.5 jit_solution(2493566879701114789)
XLA Ops:
  0.7 0.8 copy-done
  1.5 0.8 broadcast_in_dim.8
  2.3 15.9 %all-to-all-start = ((bf16[16,6,16,128]{3,2,1,0:T(8,128)(2,1)}), bf16[16,6,16,128]{3,2,1,0:T(8,128)(2,1)}, u32[]{:S(2)}, u32[]{:S(2)}) async-start(bf16[16,6,16,128]{3,2,1,0:T(8,128)(2,1)} %broadcast_in_dim.8), calls=%async_computation | async-start | bytes 786432 | tf_op jit(solution)/shard_map/all_to_all | solution.py:176
  18.3 2.9 %collective-permute-start = (bf16[128,2048]{1,0:T(8,128)(2,1)S(1)}, bf16[128,2048]{1,0:T(8,128)(2,1)S(1)}, u32[]{:S(2)}, u32[]{:S(2)}) collective-permute-start(bf16[128,2048]{1,0:T(8,128)(2,1)S(1)} %constant_dynamic-slice_fusion), channel_id=1, source_target_pairs={{0,1},{1,0},{2,3},{3,2},{4,5},{5,4},{6,7},{7,6},{8,9},{9,8},{10,11... | collective-permute-start | bytes 1572872 | tf_op jit(solution)/shard_map/ppermute | solution.py:175
  21.2 1.4 collective-permute-done.q_oth
  22.7 1.5 shard_map.59
  24.2 3.2 %collective-permute-start.1 = (bf16[256,512]{1,0:T(8,128)(2,1)}, bf16[256,512]{1,0:T(8,128)(2,1)S(1)}, u32[]{:S(2)}, u32[]{:S(2)}) collective-permute-start(bf16[256,512]{1,0:T(8,128)(2,1)} %get-tuple-element.20), channel_id=1, source_target_pairs={{0,256},{256,2},{2,258},{258,0},{1,257},{257,3},{3,259},{259,1},{4... | collective-permute-start | bytes 786440 | tf_op jit(solution)/shard_map/ppermute | solution.py:188
  27.4 4.5 %collective-permute-start.2 = (bf16[256,512]{1,0:T(8,128)(2,1)}, bf16[256,512]{1,0:T(8,128)(2,1)S(1)}, u32[]{:S(2)}, u32[]{:S(2)}) collective-permute-start(bf16[256,512]{1,0:T(8,128)(2,1)} %get-tuple-element.21), channel_id=1, source_target_pairs={{0,2},{256,258},{2,0},{258,256},{1,3},{257,259},{3,1},{259,257},{4... | collective-permute-start | bytes 786440 | tf_op jit(solution)/shard_map/ppermute | solution.py:188
  31.9 3.0 %collective-permute-start.3 = (bf16[256,512]{1,0:T(8,128)(2,1)S(1)}, bf16[256,512]{1,0:T(8,128)(2,1)S(1)}, u32[]{:S(2)}, u32[]{:S(2)}) collective-permute-start(bf16[256,512]{1,0:T(8,128)(2,1)S(1)} %get-tuple-element.22), channel_id=1, source_target_pairs={{0,258},{256,0},{2,256},{258,2},{1,259},{257,1},{3,257},{259,3},{4... | collective-permute-start | bytes 786440 | tf_op jit(solution)/shard_map/ppermute | solution.py:188
  34.9 0.1 copy.6.pos
  35.0 0.1 copy.7.neg
  35.2 0.4 shard_map.60
  35.6 0.7 all-to-all-done
  36.3 1.1 copy.12
  37.4 4.5 %collective-permute-done.2.refs_4_.q2 = bf16[256,512]{1,0:T(8,128)(2,1)S(1)} collective-permute-done((bf16[256,512]{1,0:T(8,128)(2,1)}, bf16[256,512]{1,0:T(8,128)(2,1)S(1)}, u32[]{:S(2)}, u32[]{:S(2)}) %collective-permute-start.2) | collective-permute-done | bytes 262176 | tf_op jit(solution)/shard_map/ppermute | solution.py:188
  41.9 1.0 collective-permute-done.3.refs_5_.q3
  42.9 5.1 %collective-permute-start.7 = (bf16[96,2048]{1,0:T(8,128)(2,1)S(1)}, bf16[96,2048]{1,0:T(8,128)(2,1)S(1)}, u32[]{:S(2)}, u32[]{:S(2)}) collective-permute-start(bf16[96,2048]{1,0:T(8,128)(2,1)S(1)} %shard_map.61.refs_0_), channel_id=1, source_target_pairs={{0,256},{256,2},{2,258},{258,0},{1,257},{257,3},{3,259},{259,1},{4... | collective-permute-start | bytes 1179656 | tf_op jit(solution)/shard_map/ppermute | solution.py:198
  48.1 4.7 %collective-permute-start.5 = (bf16[96,2048]{1,0:T(8,128)(2,1)S(1)}, bf16[96,2048]{1,0:T(8,128)(2,1)S(1)}, u32[]{:S(2)}, u32[]{:S(2)}) collective-permute-start(bf16[96,2048]{1,0:T(8,128)(2,1)S(1)} %shard_map.61.refs_0_), channel_id=1, source_target_pairs={{0,128},{64,192},{128,0},{192,64},{1,129},{65,193},{129,1},{193,65... | collective-permute-start | bytes 1179656 | tf_op jit(solution)/shard_map/ppermute | solution.py:199
  52.7 2.8 %collective-permute-start.6 = (bf16[96,2048]{1,0:T(8,128)(2,1)S(1)}, bf16[96,2048]{1,0:T(8,128)(2,1)S(1)}, u32[]{:S(2)}, u32[]{:S(2)}) collective-permute-start(bf16[96,2048]{1,0:T(8,128)(2,1)S(1)} %shard_map.61.refs_0_), channel_id=1, source_target_pairs={{0,192},{64,0},{128,64},{192,128},{1,193},{65,1},{129,65},{193,129... | collective-permute-start | bytes 1179656 | tf_op jit(solution)/shard_map/ppermute | solution.py:199
  55.5 2.5 %collective-permute-start.4 = (bf16[96,2048]{1,0:T(8,128)(2,1)S(1)}, bf16[96,2048]{1,0:T(8,128)(2,1)S(1)}, u32[]{:S(2)}, u32[]{:S(2)}) collective-permute-start(bf16[96,2048]{1,0:T(8,128)(2,1)S(1)} %shard_map.61.refs_0_), channel_id=1, source_target_pairs={{0,64},{64,128},{128,192},{192,0},{1,65},{65,129},{129,193},{193,1... | collective-permute-start | bytes 1179656 | tf_op jit(solution)/shard_map/ppermute | solution.py:199
  58.0 4.0 %collective-permute-start.10 = (bf16[96,2048]{1,0:T(8,128)(2,1)S(1)}, bf16[96,2048]{1,0:T(8,128)(2,1)S(1)}, u32[]{:S(2)}, u32[]{:S(2)}) collective-permute-start(bf16[96,2048]{1,0:T(8,128)(2,1)S(1)} %collective-permute-done.7.refs_0_), channel_id=1, source_target_pairs={{0,192},{64,0},{128,64},{192,128},{1,193},{65,1},{129,65},{193,129... | collective-permute-start | bytes 1179656 | tf_op jit(solution)/shard_map/ppermute | solution.py:204
  62.0 1.9 %collective-permute-start.8 = (bf16[96,2048]{1,0:T(8,128)(2,1)S(1)}, bf16[96,2048]{1,0:T(8,128)(2,1)S(1)}, u32[]{:S(2)}, u32[]{:S(2)}) collective-permute-start(bf16[96,2048]{1,0:T(8,128)(2,1)S(1)} %collective-permute-done.7.refs_0_), channel_id=1, source_target_pairs={{0,64},{64,128},{128,192},{192,0},{1,65},{65,129},{129,193},{193,1... | collective-permute-start | bytes 1179656 | tf_op jit(solution)/shard_map/ppermute | solution.py:202
  63.9 2.5 %collective-permute-start.9 = (bf16[96,2048]{1,0:T(8,128)(2,1)S(1)}, bf16[96,2048]{1,0:T(8,128)(2,1)S(1)}, u32[]{:S(2)}, u32[]{:S(2)}) collective-permute-start(bf16[96,2048]{1,0:T(8,128)(2,1)S(1)} %collective-permute-done.5.refs_2_), channel_id=1, source_target_pairs={{0,256},{256,2},{2,258},{258,0},{1,257},{257,3},{3,259},{259,1},{4... | collective-permute-start | bytes 1179656 | tf_op jit(solution)/shard_map/ppermute | solution.py:203
  66.5 3.5 %collective-permute-done.6.refs_3_ = bf16[96,2048]{1,0:T(8,128)(2,1)S(1)} collective-permute-done((bf16[96,2048]{1,0:T(8,128)(2,1)S(1)}, bf16[96,2048]{1,0:T(8,128)(2,1)S(1)}, u32[]{:S(2)}, u32[]{:S(2)}) %collective-permute-start.6) | collective-permute-done | bytes 393248 | tf_op jit(solution)/shard_map/ppermute | solution.py:199
  70.1 0.7 shard_map.62
  70.8 1.1 copy-done.2
  72.0 6.5 %collective-permute-done.10.refs_3_ = bf16[96,2048]{1,0:T(8,128)(2,1)S(1)} collective-permute-done((bf16[96,2048]{1,0:T(8,128)(2,1)S(1)}, bf16[96,2048]{1,0:T(8,128)(2,1)S(1)}, u32[]{:S(2)}, u32[]{:S(2)}) %collective-permute-start.10) | collective-permute-done | bytes 393248 | tf_op jit(solution)/shard_map/ppermute | solution.py:204
  78.5 0.7 shard_map.63
  79.2 3.4 %collective-permute-start.11 = (f32[128,768]{1,0:T(8,128)S(1)}, f32[128,768]{1,0:T(8,128)S(1)}, u32[]{:S(2)}, u32[]{:S(2)}) collective-permute-start(f32[128,768]{1,0:T(8,128)S(1)} %get-tuple-element.27), channel_id=1, source_target_pairs={{0,1},{1,0},{2,3},{3,2},{4,5},{5,4},{6,7},{7,6},{8,9},{9,8},{10,11... | collective-permute-start | bytes 1179656 | tf_op jit(solution)/shard_map/ppermute | solution.py:175
  82.6 1.3 collective-permute-done.11.sr
  84.0 0.3 shard_map.64
  84.2 13.9 %all_to_all.25.w_own.refs_1_ = bf16[4,128,768]{2,1,0:T(8,128)(2,1)S(1)} all-to-all(bf16[4,128,768]{2,1,0:T(8,128)(2,1)S(1)} %shard_map.64), channel_id=1, replica_groups=mesh['yl'=2,'x'=4,'z'=16,'yh'=2,'c'=2] {'yl','yh'}, dimensions={0} | all-to-all | bytes 1572864 | tf_op jit(solution)/shard_map/all_to_all | solution.py:176
  98.1 3.4 %collective-permute-start.12 = (bf16[4,128,768]{2,1,0:T(8,128)(2,1)S(1)}, bf16[4,128,768]{2,1,0:T(8,128)(2,1)S(1)}, u32[]{:S(2)}, u32[]{:S(2)}) collective-permute-start(bf16[4,128,768]{2,1,0:T(8,128)(2,1)S(1)} %all_to_all.25.w_own.refs_1_), channel_id=1, source_target_pairs={{0,1},{1,0},{2,3},{3,2},{4,5},{5,4},{6,7},{7,6},{8,9},{9,8},{10,11... | collective-permute-start | bytes 2359304 | tf_op jit(solution)/shard_map/ppermute | solution.py:175
  101.5 0.1 pad_add_fusion.2.at_ref
  101.6 1.8 %collective-permute-done.12.w_oth.refs_2_ = bf16[4,128,768]{2,1,0:T(8,128)(2,1)S(1)} collective-permute-done((bf16[4,128,768]{2,1,0:T(8,128)(2,1)S(1)}, bf16[4,128,768]{2,1,0:T(8,128)(2,1)S(1)}, u32[]{:S(2)}, u32[]{:S(2)}) %collective-permute-start.12) | collective-permute-done | bytes 786464 | tf_op jit(solution)/shard_map/ppermute | solution.py:175
  103.4 1.6 shard_map.65
  105.0 23.5 %all_to_all.26.parts = f32[4,192,512]{2,1,0:T(8,128)S(1)} all-to-all(f32[4,192,512]{2,1,0:T(8,128)S(1)} %shard_map.65), channel_id=1, replica_groups=mesh['yl'=2,'x'=4,'z'=16,'yh'=2,'c'=2] {'x'}, dimensions={0} | all-to-all | bytes 3145728 | tf_op jit(solution)/shard_map/all_to_all | solution.py:176
  128.5 0.8 shard_map.66.refs_5_
  129.3 11.7 %all-to-all-start.3 = ((f32[16,48,128]{2,1,0:T(8,128)}), f32[16,48,128]{2,1,0:T(8,128)S(1)}, u32[]{:S(2)}, u32[]{:S(2)}) async-start(f32[16,48,128]{2,1,0:T(8,128)} %shard_map.66.refs_5_), calls=%async_computation.3 | async-start | bytes 786432 | tf_op jit(solution)/shard_map/all_to_all | solution.py:176
  141.1 1.4 copy-done.3
  142.5 1.4 copy-done.5
  143.9 1.8 %shard_map.67 = (f32[128,2048]{1,0:T(8,128)S(1)}, f32[128,2048]{1,0:T(8,128)S(1)}) custom-call(s32[2]{0:T(128)S(1)} %pad_add_fusion.refs_0_, bf16[4,128,768]{2,1,0:T(8,128)(2,1)S(1)} %all_to_all.25.w_own.refs_1_, bf16[4,128,768]{2,1,0:T(8,128)(2,1)S(1)} %collective-permute-done.12.w_oth.refs_2_, bf16[384,2048]{1,0:T(8,128)(2,1)S(1)} %copy-done.3, ...), custom_call_target="tpu_custom_call" | custom-call | flops 805306368 | bytes 7208968 | tf_op jit(solution)/shard_map/pallas_call | solution.py:39
  145.8 4.0 %collective-permute-start.13 = (f32[128,2048]{1,0:T(8,128)S(1)}, f32[128,2048]{1,0:T(8,128)S(1)}, u32[]{:S(2)}, u32[]{:S(2)}) collective-permute-start(f32[128,2048]{1,0:T(8,128)S(1)} %get-tuple-element.31), channel_id=1, source_target_pairs={{0,1},{1,0},{2,3},{3,2},{4,5},{5,4},{6,7},{7,6},{8,9},{9,8},{10,11... | collective-permute-start | bytes 3145736 | tf_op jit(solution)/shard_map/ppermute | solution.py:175
  149.8 2.3 %collective-permute-done.13.gx = f32[128,2048]{1,0:T(8,128)S(1)} collective-permute-done((f32[128,2048]{1,0:T(8,128)S(1)}, f32[128,2048]{1,0:T(8,128)S(1)}, u32[]{:S(2)}, u32[]{:S(2)}) %collective-permute-start.13) | collective-permute-done | bytes 1048608 | tf_op jit(solution)/shard_map/ppermute | solution.py:175
  152.0 1.3 shard_map.68
  153.4 4.2 %all-to-all-done.3.refs_0_ = f32[16,48,128]{2,1,0:T(8,128)S(1)} async-done(((f32[16,48,128]{2,1,0:T(8,128)}), f32[16,48,128]{2,1,0:T(8,128)S(1)}, u32[]{:S(2)}, u32[]{:S(2)}) %all-to-all-start.3) | async-done | bytes 393248 | tf_op jit(solution)/shard_map/all_to_all | solution.py:176
  157.6 15.2 %all_to_all.27.parts = f32[8,24,128]{2,1,0:T(8,128)S(1)} all-to-all(f32[8,24,128]{2,1,0:T(8,128)S(1)} %shard_map.69), channel_id=1, replica_groups=mesh['yl'=2,'x'=4,'z'=16,'yh'=2,'c'=2] {'yl','yh','c'}, dimensions={0} | all-to-all | bytes 196608 | tf_op jit(solution)/shard_map/all_to_all | solution.py:176
  172.9 0.7 shard_map.70
  (26 shorter events, 0.5 us)
Async XLA Ops:
  0.6 0.8 copy-start
  0.6 17.6 %copy-start.1 = (bf16[128,4096]{1,0:T(8,128)(2,1)S(1)}, bf16[128,4096]{1,0:T(8,128)(2,1)}, u32[]{:S(2)}) copy-start(bf16[128,4096]{1,0:T(8,128)(2,1)} %queries.1) | copy-start | bytes 3145732
  2.3 32.6 %copy-start.7 = (s32[128]{0:T(128)S(1)}, s32[128]{0:T(128)}, u32[]{:S(2)}) copy-start(s32[128]{0:T(128)} %param.6) | copy-start | bytes 1540
  2.3 32.7 %copy-start.6 = (s32[128,7]{0,1:T(8,128)S(1)}, s32[128,7]{0,1:T(8,128)}, u32[]{:S(2)}) copy-start(s32[128,7]{0,1:T(8,128)} %param.7) | copy-start | bytes 10756
  2.3 34.0 %all-to-all-start = ((bf16[16,6,16,128]{3,2,1,0:T(8,128)(2,1)}), bf16[16,6,16,128]{3,2,1,0:T(8,128)(2,1)}, u32[]{:S(2)}, u32[]{:S(2)}) async-start(bf16[16,6,16,128]{3,2,1,0:T(8,128)(2,1)} %broadcast_in_dim.8), calls=%async_computation | async-start | bytes 786432 | tf_op jit(solution)/shard_map/all_to_all | solution.py:176
  18.3 4.4 %collective-permute-start = (bf16[128,2048]{1,0:T(8,128)(2,1)S(1)}, bf16[128,2048]{1,0:T(8,128)(2,1)S(1)}, u32[]{:S(2)}, u32[]{:S(2)}) collective-permute-start(bf16[128,2048]{1,0:T(8,128)(2,1)S(1)} %constant_dynamic-slice_fusion), channel_id=1, source_target_pairs={{0,1},{1,0},{2,3},{3,2},{4,5},{5,4},{6,7},{7,6},{8,9},{9,8},{10,11... | collective-permute-start | bytes 1572872 | tf_op jit(solution)/shard_map/ppermute | solution.py:175
  24.2 13.2 %collective-permute-start.1 = (bf16[256,512]{1,0:T(8,128)(2,1)}, bf16[256,512]{1,0:T(8,128)(2,1)S(1)}, u32[]{:S(2)}, u32[]{:S(2)}) collective-permute-start(bf16[256,512]{1,0:T(8,128)(2,1)} %get-tuple-element.20), channel_id=1, source_target_pairs={{0,256},{256,2},{2,258},{258,0},{1,257},{257,3},{3,259},{259,1},{4... | collective-permute-start | bytes 786440 | tf_op jit(solution)/shard_map/ppermute | solution.py:188
  27.4 14.6 %collective-permute-start.2 = (bf16[256,512]{1,0:T(8,128)(2,1)}, bf16[256,512]{1,0:T(8,128)(2,1)S(1)}, u32[]{:S(2)}, u32[]{:S(2)}) collective-permute-start(bf16[256,512]{1,0:T(8,128)(2,1)} %get-tuple-element.21), channel_id=1, source_target_pairs={{0,2},{256,258},{2,0},{258,256},{1,3},{257,259},{3,1},{259,257},{4... | collective-permute-start | bytes 786440 | tf_op jit(solution)/shard_map/ppermute | solution.py:188
  31.9 11.0 %collective-permute-start.3 = (bf16[256,512]{1,0:T(8,128)(2,1)S(1)}, bf16[256,512]{1,0:T(8,128)(2,1)S(1)}, u32[]{:S(2)}, u32[]{:S(2)}) collective-permute-start(bf16[256,512]{1,0:T(8,128)(2,1)S(1)} %get-tuple-element.22), channel_id=1, source_target_pairs={{0,258},{256,0},{2,256},{258,2},{1,259},{257,1},{3,257},{259,3},{4... | collective-permute-start | bytes 786440 | tf_op jit(solution)/shard_map/ppermute | solution.py:188
  42.9 15.1 %collective-permute-start.7 = (bf16[96,2048]{1,0:T(8,128)(2,1)S(1)}, bf16[96,2048]{1,0:T(8,128)(2,1)S(1)}, u32[]{:S(2)}, u32[]{:S(2)}) collective-permute-start(bf16[96,2048]{1,0:T(8,128)(2,1)S(1)} %shard_map.61.refs_0_), channel_id=1, source_target_pairs={{0,256},{256,2},{2,258},{258,0},{1,257},{257,3},{3,259},{259,1},{4... | collective-permute-start | bytes 1179656 | tf_op jit(solution)/shard_map/ppermute | solution.py:198
  48.1 15.9 %collective-permute-start.5 = (bf16[96,2048]{1,0:T(8,128)(2,1)S(1)}, bf16[96,2048]{1,0:T(8,128)(2,1)S(1)}, u32[]{:S(2)}, u32[]{:S(2)}) collective-permute-start(bf16[96,2048]{1,0:T(8,128)(2,1)S(1)} %shard_map.61.refs_0_), channel_id=1, source_target_pairs={{0,128},{64,192},{128,0},{192,64},{1,129},{65,193},{129,1},{193,65... | collective-permute-start | bytes 1179656 | tf_op jit(solution)/shard_map/ppermute | solution.py:199
  52.7 17.3 %collective-permute-start.6 = (bf16[96,2048]{1,0:T(8,128)(2,1)S(1)}, bf16[96,2048]{1,0:T(8,128)(2,1)S(1)}, u32[]{:S(2)}, u32[]{:S(2)}) collective-permute-start(bf16[96,2048]{1,0:T(8,128)(2,1)S(1)} %shard_map.61.refs_0_), channel_id=1, source_target_pairs={{0,192},{64,0},{128,64},{192,128},{1,193},{65,1},{129,65},{193,129... | collective-permute-start | bytes 1179656 | tf_op jit(solution)/shard_map/ppermute | solution.py:199
  55.5 14.6 %collective-permute-start.4 = (bf16[96,2048]{1,0:T(8,128)(2,1)S(1)}, bf16[96,2048]{1,0:T(8,128)(2,1)S(1)}, u32[]{:S(2)}, u32[]{:S(2)}) collective-permute-start(bf16[96,2048]{1,0:T(8,128)(2,1)S(1)} %shard_map.61.refs_0_), channel_id=1, source_target_pairs={{0,64},{64,128},{128,192},{192,0},{1,65},{65,129},{129,193},{193,1... | collective-permute-start | bytes 1179656 | tf_op jit(solution)/shard_map/ppermute | solution.py:199
  58.0 20.4 %collective-permute-start.10 = (bf16[96,2048]{1,0:T(8,128)(2,1)S(1)}, bf16[96,2048]{1,0:T(8,128)(2,1)S(1)}, u32[]{:S(2)}, u32[]{:S(2)}) collective-permute-start(bf16[96,2048]{1,0:T(8,128)(2,1)S(1)} %collective-permute-done.7.refs_0_), channel_id=1, source_target_pairs={{0,192},{64,0},{128,64},{192,128},{1,193},{65,1},{129,65},{193,129... | collective-permute-start | bytes 1179656 | tf_op jit(solution)/shard_map/ppermute | solution.py:204
  62.0 16.5 %collective-permute-start.8 = (bf16[96,2048]{1,0:T(8,128)(2,1)S(1)}, bf16[96,2048]{1,0:T(8,128)(2,1)S(1)}, u32[]{:S(2)}, u32[]{:S(2)}) collective-permute-start(bf16[96,2048]{1,0:T(8,128)(2,1)S(1)} %collective-permute-done.7.refs_0_), channel_id=1, source_target_pairs={{0,64},{64,128},{128,192},{192,0},{1,65},{65,129},{129,193},{193,1... | collective-permute-start | bytes 1179656 | tf_op jit(solution)/shard_map/ppermute | solution.py:202
  63.9 14.5 %collective-permute-start.9 = (bf16[96,2048]{1,0:T(8,128)(2,1)S(1)}, bf16[96,2048]{1,0:T(8,128)(2,1)S(1)}, u32[]{:S(2)}, u32[]{:S(2)}) collective-permute-start(bf16[96,2048]{1,0:T(8,128)(2,1)S(1)} %collective-permute-done.5.refs_2_), channel_id=1, source_target_pairs={{0,256},{256,2},{2,258},{258,0},{1,257},{257,3},{3,259},{259,1},{4... | collective-permute-start | bytes 1179656 | tf_op jit(solution)/shard_map/ppermute | solution.py:203
  70.8 1.1 copy-start.2
  79.2 18.9 %copy-start.4 = (bf16[384,2048]{1,0:T(8,128)(2,1)}, bf16[384,2048]{1,0:T(8,128)(2,1)S(1)}, u32[]{:S(2)}) copy-start(bf16[384,2048]{1,0:T(8,128)(2,1)S(1)} %get-tuple-element.29.refs_4_) | copy-start | bytes 4718596
  79.2 4.7 %collective-permute-start.11 = (f32[128,768]{1,0:T(8,128)S(1)}, f32[128,768]{1,0:T(8,128)S(1)}, u32[]{:S(2)}, u32[]{:S(2)}) collective-permute-start(f32[128,768]{1,0:T(8,128)S(1)} %get-tuple-element.27), channel_id=1, source_target_pairs={{0,1},{1,0},{2,3},{3,2},{4,5},{5,4},{6,7},{7,6},{8,9},{9,8},{10,11... | collective-permute-start | bytes 1179656 | tf_op jit(solution)/shard_map/ppermute | solution.py:175
  98.1 5.3 %collective-permute-start.12 = (bf16[4,128,768]{2,1,0:T(8,128)(2,1)S(1)}, bf16[4,128,768]{2,1,0:T(8,128)(2,1)S(1)}, u32[]{:S(2)}, u32[]{:S(2)}) collective-permute-start(bf16[4,128,768]{2,1,0:T(8,128)(2,1)S(1)} %all_to_all.25.w_own.refs_1_), channel_id=1, source_target_pairs={{0,1},{1,0},{2,3},{3,2},{4,5},{5,4},{6,7},{7,6},{8,9},{9,8},{10,11... | collective-permute-start | bytes 2359304 | tf_op jit(solution)/shard_map/ppermute | solution.py:175
  129.3 28.2 %all-to-all-start.3 = ((f32[16,48,128]{2,1,0:T(8,128)}), f32[16,48,128]{2,1,0:T(8,128)S(1)}, u32[]{:S(2)}, u32[]{:S(2)}) async-start(f32[16,48,128]{2,1,0:T(8,128)} %shard_map.66.refs_5_), calls=%async_computation.3 | async-start | bytes 786432 | tf_op jit(solution)/shard_map/all_to_all | solution.py:176
  141.1 1.4 copy-start.3
  142.5 1.4 copy-start.5
  145.8 6.3 %collective-permute-start.13 = (f32[128,2048]{1,0:T(8,128)S(1)}, f32[128,2048]{1,0:T(8,128)S(1)}, u32[]{:S(2)}, u32[]{:S(2)}) collective-permute-start(f32[128,2048]{1,0:T(8,128)S(1)} %get-tuple-element.31), channel_id=1, source_target_pairs={{0,1},{1,0},{2,3},{3,2},{4,5},{5,4},{6,7},{7,6},{8,9},{9,8},{10,11... | collective-permute-start | bytes 3145736 | tf_op jit(solution)/shard_map/ppermute | solution.py:175
